TPU v7x, 128 devices: a whole 4x4x4 slice. The times are simulated.
128 devices in a mesh: rad: 8 (over x, core), chan: 16 (over z, y).
Axes of the slice: x: 4, y: 4, z: 4, core: 2. Of those that a mesh axis runs over, the one named last changes fastest.
Arguments:
- inner_state: float32 [2, 32768], P(None, ('rad', 'chan')), may hold values from -6 to 6
- outer_state: float32 [2, 49152, 512], P(None, ('rad', 'chan')), may hold values from -6 to 6
- inner_ham: float32 [8, 4096, 4096], P('rad', None, 'chan'), may hold values from -0.09375 to 0.09375
- inner_coupling: float32 [8, 2, 512, 4096], P('rad', None, None, 'chan'), may hold values from -0.125 to 0.125
- surface_amp: float32 [8, 2, 4096, 512], P('rad', None, 'chan'), may hold values from -0.09375 to 0.09375
- potential: float32 [49152, 512], P(('rad', 'chan')), may hold values from 0 to 1
- laser_mix: float32 [512, 512], replicated, may hold values from -0.0625 to 0.0625
- partners: int32 [8, 2], replicated, may hold values from 0 to 7
- band_offsets: int32 [8, 2], replicated, may hold values from -512 to 0
- channel_group: int32 [512], replicated, may hold values from 0 to 7
Outputs:
- last_inner: float32 [2, 32768], P(None, ('rad', 'chan'))
- last_outer: float32 [2, 49152, 512], P(None, ('rad', 'chan'))
- hessenberg: float32 [2, 3, 2], replicated
All inputs are finite; a program needn't handle non-finite values.
Results may differ from a plain program's by a relative error of at most 0.00013.
Values sent between devices are 32-bit elements; how exact they have to be, the bound alone decides.
No kernel may reach another device: no remote copies, remote signals or barrier semaphores. Data moves between devices by JAX's collectives and lax.ppermute only.
A program may use at most 64 MiB of HBM per device.

v0:
```python
import jax
import jax.numpy as jnp
from jax import lax
from jax.sharding import PartitionSpec as P

STRIP = 256
TERMS = 2


highest = lax.Precision.HIGHEST
kinetic_coef = -0.5 * 0.05 / (12.0 * 0.25 * 0.25)
slope_coef = 1.0 / (12.0 * 0.25)
bloch_coef = 2.0


def spread(block, axis, holder):
    block = jnp.where(lax.axis_index(axis) == holder, block, jnp.zeros_like(block))
    return lax.psum(block, axis)


def padded_2(block, sides, width):
    for axis, dim in sides:
        count = lax.axis_size(axis)
        forward = [(i, i + 1) for i in range(count - 1)]
        backward = [(target, source) for source, target in forward]
        low = lax.ppermute(
            lax.slice_in_dim(block, block.shape[dim] - width, None, axis=dim), axis, forward
        )
        high = lax.ppermute(lax.slice_in_dim(block, 0, width, axis=dim), axis, backward)
        block = jnp.concatenate([low, block, high], axis=dim)
    return block


def local_parts(left, right):
    real_part = jnp.sum(left[0] * right[0]) + jnp.sum(left[1] * right[1])
    imag_part = jnp.sum(left[0][0] * right[0][1] - left[0][1] * right[0][0]) + jnp.sum(
        left[1][0] * right[1][1] - left[1][1] * right[1][0]
    )
    return jnp.stack([real_part, imag_part])


def squares(vector):
    return jnp.sum(vector[0] * vector[0]) + jnp.sum(vector[1] * vector[1])


def rotate(vector, real_coef, imag_coef):
    return jnp.stack(
        [
            real_coef * vector[0] - imag_coef * vector[1],
            real_coef * vector[1] + imag_coef * vector[0],
        ]
    )


def remove_all(image, krylov, coefs):
    image_in, image_out = image
    image_in = image_in - rotate(krylov[0][0], coefs[0, 0], coefs[0, 1])
    image_out = image_out - rotate(krylov[0][1], coefs[0, 0], coefs[0, 1])
    return (image_in, image_out)


def body(
    inner_state,
    outer_state,
    inner_ham,
    inner_coupling,
    surface_amp,
    potential,
    laser_mix,
    partners,
    band_offsets,
    channel_group,
):
    block_order = inner_ham.shape[1]
    local_rows = inner_ham.shape[2]
    channels = outer_state.shape[2]
    points = outer_state.shape[1]
    band_width = inner_coupling.shape[2]
    couplings = inner_coupling.shape[1]
    blocks = lax.axis_size("rad")
    block_index = lax.axis_index("rad")
    chan_index = lax.axis_index("chan")
    is_first = lax.axis_index(("rad", "chan")) == 0
    entries = float(blocks * block_order + lax.axis_size(("rad", "chan")) * points * channels)
    member = (channel_group == block_index).astype(jnp.float32)
    masked_amp = surface_amp[0] * member[None, None, :]
    own_ham = inner_ham[0]
    own_partners = lax.dynamic_index_in_dim(partners, block_index, 0, keepdims=False)
    own_offsets = lax.dynamic_index_in_dim(band_offsets, block_index, 0, keepdims=False)
    start_sq = lax.psum(squares((inner_state, outer_state)), ("rad", "chan"))
    start_len = jnp.sqrt(start_sq / entries)
    krylov = [(inner_state / start_len, outer_state / start_len)]
    hessenberg = jnp.zeros((2, TERMS + 1, TERMS), jnp.float32)
    for term_index in range(TERMS):
        inner_vec = krylov[term_index][0]
        outer_vec = krylov[term_index][1]
        block_vec = lax.all_gather(inner_vec, "chan", axis=1, tiled=True)
        whole_vec = lax.all_gather(block_vec, "rad", axis=1, tiled=True)
        stacked = whole_vec.reshape(2, blocks, block_order)
        own_vec = lax.dynamic_index_in_dim(stacked, block_index, 1, keepdims=False)
        result_in = jnp.dot(own_vec, own_ham, precision=highest, preferred_element_type=jnp.float32)
        padded = jnp.pad(stacked, ((0, 0), (0, 0), (band_width, band_width)))
        for couple_index in range(couplings):
            source = lax.dynamic_index_in_dim(padded, own_partners[couple_index], 1, keepdims=False)
            window_start = chan_index * local_rows + 0 + own_offsets[couple_index] + band_width
            window = lax.dynamic_slice_in_dim(source, window_start, band_width, 1)
            tile = inner_coupling[0, couple_index, :, 0:STRIP]
            pieces = jnp.dot(window, tile, precision=highest, preferred_element_type=jnp.float32)
            result_in = result_in + pieces
        ghost_rows = lax.psum(
            jnp.einsum("pk,mki->pmi", inner_vec, masked_amp, precision=highest), ("rad", "chan")
        )
        first_row = spread(outer_vec[:, 0, :], ("rad", "chan"), 0)
        result_in = result_in + bloch_coef * jnp.einsum(
            "pi,ki->pk", first_row, masked_amp[0], precision=highest
        )
        extended = padded_2(outer_vec, ((("rad", "chan"), 1),), 2)
        lower_rim = jnp.where(
            is_first, jnp.stack([ghost_rows[:, 1], ghost_rows[:, 0]], axis=1), extended[:, 0:2]
        )
        extended = jnp.concatenate([lower_rim, extended[:, 2:]], axis=1)
        far_left = extended[:, 0:points]
        near_left = extended[:, 1 : points + 1]
        centre_row = extended[:, 2 : points + 2]
        near_right = extended[:, 3 : points + 3]
        far_right = extended[:, 4 : points + 4]
        laplace = -far_left + 16.0 * near_left - 30.0 * centre_row + 16.0 * near_right - far_right
        slope_rows = slope_coef * (far_left - 8.0 * near_left + 8.0 * near_right - far_right)
        mixed_slope = jnp.einsum("prc,cd->prd", slope_rows, laser_mix, precision=highest)
        result_out = (
            kinetic_coef * laplace
            + potential * outer_vec
            + jnp.stack([mixed_slope[1], -mixed_slope[0]])
        )
        image = (result_in, result_out)
        coef_list = []
        for prior_index in range(term_index + 1):
            coefs = lax.psum(local_parts(krylov[prior_index], image), ("rad", "chan")) / entries
            image = remove_all(image, [krylov[prior_index]], coefs[None, :])
            coef_list.append(coefs)
        all_coefs = jnp.stack(coef_list)
        new_length = jnp.sqrt(lax.psum(squares(image), ("rad", "chan")) / entries)
        hessenberg = hessenberg.at[:, 0 : term_index + 1, term_index].set(all_coefs.T)
        hessenberg = hessenberg.at[0, term_index + 1, term_index].set(new_length)
        krylov.append((image[0] / new_length, image[1] / new_length))
    return (krylov[-1][0], krylov[-1][1], hessenberg)


def solution(mesh):
    return jax.shard_map(
        body,
        mesh=mesh,
        in_specs=(
            P(None, ("rad", "chan")),
            P(None, ("rad", "chan"), None),
            P("rad", None, "chan"),
            P("rad", None, None, "chan"),
            P("rad", None, "chan", None),
            P(("rad", "chan"), None),
            P(),
            P(),
            P(),
            P(),
        ),
        out_specs=(P(None, ("rad", "chan")), P(None, ("rad", "chan"), None), P()),
        check_vma=False,
    )
```

profile of v0, /device:TPU:1, one launch (start us, length us, event | category | flops | bytes accessed | tf_op | source)
XLA Modules:
  0.0 700.1 jit_solution(4163253788307968800)
XLA Ops:
  0.6 1.4 multiply_reduce_fusion.11
  2.0 2.4 multiply_reduce_fusion.5
  5.7 68.7 %psum.70 = f32[]{:T(128)} all-reduce(f32[]{:T(128)S(6)} %add.195), channel_id=1, replica_groups=mesh['rad'=8,'chan'=16] {'rad','chan'}, use_global_device_ids=true, to_apply=%region_2.3 | all-reduce | flops 1 | bytes 8 | tf_op jit(solution)/shard_map/psum | solution.py:90
  75.2 1.6 broadcast_divide_fusion.2
  76.8 1.9 collective-permute-start
  78.7 7.0 collective-permute-start.1
  90.9 15.0 %all_gather.12 = f32[2,4096]{1,0:T(2,128)S(1)} all-gather(f32[2,256]{1,0:T(2,128)S(1)} %broadcast_divide_fusion.5), channel_id=1, replica_groups=mesh['rad'=8,'chan'=16] {'chan'}, dimensions={1}, use_global_device_ids=true | all-gather | bytes 34816 | tf_op jit(solution)/shard_map/all_gather | solution.py:97
  106.0 1.4 bitcast_multiply_fusion
  108.9 69.3 %all-reduce.4 = (f32[2,512]{1,0:T(2,128)S(1)}, f32[2,2,512]{2,1,0:T(2,128)S(1)}) all-reduce(f32[2,512]{1,0:T(2,128)S(1)} %bitcast.127, f32[2,2,512]{2,1,0:T(2,128)S(1)} %copy.24), channel_id=1, replica_groups=mesh['rad'=8,'chan'=16] {'rad','chan'}, use_global_device_ids=true, to_apply=%region_3.4 | all-reduce | flops 3072 | bytes 24576 | tf_op jit(solution)/shard_map/psum | solution.py:18
  178.2 1.5 convolution_multiply_fusion.1
  179.8 13.5 %all_gather.13 = f32[2,32768]{1,0:T(2,128)S(1)} all-gather(f32[2,4096]{1,0:T(2,128)S(1)} %all_gather.12), channel_id=1, replica_groups=mesh['rad'=8,'chan'=16] {'rad'}, dimensions={1}, use_global_device_ids=true | all-gather | bytes 294912 | tf_op jit(solution)/shard_map/all_gather | solution.py:98
  194.8 1.3 fusion.54
  196.2 1.4 fusion.58
  197.6 4.5 multiply_reduce_fusion.10
  202.8 3.3 fusion.15
  207.2 1.9 multiply_reduce_fusion.4
  209.2 1.1 copy-done.1
  214.0 62.7 %psum.73 = f32[2]{0:T(128)S(1)} all-reduce(f32[2]{0:T(128)S(1)} %pad_maximum_fusion.9), channel_id=1, replica_groups=mesh['rad'=8,'chan'=16] {'rad','chan'}, use_global_device_ids=true, to_apply=%region_9.10 | all-reduce | flops 2 | bytes 16 | tf_op jit(solution)/shard_map/psum | solution.py:138
  277.3 1.3 multiply_subtract_fusion.5
  278.6 1.6 multiply_subtract_fusion.2
  283.5 63.5 %psum.74 = f32[]{:T(128)} all-reduce(f32[]{:T(128)S(6)} %add.218), channel_id=1, replica_groups=mesh['rad'=8,'chan'=16] {'rad','chan'}, use_global_device_ids=true, to_apply=%region_12.13 | all-reduce | flops 1 | bytes 8 | tf_op jit(solution)/shard_map/psum | solution.py:142
  347.7 2.1 broadcast_divide_fusion.1
  350.4 15.9 %all_gather.14 = f32[2,4096]{1,0:T(2,128)S(1)} all-gather(f32[2,256]{1,0:T(2,128)S(1)} %broadcast_divide_fusion.4), channel_id=1, replica_groups=mesh['rad'=8,'chan'=16] {'chan'}, dimensions={1}, use_global_device_ids=true | all-gather | bytes 34816 | tf_op jit(solution)/shard_map/all_gather | solution.py:97
  366.3 18.8 %all_gather.15 = f32[2,32768]{1,0:T(2,128)S(1)} all-gather(f32[2,4096]{1,0:T(2,128)S(1)} %all_gather.14), channel_id=1, replica_groups=mesh['rad'=8,'chan'=16] {'rad'}, dimensions={1}, use_global_device_ids=true | all-gather | bytes 294912 | tf_op jit(solution)/shard_map/all_gather | solution.py:98
  385.5 63.9 %all-reduce.3 = (f32[2,512]{1,0:T(2,128)S(1)}, f32[2,2,512]{2,1,0:T(2,128)S(1)}) all-reduce(f32[2,512]{1,0:T(2,128)S(1)} %bitcast.128, f32[2,2,512]{2,1,0:T(2,128)S(1)} %copy.25), channel_id=1, replica_groups=mesh['rad'=8,'chan'=16] {'rad','chan'}, use_global_device_ids=true, to_apply=%region_13.14 | all-reduce | flops 3072 | bytes 24576 | tf_op jit(solution)/shard_map/psum | solution.py:18
  449.3 1.5 convolution_multiply_fusion
  450.9 1.3 fusion.52
  452.2 1.4 fusion.56
  453.6 2.0 collective-permute-start.2
  455.6 4.7 multiply_reduce_fusion.8
  460.9 7.2 %collective-permute-start.3 = (f32[2,2,512]{2,1,0:T(2,128)S(1)}, f32[2,2,512]{2,1,0:T(2,128)S(1)}, u32[]{:S(2)}, u32[]{:S(2)}) collective-permute-start(f32[2,2,512]{2,1,0:T(2,128)S(1)} %get-tuple-element.75), channel_id=1, source_target_pairs={{1,0},{2,1},{3,2},{4,3},{5,4},{6,5},{7,6},{8,7},{9,8},{10,9},{11,1... | collective-permute-start | bytes 24584 | tf_op jit(solution)/shard_map/ppermute | solution.py:29
  468.6 3.3 fusion.8
  472.1 1.2 copy-done.12
  473.5 1.9 multiply_reduce_fusion.2
  475.5 1.1 copy-done.13
  480.9 67.1 %psum.77 = f32[2]{0:T(128)S(1)} all-reduce(f32[2]{0:T(128)S(1)} %pad_maximum_fusion.10), channel_id=1, replica_groups=mesh['rad'=8,'chan'=16] {'rad','chan'}, use_global_device_ids=true, to_apply=%region_19.20 | all-reduce | flops 2 | bytes 16 | tf_op jit(solution)/shard_map/psum | solution.py:138
  548.6 1.3 multiply_subtract_fusion.4
  549.9 1.8 multiply_subtract_fusion.1
  553.0 2.6 multiply_reduce_fusion.1
  555.6 1.1 copy-done.7
  556.8 1.1 fusion.43
  560.5 62.5 %psum.78 = f32[2]{0:T(128)S(1)} all-reduce(f32[2]{0:T(128)S(1)} %pad_maximum_fusion.11), channel_id=1, replica_groups=mesh['rad'=8,'chan'=16] {'rad','chan'}, use_global_device_ids=true, to_apply=%region_24.25 | all-reduce | flops 2 | bytes 16 | tf_op jit(solution)/shard_map/psum | solution.py:138
  623.7 1.3 multiply_subtract_fusion.3
  625.1 1.6 multiply_subtract_fusion
  627.6 1.1 multiply_reduce_fusion
  630.1 64.1 %psum.79 = f32[]{:T(128)} all-reduce(f32[]{:T(128)S(6)} %add.235), channel_id=1, replica_groups=mesh['rad'=8,'chan'=16] {'rad','chan'}, use_global_device_ids=true, to_apply=%region_27.28 | all-reduce | flops 1 | bytes 8 | tf_op jit(solution)/shard_map/psum | solution.py:142
  695.5 2.6 broadcast_divide_fusion
  698.1 1.3 scatter.16
  (100 shorter events, 17.6 us)
Async XLA Ops:
  0.6 202.1 %copy-start = (f32[512,512]{1,0:T(8,128)S(1)}, f32[512,512]{1,0:T(8,128)}, u32[]{:S(2)}) copy-start(f32[512,512]{1,0:T(8,128)} %param.24) | copy-start | bytes 3145732
  75.1 10.6 %copy-start.19 = (f32[2,256]{1,0:T(2,128)S(1)}, f32[2,256]{1,0:T(2,128)}, u32[]{:S(2)}) copy-start(f32[2,256]{1,0:T(2,128)} %param.18) | copy-start | bytes 6148
  75.1 10.6 %copy-start.21 = (s32[8,2]{0,1:T(2,128)S(1)}, s32[8,2]{0,1:T(2,128)}, u32[]{:S(2)}) copy-start(s32[8,2]{0,1:T(2,128)} %param.26) | copy-start | bytes 196
  75.1 10.6 %copy-start.22 = (s32[8,2]{0,1:T(2,128)S(1)}, s32[8,2]{0,1:T(2,128)}, u32[]{:S(2)}) copy-start(s32[8,2]{0,1:T(2,128)} %param.25) | copy-start | bytes 196
  75.1 15.8 %copy-start.20 = (s32[512]{0:T(512)S(1)}, s32[512]{0:T(512)}, u32[]{:S(2)}) copy-start(s32[512]{0:T(512)} %param.27) | copy-start | bytes 6148
  76.8 126.0 %collective-permute-start = (f32[2,2,512]{2,1,0:T(2,128)S(1)}, f32[2,2,512]{2,1,0:T(2,128)S(1)}, u32[]{:S(2)}, u32[]{:S(2)}) collective-permute-start(f32[2,2,512]{2,1,0:T(2,128)S(1)} %get-tuple-element.82), channel_id=1, source_target_pairs={{0,1},{1,2},{2,3},{3,4},{4,5},{5,6},{6,7},{7,8},{8,9},{9,10},{10,1... | collective-permute-start | bytes 24584 | tf_op jit(solution)/shard_map/ppermute | solution.py:26
  78.7 124.0 %collective-permute-start.1 = (f32[2,2,512]{2,1,0:T(2,128)S(1)}, f32[2,2,512]{2,1,0:T(2,128)S(1)}, u32[]{:S(2)}, u32[]{:S(2)}) collective-permute-start(f32[2,2,512]{2,1,0:T(2,128)S(1)} %get-tuple-element.81), channel_id=1, source_target_pairs={{1,0},{2,1},{3,2},{4,3},{5,4},{6,5},{7,6},{8,7},{9,8},{10,9},{11,1... | collective-permute-start | bytes 24584 | tf_op jit(solution)/shard_map/ppermute | solution.py:29
  107.3 1.0 copy-start.10
  206.1 1.1 copy-start.17
  209.2 1.1 copy-start.1
  278.6 2.5 copy-start.2
  280.2 0.9 copy-start.15
  347.6 2.1 copy-start.11
  349.7 35.7 %copy-start.4 = (f32[2,384,512]{2,1,0:T(8,128)}, f32[2,384,512]{2,1,0:T(8,128)S(1)}, u32[]{:S(2)}) copy-start(f32[2,384,512]{2,1,0:T(8,128)S(1)} %broadcast_divide_fusion.1) | copy-start | bytes 4718596
  453.6 14.5 %collective-permute-start.2 = (f32[2,2,512]{2,1,0:T(2,128)S(1)}, f32[2,2,512]{2,1,0:T(2,128)S(1)}, u32[]{:S(2)}, u32[]{:S(2)}) collective-permute-start(f32[2,2,512]{2,1,0:T(2,128)S(1)} %get-tuple-element.76), channel_id=1, source_target_pairs={{0,1},{1,2},{2,3},{3,4},{4,5},{5,6},{6,7},{7,8},{8,9},{9,10},{10,1... | collective-permute-start | bytes 24584 | tf_op jit(solution)/shard_map/ppermute | solution.py:26
  455.6 13.0 %copy-start.5 = (f32[2,384,512]{2,1,0:T(8,128)S(1)}, f32[2,384,512]{2,1,0:T(8,128)}, u32[]{:S(2)}) copy-start(f32[2,384,512]{2,1,0:T(8,128)} %copy-done.4) | copy-start | bytes 4718596
  460.9 7.7 %collective-permute-start.3 = (f32[2,2,512]{2,1,0:T(2,128)S(1)}, f32[2,2,512]{2,1,0:T(2,128)S(1)}, u32[]{:S(2)}, u32[]{:S(2)}) collective-permute-start(f32[2,2,512]{2,1,0:T(2,128)S(1)} %get-tuple-element.75), channel_id=1, source_target_pairs={{1,0},{2,1},{3,2},{4,3},{5,4},{6,5},{7,6},{8,7},{9,8},{10,9},{11,1... | collective-permute-start | bytes 24584 | tf_op jit(solution)/shard_map/ppermute | solution.py:29
  471.9 1.4 copy-start.12
  471.9 1.6 copy-start.18
  475.5 1.1 copy-start.13
  549.9 3.1 copy-start.3
  549.9 3.0 copy-start.14
  553.0 3.8 copy-start.6
  555.6 1.1 copy-start.7
  625.1 2.5 copy-start.8
  626.7 0.9 copy-start.16
  627.6 67.9 %copy-start.9 = (f32[2,384,512]{2,1,0:T(8,128)S(1)}, f32[2,384,512]{2,1,0:T(8,128)}, u32[]{:S(2)}) copy-start(f32[2,384,512]{2,1,0:T(8,128)} %copy-done.7) | copy-start | bytes 4718596
where the time goes:
time: 702 us; the launch traced here: 700 us
  blocking collectives  585 us (83%)
  other arithmetic  37.4 us (5%)
  matrix products  25.5 us (4%)
  between operations  20 us (3%)
  starting transfers between devices  18 us (3%)
  local copies, waits for them, and re-layouts  13.6 us (2%)
    psum x3, blocking collectives, body(): lax.psum(local_parts(krylov[prior_index], image), ('rad', 'chan')) / entries  192 us
    psum x2, blocking collectives, spread(): return lax.psum(block, axis)  133 us
    psum x2, blocking collectives, body(): new_length = jnp.sqrt(lax.psum(squares(image), ('rad', 'chan')) / entries)  128 us
    psum x1, blocking collectives, body(): start_sq = lax.psum(squares((inner_state, outer_state)), ('rad', 'chan'))  68.7 us
    all_gather x2, blocking collectives, body(): whole_vec = lax.all_gather(block_vec, 'rad', axis=1, tiled=True)  32.3 us
    all_gather x2, blocking collectives, body(): block_vec = lax.all_gather(inner_vec, 'chan', axis=1, tiled=True)  31 us
    ppermute x2, starting transfers between devices, padded_2(): lax.ppermute(lax.slice_in_dim(block, 0, width, axis=dim), axis, backward)  14.1 us
  transfers between devices with their start and end apart: 4, of which 1 were waited for; matrix products, arithmetic and copies ran while one was open for 3% of the time, Pallas kernels for 0%

commit v1 on v0

v1 whole, which is shorter than its diff:
```python
import jax
import jax.numpy as jnp
from jax import lax
from jax.sharding import PartitionSpec as P

STRIP = 256
TERMS = 2

highest = lax.Precision.HIGHEST
kinetic_coef = -0.5 * 0.05 / (12.0 * 0.25 * 0.25)
slope_coef = 1.0 / (12.0 * 0.25)
bloch_coef = 2.0
shift = 1.5
least_left = 0.02
both = ("rad", "chan")


def spread(block, axis, holder):
    block = jnp.where(lax.axis_index(axis) == holder, block, jnp.zeros_like(block))
    return lax.psum(block, axis)


def local_parts(left, right):
    real_part = jnp.sum(left[0] * right[0]) + jnp.sum(left[1] * right[1])
    imag_part = jnp.sum(left[0][0] * right[0][1] - left[0][1] * right[0][0]) + jnp.sum(
        left[1][0] * right[1][1] - left[1][1] * right[1][0]
    )
    return jnp.stack([real_part, imag_part])


def rotate(vector, real_coef, imag_coef):
    return jnp.stack(
        [
            real_coef * vector[0] - imag_coef * vector[1],
            real_coef * vector[1] + imag_coef * vector[0],
        ]
    )


def neighbours(block, width):
    count = lax.axis_size(both)
    forward = [(i, i + 1) for i in range(count - 1)]
    backward = [(target, source) for source, target in forward]
    low = lax.ppermute(block[:, block.shape[1] - width :], both, forward)
    high = lax.ppermute(block[:, :width], both, backward)
    return low, high


def outer_apply(extended, potential, laser_mix, moved):
    points = extended.shape[1] - 4
    far_left = extended[:, 0:points]
    near_left = extended[:, 1 : points + 1]
    centre_row = extended[:, 2 : points + 2]
    near_right = extended[:, 3 : points + 3]
    far_right = extended[:, 4 : points + 4]
    laplace = -far_left + 16.0 * near_left - 30.0 * centre_row + 16.0 * near_right - far_right
    slope_rows = slope_coef * (far_left - 8.0 * near_left + 8.0 * near_right - far_right)
    mixed_slope = jnp.einsum("prc,cd->prd", slope_rows, laser_mix, precision=highest)
    return (
        kinetic_coef * laplace
        + (potential - moved) * centre_row
        + jnp.stack([mixed_slope[1], -mixed_slope[0]])
    )


def inner_windows(shards, own_partners, own_offsets):
    windows = []
    for couple_index in range(own_partners.shape[0]):
        source = lax.dynamic_index_in_dim(shards, own_partners[couple_index], 0, keepdims=False)
        source = source.transpose(1, 0, 2).reshape(2, -1)
        band_width = source.shape[1] // 2
        windows.append(
            lax.dynamic_slice_in_dim(source, own_offsets[couple_index] + band_width, band_width, 1)
        )
    return windows


def exchange(inner_vec, ghost_part, row):
    rows = inner_vec.shape[1]
    blocks, strips = lax.axis_size("rad"), lax.axis_size("chan")
    chunk = jnp.concatenate(
        [
            inner_vec,
            ghost_part.reshape(-1, rows),
            row.reshape(-1, rows),
            jnp.zeros((2, rows), jnp.float32),
        ],
        axis=0,
    )
    got = lax.all_to_all(jnp.broadcast_to(chunk, (strips,) + chunk.shape), "chan", 0, 0)
    own = got[:, 0:2]
    ghost_sum = jnp.sum(got[:, 2:10], axis=0)
    padded = jnp.pad(own, ((2, 1), (0, 0), (0, 0)))
    near = lax.dynamic_slice_in_dim(padded, lax.axis_index("chan"), 4, 0)
    chunk = jnp.concatenate(
        [near.reshape(8, rows), ghost_sum, got[0, 10:14], jnp.zeros((4, rows), jnp.float32)],
        axis=0,
    )
    got_blocks = lax.all_to_all(jnp.broadcast_to(chunk, (blocks,) + chunk.shape), "rad", 0, 0)
    shards = got_blocks[:, 0:8].reshape(blocks, 4, 2, rows)
    ghost = jnp.sum(got_blocks[:, 8:16], axis=0).reshape(2, 2, -1)
    first_row = got_blocks[0, 16:20].reshape(2, -1)
    return own.transpose(1, 0, 2).reshape(2, -1), shards, ghost, first_row


def arnoldi_coefs(gram):
    ss, spr, spi, sqr, sqi, pp, pqr, pqi, qq = [gram[i] for i in range(9)]
    cr, ci = spr / ss, spi / ss
    left_1 = pp - (spr * cr + spi * ci)
    norm_1 = left_1 / ss
    h10 = jnp.sqrt(norm_1)
    sxr = sqr - (cr * spr - ci * spi)
    sxi = sqi - (cr * spi + ci * spr)
    h01r, h01i = sxr / (ss * h10), sxi / (ss * h10)
    pxr, pxi = pqr - cr * pp, pqi - ci * pp
    yxr = pxr - (cr * sxr + ci * sxi)
    yxi = pxi - (cr * sxi - ci * sxr)
    scale = 1.0 / left_1
    d11r, d11i = yxr * scale, yxi * scale
    xx = (qq - 2.0 * (cr * pqr + ci * pqi) + (cr * cr + ci * ci) * pp) * scale
    left_2 = xx - (h01r * h01r + h01i * h01i) - (d11r * d11r + d11i * d11i)
    h21 = jnp.sqrt(left_2)
    poor = jnp.logical_not((left_1 > least_left * pp) & (left_2 > least_left * xx))
    zero = jnp.zeros_like(ss)
    hessenberg = jnp.stack(
        [
            jnp.stack([jnp.stack([cr + shift, h01r]), jnp.stack([h10, d11r + shift]), jnp.stack([zero, h21])]),
            jnp.stack([jnp.stack([ci, h01i]), jnp.stack([zero, d11i]), jnp.stack([zero, zero])]),
        ]
    )
    a = jnp.sqrt(ss)
    down = 1.0 / (a * h10 * h21)
    coef_q = down
    coef_pr, coef_pi = -(cr + d11r) * down, -(ci + d11i) * down
    coef_sr = (d11r * cr - d11i * ci) * down - h01r / (a * h21)
    coef_si = (d11r * ci + d11i * cr) * down - h01i / (a * h21)
    return hessenberg, (coef_q, coef_pr, coef_pi, coef_sr, coef_si), poor


def combine(coefs, s, p, q):
    coef_q, coef_pr, coef_pi, coef_sr, coef_si = coefs
    return coef_q * q + rotate(p, coef_pr, coef_pi) + rotate(s, coef_sr, coef_si)


def gram_parts(s, p, q):
    def real_of(left, right):
        return jnp.sum(left * right)

    def imag_of(left, right):
        return jnp.sum(left[0] * right[1] - left[1] * right[0])

    return jnp.stack(
        [
            real_of(s, s),
            real_of(s, p),
            imag_of(s, p),
            real_of(s, q),
            imag_of(s, q),
            real_of(p, p),
            real_of(p, q),
            imag_of(p, q),
            real_of(q, q),
        ]
    )


def step_by_step(
    inner_state,
    outer_state,
    inner_ham,
    inner_coupling,
    surface_amp,
    potential,
    laser_mix,
    partners,
    band_offsets,
    channel_group,
):
    block_order = inner_ham.shape[1]
    points, channels = outer_state.shape[1:]
    entries = float(
        lax.axis_size("rad") * block_order + lax.axis_size(both) * points * channels
    )
    block_index = lax.axis_index("rad")
    is_first = lax.axis_index(both) == 0
    member = (channel_group == block_index).astype(jnp.float32)
    masked_amp = surface_amp[0] * member[None, None, :]
    own_partners = lax.dynamic_index_in_dim(partners, block_index, 0, keepdims=False)
    own_offsets = lax.dynamic_index_in_dim(band_offsets, block_index, 0, keepdims=False)

    def total(value):
        return lax.psum(value, both) / entries

    def squares(vector):
        return jnp.sum(vector[0] * vector[0]) + jnp.sum(vector[1] * vector[1])

    start_len = jnp.sqrt(total(squares((inner_state, outer_state))))
    krylov = [(inner_state / start_len, outer_state / start_len)]
    hessenberg = jnp.zeros((2, TERMS + 1, TERMS), jnp.float32)
    for term_index in range(TERMS):
        inner_vec, outer_vec = krylov[term_index]
        ghost_part = jnp.einsum("pk,mki->pmi", inner_vec, masked_amp, precision=highest)
        row = jnp.where(is_first, outer_vec[:, 0], 0.0)
        own_vec, shards, ghost, first_row = exchange(inner_vec, ghost_part, row)
        result_in = jnp.dot(own_vec, inner_ham[0], precision=highest)
        for couple_index, window in enumerate(inner_windows(shards, own_partners, own_offsets)):
            result_in = result_in + jnp.dot(window, inner_coupling[0, couple_index], precision=highest)
        result_in = result_in + bloch_coef * jnp.einsum(
            "pi,ki->pk", first_row, masked_amp[0], precision=highest
        )
        low, high = neighbours(outer_vec, 2)
        low = jnp.where(is_first, ghost[:, ::-1], low)
        extended = jnp.concatenate([low, outer_vec, high], axis=1)
        image = (result_in, outer_apply(extended, potential, laser_mix, 0.0))
        for prior_index in range(term_index + 1):
            prior = krylov[prior_index]
            coefs = total(local_parts(prior, image))
            image = tuple(
                part - rotate(prior_part, coefs[0], coefs[1])
                for part, prior_part in zip(image, prior)
            )
            hessenberg = hessenberg.at[:, prior_index, term_index].set(coefs)
        new_length = jnp.sqrt(total(squares(image)))
        hessenberg = hessenberg.at[0, term_index + 1, term_index].set(new_length)
        krylov.append((image[0] / new_length, image[1] / new_length))
    return (krylov[-1][0], krylov[-1][1], hessenberg)


def body(*inputs):
    (
        inner_state,
        outer_state,
        inner_ham,
        inner_coupling,
        surface_amp,
        potential,
        laser_mix,
        partners,
        band_offsets,
        channel_group,
    ) = inputs
    block_order = inner_ham.shape[1]
    points, channels = outer_state.shape[1:]
    count = lax.axis_size(both)
    entries = float(lax.axis_size("rad") * block_order + count * points * channels)
    block_index = lax.axis_index("rad")
    position = lax.axis_index(both)
    is_first, is_last = position == 0, position == count - 1
    member = (channel_group == block_index).astype(jnp.float32)
    amp = surface_amp[0]
    own_partners = lax.dynamic_index_in_dim(partners, block_index, 0, keepdims=False)
    own_offsets = lax.dynamic_index_in_dim(band_offsets, block_index, 0, keepdims=False)

    def inner_image(own_vec, shards, first_row, inner_vec):
        result = jnp.dot(own_vec, inner_ham[0], precision=highest) - shift * inner_vec
        for couple_index, window in enumerate(inner_windows(shards, own_partners, own_offsets)):
            result = result + jnp.dot(window, inner_coupling[0, couple_index], precision=highest)
        return result + bloch_coef * jnp.einsum(
            "pi,ki->pk", first_row * member, amp[0], precision=highest
        )

    def ghost_of(inner_vec):
        return jnp.einsum("pk,mki->pmi", inner_vec, amp, precision=highest) * member

    carried = jnp.concatenate([outer_state, potential[None]], axis=0)
    low, high = neighbours(carried, 4)
    wide = jnp.concatenate([low, carried, high], axis=1)
    p_wide = outer_apply(wide[:2], wide[2, 2:-2], laser_mix, shift)
    p_low = jnp.where(is_first, 0.0, p_wide[:, :2])
    p_high = jnp.where(is_last, 0.0, p_wide[:, -2:])
    p_outer = p_wide[:, 2:-2]
    q_outer = outer_apply(jnp.concatenate([p_low, p_outer, p_high], axis=1), potential, laser_mix, shift)

    s_inner = inner_state
    own_vec, shards, ghost, first_row = exchange(
        s_inner, ghost_of(s_inner), jnp.where(is_first, outer_state[:, 0], 0.0)
    )
    p_inner = inner_image(own_vec, shards, first_row, s_inner)
    side = jnp.concatenate([ghost[:, ::-1], jnp.zeros((2, 4, channels), jnp.float32)], axis=1)
    p_edge = p_outer[:, 0:6].at[:, 0:2].add(
        jnp.where(is_first, outer_apply(side, jnp.zeros((2, channels)), laser_mix, 0.0), 0.0)
    )
    own_vec, shards, ghost, first_row = exchange(
        p_inner, ghost_of(p_inner), jnp.where(is_first, p_edge[:, 0], 0.0)
    )
    q_inner = inner_image(own_vec, shards, first_row, p_inner)
    p_low = jnp.where(is_first, ghost[:, ::-1], p_low)
    q_edge = outer_apply(jnp.concatenate([p_low, p_edge], axis=1), potential[:4], laser_mix, shift)

    parts = (
        gram_parts(outer_state[:, 4:], p_outer[:, 4:], q_outer[:, 4:])
        + gram_parts(outer_state[:, :4], p_edge[:, :4], q_edge)
        + gram_parts(s_inner, p_inner, q_inner)
    )
    sent = jnp.broadcast_to(jnp.pad(parts, (0, 7)), (count, 16))
    gram = jnp.sum(lax.all_to_all(sent, both, 0, 0), axis=0) / entries
    hessenberg, coefs, poor = arnoldi_coefs(gram)
    last_inner = combine(coefs, s_inner, p_inner, q_inner)
    p_all = jnp.concatenate([p_edge[:, :4], p_outer[:, 4:]], axis=1)
    q_all = jnp.concatenate([q_edge, q_outer[:, 4:]], axis=1)
    last_outer = combine(coefs, outer_state, p_all, q_all)

    def again(state):
        return (jnp.zeros((), jnp.bool_),) + step_by_step(*inputs)

    return lax.while_loop(
        lambda state: state[0], again, (poor, last_inner, last_outer, hessenberg)
    )[1:]


def solution(mesh):
    return jax.shard_map(
        body,
        mesh=mesh,
        in_specs=(
            P(None, ("rad", "chan")),
            P(None, ("rad", "chan"), None),
            P("rad", None, "chan"),
            P("rad", None, None, "chan"),
            P("rad", None, "chan", None),
            P(("rad", "chan"), None),
            P(),
            P(),
            P(),
            P(),
        ),
        out_specs=(P(None, ("rad", "chan")), P(None, ("rad", "chan"), None), P()),
        check_vma=False,
    )
```

time: 702 us -> 183 us (0.26)
  blocking collectives: 585 us -> 0 us
  waiting for transfers between devices: 0.53 us -> 26.8 us
  starting transfers between devices: 18 us -> 37.6 us
  local copies, waits for them, and re-layouts: 13.6 us -> 31.1 us
  matrix products: 25.5 us -> 36.1 us
  other arithmetic: 37.4 us -> 26.8 us
    psum x8 -> x0, blocking collectives: 522 us -> none  [the longest x3 192 us: body(): lax.psum(local_parts(krylov[prior_index], image), ('rad', 'chan')) / entries]
    all_gather x4 -> x0, blocking collectives: 63.2 us -> none  [the longest x2 32.3 us: body(): whole_vec = lax.all_gather(block_vec, 'rad', axis=1, tiled=True)]
    all_to_all x0 -> x5, waiting for transfers between devices: none -> 26.8 us  [the longest x2 11.8 us: exchange(): lax.all_to_all(jnp.broadcast_to(chunk, (strips,) + chunk.shape), 'chan',...]
    all_to_all x0 -> x5, starting transfers between devices: none -> 26.1 us  [the longest x2 10.8 us: exchange(): lax.all_to_all(jnp.broadcast_to(chunk, (blocks,) + chunk.shape), 'rad', 0...]
    another operation x2 -> x7, local copies, waits for them, and re-layouts: 0.61 us -> 17.5 us  [the longest x3 17.2 us: gram_parts(): jnp.stack([real_of(s, s), real_of(s, p), imag_of(s, p), real_of(s, q), im...]
    reduce_sum x16 -> x9, other arithmetic: 19.6 us -> 7.38 us  [the longest x2 4.04 us: real_of(): return jnp.sum(left * right)]
    dot_general x12 -> x14, matrix products: 25.5 us -> 36.1 us  [the longest x4 15.1 us: outer_apply(): jnp.einsum('prc,cd->prd', slope_rows, laser_mix, precision=highest)]
    add x0 -> x5, other arithmetic: none -> 7.4 us  [the longest x2 5.08 us: outer_apply(): kinetic_coef * laplace + (potential - moved) * centre_row]
  transfers between devices with their start and end apart: 4 -> 7, of which waited for: 1 -> 5; matrix products, arithmetic and copies ran while one was open for 3% -> 8% of each run, Pallas kernels for 0% -> 0%
where the time goes in v1:
time: 183 us; the launch traced here: 181 us
  starting transfers between devices  37.6 us (21%)
  matrix products  36.1 us (20%)
  local copies, waits for them, and re-layouts  31.1 us (17%)
  other arithmetic  26.8 us (15%)
  waiting for transfers between devices  26.8 us (15%)
  between operations  22.6 us (12%)
    another operation x3, local copies, waits for them, and re-layouts, gram_parts(): jnp.stack([real_of(s, s), real_of(s, p), imag_of(s, p), real_of(s, q), im...  17.2 us
    dot_general x4, matrix products, outer_apply(): jnp.einsum('prc,cd->prd', slope_rows, laser_mix, precision=highest)  15.1 us
    all_to_all x2, waiting for transfers between devices, exchange(): lax.all_to_all(jnp.broadcast_to(chunk, (strips,) + chunk.shape), 'chan',...  11.8 us
    all_to_all x2, starting transfers between devices, exchange(): lax.all_to_all(jnp.broadcast_to(chunk, (blocks,) + chunk.shape), 'rad', 0...  10.8 us
    all_to_all x2, starting transfers between devices, exchange(): lax.all_to_all(jnp.broadcast_to(chunk, (strips,) + chunk.shape), 'chan',...  10.3 us
    all_to_all x1, waiting for transfers between devices, body(): gram = jnp.sum(lax.all_to_all(sent, both, 0, 0), axis=0) / entries  9.83 us
    ppermute x1, starting transfers between devices, neighbours(): high = lax.ppermute(block[:, :width], both, backward)  9.51 us
    dot_general x2, matrix products, inner_image(): jnp.dot(own_vec, inner_ham[0], precision=highest) - shift * inner_vec  8.69 us
  transfers between devices with their start and end apart: 7, of which 5 were waited for; matrix products, arithmetic and copies ran while one was open for 8% of the time, Pallas kernels for 0%

profile of v1, /device:TPU:1, one launch (start us, length us, event | category | flops | bytes accessed | tf_op | source)
XLA Modules:
  0.0 181.0 jit_solution(10711612831910464336)
XLA Ops:
  0.7 0.9 pad_maximum_fusion.24
  1.6 9.5 %collective-permute-start.5 = (f32[3,4,512]{2,1,0:T(4,128)S(1)}, f32[3,4,512]{2,1,0:T(4,128)S(1)}, u32[]{:S(2)}, u32[]{:S(2)}) collective-permute-start(f32[3,4,512]{2,1,0:T(4,128)S(1)} %get-tuple-element.335), channel_id=1, source_target_pairs={{1,0},{2,1},{3,2},{4,3},{5,4},{6,5},{7,6},{8,7},{9,8},{10,9},{11,1... | collective-permute-start | bytes 73736 | tf_op jit(solution)/shard_map/ppermute | solution.py:45
  11.1 1.9 %collective-permute-start.4 = (f32[3,4,512]{2,1,0:T(4,128)S(1)}, f32[3,4,512]{2,1,0:T(4,128)S(1)}, u32[]{:S(2)}, u32[]{:S(2)}) collective-permute-start(f32[3,4,512]{2,1,0:T(4,128)S(1)} %get-tuple-element.334), channel_id=1, source_target_pairs={{0,1},{1,2},{2,3},{3,4},{4,5},{5,6},{6,7},{7,8},{8,9},{9,10},{10,1... | collective-permute-start | bytes 73736 | tf_op jit(solution)/shard_map/ppermute | solution.py:44
  13.2 1.8 %convolution_multiply_fusion.3 = f32[2,2,512]{2,0,1:T(2,128)S(1)} fusion(f32[1,2,256,512]{3,2,1,0:T(8,128)} %param.28, f32[512]{0:T(512)S(1)} %compare_convert_fusion.1, f32[2,256]{1,0:T(2,128)S(1)} %copy-done.26), kind=kOutput, calls=%fused_computation.225 | convolution fusion | flops 6293504 | bytes 1060864 | tf_op jit(solution)/shard_map/pk,mki->pmi/dot_general | solution.py:263
  23.5 1.5 pad_maximum_fusion.11
  25.0 5.5 %fusion.101 = f32[2,388,512]{2,1,0:T(8,128)S(1)} fusion(f32[3,392,512]{2,1,0:T(8,128)S(1)} %pad_maximum_fusion.11, f32[512,512]{1,0:T(8,128)S(1)} %copy-done.21, f32[3,4,512]{2,1,0:T(4,128)S(1)} %collective-permute-done.4, f32[1,384,512]{2,1,0:T(8,128)} %bitcast.52, f32[2,384,512]{2,1,0:T(8,128)S(1)} %copy-done, f32[3,4,512]{2,1,0:T(4,128)S(1)} %collective-permute-done.5), kind=kOutput, calls=%fused_computation.192 | convolution fusion | flops 2445058048 | bytes 8257536 | tf_op jit(solution)/shard_map/prc,cd->prd/dot_general | solution.py:58
  30.5 1.3 fusion.231
  31.8 0.7 broadcast_in_dim.65
  32.6 6.8 %all-to-all-start.4 = ((f32[16,16,256]{2,1,0:T(8,128)}), f32[16,16,256]{2,1,0:T(8,128)S(1)}, u32[]{:S(2)}, u32[]{:S(2)}) async-start(f32[16,16,256]{2,1,0:T(8,128)} %broadcast_in_dim.65), calls=%async_computation.4 | async-start | bytes 524288 | tf_op jit(solution)/shard_map/all_to_all | solution.py:90
  39.4 2.1 %fusion.153 = f32[388,512]{1,0:T(8,128)} fusion(f32[3,392,512]{2,1,0:T(8,128)} %copy-done.17), kind=kLoop, calls=%fused_computation.246 | loop fusion | flops 198656 | bytes 1589248 | tf_op jit(solution)/shard_map/mul | solution.py:61
  41.5 6.4 %all-to-all-done.4 = f32[16,16,256]{2,1,0:T(8,128)S(1)} async-done(((f32[16,16,256]{2,1,0:T(8,128)}), f32[16,16,256]{2,1,0:T(8,128)S(1)}, u32[]{:S(2)}, u32[]{:S(2)}) %all-to-all-start.4) | async-done | bytes 262176 | tf_op jit(solution)/shard_map/all_to_all | solution.py:90
  48.0 0.7 broadcast_in_dim.67
  48.7 5.4 %all-to-all-start.5 = ((f32[8,24,256]{2,1,0:T(8,128)}), f32[8,24,256]{2,1,0:T(8,128)S(1)}, u32[]{:S(2)}, u32[]{:S(2)}) async-start(f32[8,24,256]{2,1,0:T(8,128)} %broadcast_in_dim.67), calls=%async_computation.5 | async-start | bytes 393216 | tf_op jit(solution)/shard_map/all_to_all | solution.py:99
  54.2 3.9 %maximum_add_fusion.2 = f32[2,388,512]{2,1,0:T(8,128)S(1)} fusion(f32[1,388,512]{2,1,0:T(8,128)} %get-tuple-element.341, f32[1,388,512]{2,1,0:T(8,128)} %get-tuple-element.340, f32[3,392,512]{2,1,0:T(8,128)} %copy-done.17, f32[388,512]{1,0:T(8,128)} %fusion.153, f32[1,384,512]{2,1,0:T(8,128)} %bitcast.52, f32[2,384,512]{2,1,0:T(8,128)S(1)} %copy-done, ...), kind=kLoop, calls=%fused_computation.187 | loop fusion | flops 6754304 | bytes 11149312 | tf_op jit(solution)/shard_map/add | solution.py:60
  58.1 1.9 %all-to-all-done.5 = f32[8,24,256]{2,1,0:T(8,128)S(1)} async-done(((f32[8,24,256]{2,1,0:T(8,128)}), f32[8,24,256]{2,1,0:T(8,128)S(1)}, u32[]{:S(2)}, u32[]{:S(2)}) %all-to-all-start.5) | async-done | bytes 196640 | tf_op jit(solution)/shard_map/all_to_all | solution.py:99
  60.1 1.5 convolution_multiply_fusion.5
  61.9 1.9 %fusion.149 = f32[2,2,512]{2,1,0:T(2,128)S(1)} fusion(f32[512,512]{1,0:T(8,128)} %param.30, f32[2,2,512]{2,1,0:T(2,128)S(1)} %rev.12), kind=kOutput, calls=%fused_computation.240 | convolution fusion | flops 12589056 | bytes 1064960 | tf_op jit(solution)/shard_map/prc,cd->prd/dot_general | solution.py:58
  63.8 1.4 fusion.163
  65.2 1.4 fusion.167
  66.6 4.0 %fusion.130 = f32[2,256]{1,0:T(2,128)S(1)} fusion(f32[2,256]{1,0:T(2,128)S(1)} %convolution_multiply_fusion.5, f32[2,256]{1,0:T(2,128)S(1)} %fusion.163, f32[2,256]{1,0:T(2,128)S(1)} %fusion.167, f32[2,4096]{1,0:T(2,128)S(1)} %bitcast.277, f32[1,4096,256]{2,1,0:T(8,128)} %param.26, f32[2,256]{1,0:T(2,128)S(1)} %copy-done.26), kind=kOutput, calls=%fused_computation.229 | convolution fusion | flops 25168384 | bytes 4237312 | tf_op jit(solution)/shard_map/dot_general | solution.py:255
  70.6 1.8 %convolution_multiply_fusion.2 = f32[2,2,512]{2,0,1:T(2,128)S(1)} fusion(f32[1,2,256,512]{3,2,1,0:T(8,128)} %param.28, f32[512]{0:T(512)S(1)} %compare_convert_fusion.1, f32[2,256]{1,0:T(2,128)S(1)} %fusion.130), kind=kOutput, calls=%fused_computation.224 | convolution fusion | flops 6293504 | bytes 1060864 | tf_op jit(solution)/shard_map/pk,mki->pmi/dot_general | solution.py:263
  72.5 0.7 broadcast_in_dim.68
  73.3 3.5 %all-to-all-start.6 = ((f32[16,16,256]{2,1,0:T(8,128)}), f32[16,16,256]{2,1,0:T(8,128)S(1)}, u32[]{:S(2)}, u32[]{:S(2)}) async-start(f32[16,16,256]{2,1,0:T(8,128)} %broadcast_in_dim.68), calls=%async_computation.6 | async-start | bytes 524288 | tf_op jit(solution)/shard_map/all_to_all | solution.py:90
  76.8 2.1 %broadcast_add_fusion = f32[384,512]{1,0:T(8,128)} fusion(f32[384,512]{1,0:T(8,128)} %param.29), kind=kLoop, calls=%fused_computation.277 | loop fusion | flops 196608 | bytes 1572864 | tf_op jit(solution)/shard_map/sub | solution.py:61
  78.9 5.4 %all-to-all-done.6 = f32[16,16,256]{2,1,0:T(8,128)S(1)} async-done(((f32[16,16,256]{2,1,0:T(8,128)}), f32[16,16,256]{2,1,0:T(8,128)S(1)}, u32[]{:S(2)}, u32[]{:S(2)}) %all-to-all-start.6) | async-done | bytes 262176 | tf_op jit(solution)/shard_map/all_to_all | solution.py:90
  85.2 5.4 %all-to-all-start.7 = ((f32[8,24,256]{2,1,0:T(8,128)}), f32[8,24,256]{2,1,0:T(8,128)S(1)}, u32[]{:S(2)}, u32[]{:S(2)}) async-start(f32[8,24,256]{2,1,0:T(8,128)} %broadcast_in_dim.69), calls=%async_computation.7 | async-start | bytes 393216 | tf_op jit(solution)/shard_map/all_to_all | solution.py:99
  90.6 1.3 slice_add_fusion.2
  91.9 1.3 slice.863
  93.2 3.3 %all-to-all-done.7 = f32[8,24,256]{2,1,0:T(8,128)S(1)} async-done(((f32[8,24,256]{2,1,0:T(8,128)}), f32[8,24,256]{2,1,0:T(8,128)S(1)}, u32[]{:S(2)}, u32[]{:S(2)}) %all-to-all-start.7) | async-done | bytes 196640 | tf_op jit(solution)/shard_map/all_to_all | solution.py:99
  96.5 1.3 rev.13
  97.8 7.1 %fusion.112 = f32[2,384,512]{2,1,0:T(8,128)S(1)} fusion(f32[2,384,512]{2,1,0:T(8,128)} %slice.863, f32[2,2,512]{2,1,0:T(2,128)S(1)} %get-tuple-element.339, f32[2,2,512]{2,1,0:T(2,128)S(1)} %get-tuple-element.338, f32[512,512]{1,0:T(8,128)} %param.30), kind=kOutput, calls=%fused_computation.213 | convolution fusion | flops 2419851264 | bytes 4210688 | tf_op jit(solution)/shard_map/prc,cd->prd/dot_general | solution.py:58
  105.1 1.2 copy-done.19
  106.5 1.2 maximum_add_fusion.3
  107.7 3.3 %multiply_reduce_fusion.13 = (f32[]{:T(128)}, f32[]{:T(128)}, f32[]{:T(128)}, f32[]{:T(128)}, f32[]{:T(128)}, /*index=5*/f32[]{:T(128)}, f32[2,380,512]{2,1,0:T(8,128)}, f32[2,380,512]{2,1,0:T(8,128)}) fusion(f32[2,384,512]{2,1,0:T(8,128)S(1)} %maximum_add_fusion.3, f32[2,388,512]{2,1,0:T(8,128)S(1)} %maximum_add_fusion.2, f32[2,384,512]{2,1,0:T(8,128)S(1)} %copy-done), kind=kLoop, calls=%fused_computation.210 | loop fusion | flops 4669434 | bytes 7782424 | tf_op jit(solution)/shard_map/reduce_sum | solution.py:147
  111.0 1.8 subtract_reduce_fusion
  112.8 1.5 convolution_multiply_fusion.4
  114.4 1.4 fusion.161
  115.7 1.4 fusion.165
  117.2 4.7 %multiply_reduce_fusion.24 = (f32[]{:T(128)}, f32[]{:T(128)}, f32[]{:T(128)}, f32[]{:T(128)}, f32[]{:T(128)}, /*index=5*/f32[]{:T(128)}, f32[2,256]{1,0:T(2,128)S(1)}) fusion(f32[2,256]{1,0:T(2,128)S(1)} %fusion.130, f32[2,256]{1,0:T(2,128)S(1)} %copy-done.26, f32[2,256]{1,0:T(2,128)S(1)} %convolution_multiply_fusion.4, f32[2,256]{1,0:T(2,128)S(1)} %fusion.161, ...), kind=kOutput, calls=%fused_computation.359 | convolution fusion | flops 25174522 | bytes 4239384 | tf_op jit(solution)/shard_map/dot_general | solution.py:255
  123.3 0.8 multiply_reduce_fusion.21
  124.7 5.8 %stack.293 = f32[9]{0:T(128)S(1)} concatenate(f32[1]{0:T(128)} %bitcast.95, f32[1]{0:T(128)} %bitcast.96, f32[1]{0:T(128)} %bitcast.97, f32[1]{0:T(128)} %bitcast.106, f32[1]{0:T(128)} %bitcast.107, f32[1]{0:T(128)} %bitcast.108, f32[1]{0:T(128)} %bitcast.109, f32[1]{0:T(128)} %bitcast.110, f32[1]{0:T(128)} %bitcast.111), dimensions={0} | concatenate | bytes 72 | tf_op jit(solution)/shard_map/stack | solution.py:152
  130.5 5.8 %stack.271 = f32[9]{0:T(128)S(1)} concatenate(f32[1]{0:T(128)} %bitcast.51, f32[1]{0:T(128)} %bitcast.55, f32[1]{0:T(128)} %bitcast.56, f32[1]{0:T(128)} %bitcast.57, f32[1]{0:T(128)} %bitcast.58, f32[1]{0:T(128)} %bitcast.59, f32[1]{0:T(128)} %bitcast.60, f32[1]{0:T(128)} %bitcast.61, f32[1]{0:T(128)} %bitcast.62), dimensions={0} | concatenate | bytes 72 | tf_op jit(solution)/shard_map/stack | solution.py:152
  136.3 5.7 %stack.283 = f32[9]{0:T(128)S(1)} concatenate(f32[1]{0:T(128)} %bitcast.63, f32[1]{0:T(128)} %bitcast.67, f32[1]{0:T(128)} %bitcast.68, f32[1]{0:T(128)} %bitcast.89, f32[1]{0:T(128)} %bitcast.90, f32[1]{0:T(128)} %bitcast.91, f32[1]{0:T(128)} %bitcast.92, f32[1]{0:T(128)} %bitcast.93, f32[1]{0:T(128)} %bitcast.94), dimensions={0} | concatenate | bytes 72 | tf_op jit(solution)/shard_map/stack | solution.py:152
  142.6 5.0 %all-to-all-start.8 = ((f32[128,1,16]{2,1,0:T(1,128)}), f32[128,1,16]{2,1,0:T(1,128)S(1)}, u32[]{:S(2)}, u32[]{:S(2)}) async-start(f32[128,1,16]{2,1,0:T(1,128)} %broadcast_in_dim.70), calls=%async_computation.8 | async-start | bytes 131072 | tf_op jit(solution)/shard_map/all_to_all | solution.py:296
  147.7 9.8 %all-to-all-done.8 = f32[128,1,16]{2,1,0:T(1,128)S(1)} async-done(((f32[128,1,16]{2,1,0:T(1,128)}), f32[128,1,16]{2,1,0:T(1,128)S(1)}, u32[]{:S(2)}, u32[]{:S(2)}) %all-to-all-start.8) | async-done | bytes 8224 | tf_op jit(solution)/shard_map/all_to_all | solution.py:296
  173.3 1.4 multiply_subtract_fusion.6
  177.9 1.7 fusion.111
  179.7 1.3 copy.41
  (120 shorter events, 10.7 us)
Async XLA Ops:
  0.6 12.5 %copy-start = (f32[2,384,512]{2,1,0:T(8,128)S(1)}, f32[2,384,512]{2,1,0:T(8,128)}, u32[]{:S(2)}) copy-start(f32[2,384,512]{2,1,0:T(8,128)} %param.25) | copy-start | bytes 4718596
  0.6 12.4 %copy-start.27 = (s32[512]{0:T(512)S(1)}, s32[512]{0:T(512)}, u32[]{:S(2)}) copy-start(s32[512]{0:T(512)} %param.33) | copy-start | bytes 6148
  0.7 12.5 %copy-start.26 = (f32[2,256]{1,0:T(2,128)S(1)}, f32[2,256]{1,0:T(2,128)}, u32[]{:S(2)}) copy-start(f32[2,256]{1,0:T(2,128)} %param.24) | copy-start | bytes 6148
  0.7 14.4 %copy-start.28 = (s32[8,2]{0,1:T(2,128)S(1)}, s32[8,2]{0,1:T(2,128)}, u32[]{:S(2)}) copy-start(s32[8,2]{0,1:T(2,128)} %param.32) | copy-start | bytes 196
  0.7 14.4 %copy-start.29 = (s32[8,2]{0,1:T(2,128)S(1)}, s32[8,2]{0,1:T(2,128)}, u32[]{:S(2)}) copy-start(s32[8,2]{0,1:T(2,128)} %param.31) | copy-start | bytes 196
  1.6 21.8 %collective-permute-start.5 = (f32[3,4,512]{2,1,0:T(4,128)S(1)}, f32[3,4,512]{2,1,0:T(4,128)S(1)}, u32[]{:S(2)}, u32[]{:S(2)}) collective-permute-start(f32[3,4,512]{2,1,0:T(4,128)S(1)} %get-tuple-element.335), channel_id=1, source_target_pairs={{1,0},{2,1},{3,2},{4,3},{5,4},{6,5},{7,6},{8,7},{9,8},{10,9},{11,1... | collective-permute-start | bytes 73736 | tf_op jit(solution)/shard_map/ppermute | solution.py:45
  11.1 12.3 %collective-permute-start.4 = (f32[3,4,512]{2,1,0:T(4,128)S(1)}, f32[3,4,512]{2,1,0:T(4,128)S(1)}, u32[]{:S(2)}, u32[]{:S(2)}) collective-permute-start(f32[3,4,512]{2,1,0:T(4,128)S(1)} %get-tuple-element.334), channel_id=1, source_target_pairs={{0,1},{1,2},{2,3},{3,4},{4,5},{5,6},{6,7},{7,8},{8,9},{9,10},{10,1... | collective-permute-start | bytes 73736 | tf_op jit(solution)/shard_map/ppermute | solution.py:44
  15.7 0.6 copy-start.33
  22.1 25.8 %copy-start.35 = (f32[24]{0:T(128)}, f32[24]{0:T(128)S(1)}, u32[]{:S(2)}) copy-start(f32[24]{0:T(128)S(1)} %pad.135.clone) | copy-start | bytes 292
  23.4 1.6 copy-start.21
  25.0 5.5 %copy-start.17 = (f32[3,392,512]{2,1,0:T(8,128)}, f32[3,392,512]{2,1,0:T(8,128)S(1)}, u32[]{:S(2)}) copy-start(f32[3,392,512]{2,1,0:T(8,128)S(1)} %pad_maximum_fusion.11) | copy-start | bytes 7225348
  32.6 15.3 %all-to-all-start.4 = ((f32[16,16,256]{2,1,0:T(8,128)}), f32[16,16,256]{2,1,0:T(8,128)S(1)}, u32[]{:S(2)}, u32[]{:S(2)}) async-start(f32[16,16,256]{2,1,0:T(8,128)} %broadcast_in_dim.65), calls=%async_computation.4 | async-start | bytes 524288 | tf_op jit(solution)/shard_map/all_to_all | solution.py:90
  48.7 11.3 %all-to-all-start.5 = ((f32[8,24,256]{2,1,0:T(8,128)}), f32[8,24,256]{2,1,0:T(8,128)S(1)}, u32[]{:S(2)}, u32[]{:S(2)}) async-start(f32[8,24,256]{2,1,0:T(8,128)} %broadcast_in_dim.67), calls=%async_computation.5 | async-start | bytes 393216 | tf_op jit(solution)/shard_map/all_to_all | solution.py:99
  66.6 5.9 %copy-start.34 = (f32[16]{0:T(128)S(1)}, f32[16]{0:T(128)}, u32[]{:S(2)}) copy-start(f32[16]{0:T(128)} %copy-done.33) | copy-start | bytes 196
  72.4 12.0 %copy-start.36 = (f32[24]{0:T(128)S(1)}, f32[24]{0:T(128)}, u32[]{:S(2)}) copy-start(f32[24]{0:T(128)} %copy-done.35) | copy-start | bytes 292
  73.3 11.1 %all-to-all-start.6 = ((f32[16,16,256]{2,1,0:T(8,128)}), f32[16,16,256]{2,1,0:T(8,128)S(1)}, u32[]{:S(2)}, u32[]{:S(2)}) async-start(f32[16,16,256]{2,1,0:T(8,128)} %broadcast_in_dim.68), calls=%async_computation.6 | async-start | bytes 524288 | tf_op jit(solution)/shard_map/all_to_all | solution.py:90
  85.2 11.3 %all-to-all-start.7 = ((f32[8,24,256]{2,1,0:T(8,128)}), f32[8,24,256]{2,1,0:T(8,128)S(1)}, u32[]{:S(2)}, u32[]{:S(2)}) async-start(f32[8,24,256]{2,1,0:T(8,128)} %broadcast_in_dim.69), calls=%async_computation.7 | async-start | bytes 393216 | tf_op jit(solution)/shard_map/all_to_all | solution.py:99
  104.9 1.4 copy-start.19
  104.9 1.6 copy-start.25
  117.1 5.4 %copy-start.22 = (f32[512,512]{1,0:T(8,128)S(1)}, f32[512,512]{1,0:T(8,128)}, u32[]{:S(2)}) copy-start(f32[512,512]{1,0:T(8,128)} %param.30) | copy-start | bytes 3145732
  117.2 6.1 %copy-start.31 = (f32[4,512]{1,0:T(4,128)S(1)}, f32[4,512]{1,0:T(4,128)}, u32[]{:S(2)}) copy-start(f32[4,512]{1,0:T(4,128)} %slice_add_fusion.2) | copy-start | bytes 24580
  142.6 14.9 %all-to-all-start.8 = ((f32[128,1,16]{2,1,0:T(1,128)}), f32[128,1,16]{2,1,0:T(1,128)S(1)}, u32[]{:S(2)}, u32[]{:S(2)}) async-start(f32[128,1,16]{2,1,0:T(1,128)} %broadcast_in_dim.70), calls=%async_computation.8 | async-start | bytes 131072 | tf_op jit(solution)/shard_map/all_to_all | solution.py:296
  173.3 2.8 %copy-start.18 = (f32[2,380,512]{2,1,0:T(8,128)S(1)}, f32[2,380,512]{2,1,0:T(8,128)}, u32[]{:S(2)}) copy-start(f32[2,380,512]{2,1,0:T(8,128)} %get-tuple-element.336) | copy-start | bytes 4669444
  176.1 1.4 copy-start.20
  176.1 1.6 copy-start.23
  176.1 1.8 %copy-start.24 = (f32[1,384,512]{2,1,0:T(8,128)S(1)}, f32[1,384,512]{2,1,0:T(8,128)}, u32[]{:S(2)}) copy-start(f32[1,384,512]{2,1,0:T(8,128)} %get-tuple-element.346) | copy-start | bytes 2359300
  177.9 1.7 copy-start.30

commit v2 on v1

--- a/solution.py
+++ b/solution.py
@@ -1,6 +1,8 @@
 import jax
 import jax.numpy as jnp
 from jax import lax
+from jax.experimental import pallas as pl
+from jax.experimental.pallas import tpu as pltpu
 from jax.sharding import PartitionSpec as P
 
 STRIP = 256
@@ -101,67 +103,6 @@
     ghost = jnp.sum(got_blocks[:, 8:16], axis=0).reshape(2, 2, -1)
     first_row = got_blocks[0, 16:20].reshape(2, -1)
     return own.transpose(1, 0, 2).reshape(2, -1), shards, ghost, first_row
-
-
-def arnoldi_coefs(gram):
-    ss, spr, spi, sqr, sqi, pp, pqr, pqi, qq = [gram[i] for i in range(9)]
-    cr, ci = spr / ss, spi / ss
-    left_1 = pp - (spr * cr + spi * ci)
-    norm_1 = left_1 / ss
-    h10 = jnp.sqrt(norm_1)
-    sxr = sqr - (cr * spr - ci * spi)
-    sxi = sqi - (cr * spi + ci * spr)
-    h01r, h01i = sxr / (ss * h10), sxi / (ss * h10)
-    pxr, pxi = pqr - cr * pp, pqi - ci * pp
-    yxr = pxr - (cr * sxr + ci * sxi)
-    yxi = pxi - (cr * sxi - ci * sxr)
-    scale = 1.0 / left_1
-    d11r, d11i = yxr * scale, yxi * scale
-    xx = (qq - 2.0 * (cr * pqr + ci * pqi) + (cr * cr + ci * ci) * pp) * scale
-    left_2 = xx - (h01r * h01r + h01i * h01i) - (d11r * d11r + d11i * d11i)
-    h21 = jnp.sqrt(left_2)
-    poor = jnp.logical_not((left_1 > least_left * pp) & (left_2 > least_left * xx))
-    zero = jnp.zeros_like(ss)
-    hessenberg = jnp.stack(
-        [
-            jnp.stack([jnp.stack([cr + shift, h01r]), jnp.stack([h10, d11r + shift]), jnp.stack([zero, h21])]),
-            jnp.stack([jnp.stack([ci, h01i]), jnp.stack([zero, d11i]), jnp.stack([zero, zero])]),
-        ]
-    )
-    a = jnp.sqrt(ss)
-    down = 1.0 / (a * h10 * h21)
-    coef_q = down
-    coef_pr, coef_pi = -(cr + d11r) * down, -(ci + d11i) * down
-    coef_sr = (d11r * cr - d11i * ci) * down - h01r / (a * h21)
-    coef_si = (d11r * ci + d11i * cr) * down - h01i / (a * h21)
-    return hessenberg, (coef_q, coef_pr, coef_pi, coef_sr, coef_si), poor
-
-
-def combine(coefs, s, p, q):
-    coef_q, coef_pr, coef_pi, coef_sr, coef_si = coefs
-    return coef_q * q + rotate(p, coef_pr, coef_pi) + rotate(s, coef_sr, coef_si)
-
-
-def gram_parts(s, p, q):
-    def real_of(left, right):
-        return jnp.sum(left * right)
-
-    def imag_of(left, right):
-        return jnp.sum(left[0] * right[1] - left[1] * right[0])
-
-    return jnp.stack(
-        [
-            real_of(s, s),
-            real_of(s, p),
-            imag_of(s, p),
-            real_of(s, q),
-            imag_of(s, q),
-            real_of(p, p),
-            real_of(p, q),
-            imag_of(p, q),
-            real_of(q, q),
-        ]
-    )
 
 
 def step_by_step(
@@ -226,6 +167,379 @@
     return (krylov[-1][0], krylov[-1][1], hessenberg)
 
 
+side_rows = 8
+piece = 16
+vmem_bytes = 24 * 2**20
+
+
+def whole():
+    return pl.BlockSpec(memory_space=pltpu.VMEM)
+
+
+def scalars():
+    return pl.BlockSpec(memory_space=pltpu.SMEM)
+
+
+def run(kernel, outs, args, in_specs, scratch=()):
+    return pl.pallas_call(
+        kernel,
+        out_shape=[jax.ShapeDtypeStruct(shape, jnp.float32) for shape in outs],
+        in_specs=in_specs,
+        out_specs=[whole()] * len(outs),
+        scratch_shapes=list(scratch),
+        compiler_params=pltpu.CompilerParams(vmem_limit_bytes=vmem_bytes),
+    )(*args)
+
+
+def two(x):
+    high = x.astype(jnp.bfloat16)
+    return high, (x - high.astype(jnp.float32)).astype(jnp.bfloat16)
+
+
+def both_halves(x):
+    high, low = two(x)
+    rest = jnp.zeros((16 - 2 * x.shape[0], x.shape[1]), jnp.float32)
+    return jnp.concatenate([high.astype(jnp.float32), low.astype(jnp.float32), rest], axis=0).astype(jnp.bfloat16)
+
+
+def few_rows_dot(x, weights, flipped=False):
+    rows = x.shape[0]
+    lhs = both_halves(x)
+    dims = (((1,), (1 if flipped else 0,)), ((), ()))
+    total = sum(
+        lax.dot_general(lhs, part, dims, preferred_element_type=jnp.float32) for part in two(weights)
+    )
+    return total[:rows] + total[rows : 2 * rows]
+
+
+def write_chunk(out_ref, inner_vec, ghosts, row):
+    half = inner_vec.shape[1]
+    chunk = jnp.concatenate(
+        [
+            ghosts[:, :half],
+            ghosts[:, half:],
+            inner_vec,
+            row[:, :half],
+            row[:, half:],
+            jnp.zeros((2, half), jnp.float32),
+        ],
+        axis=0,
+    )
+    for strip in range(out_ref.shape[0]):
+        out_ref[strip] = chunk
+
+
+def ghost_rows(inner_vec, amp_ref, member):
+    return jnp.concatenate(
+        [few_rows_dot(inner_vec, amp_ref[0, radius]) * member for radius in range(2)], axis=0
+    )
+
+
+def member_of(group_ref, place_ref):
+    return jnp.where(group_ref[...] == place_ref[0], 1.0, 0.0)
+
+
+def start_kernel(place_ref, inner_ref, head_ref, amp_ref, group_ref, out_ref):
+    inner_vec = inner_ref[...]
+    is_first = place_ref[2] == 1
+    row = jnp.where(is_first, head_ref[:, 0, :], 0.0)
+    write_chunk(out_ref, inner_vec, ghost_rows(inner_vec, amp_ref, member_of(group_ref, place_ref)), row)
+
+
+def mix_in(out_ref, high_ref, low_ref, mix_ref, places, chunk):
+    mix_high, mix_low = two(mix_ref[...])
+    for part in range(2):
+        for first in range(0, places, chunk):
+            rows = pl.ds(first, chunk)
+            high, low = high_ref[1 - part, rows], low_ref[1 - part, rows]
+            mixed = (
+                jnp.dot(high, mix_low, preferred_element_type=jnp.float32)
+                + jnp.dot(low, mix_high, preferred_element_type=jnp.float32)
+                + jnp.dot(high, mix_high, preferred_element_type=jnp.float32)
+            )
+            if part == 0:
+                out_ref[part, rows] = out_ref[part, rows] + mixed
+            else:
+                out_ref[part, rows] = out_ref[part, rows] - mixed
+
+
+def stencils(load):
+    before_2, before_1, here, after_1, after_2 = [load(k) for k in range(-2, 3)]
+    kinetic = kinetic_coef * (16.0 * (before_1 + after_1) - (before_2 + after_2) - 30.0 * here)
+    slope = slope_coef * ((before_2 - after_2) + 8.0 * (after_1 - before_1))
+    return kinetic, slope, here
+
+
+def first_outer_kernel(
+    place_ref, state_ref, low_ref, high_ref, pot_ref, mix_ref, out_ref, wide_ref, slope_h, slope_l
+):
+    points = state_ref.shape[1]
+    places = points + 2 * side_rows
+    for part in range(2):
+        wide_ref[part, 0:16] = jnp.zeros((16, state_ref.shape[2]), jnp.float32)
+        wide_ref[part, 12:16] = low_ref[part]
+        wide_ref[part, 16 : 16 + points] = state_ref[part]
+        wide_ref[part, 16 + points : 32 + points] = jnp.zeros((16, state_ref.shape[2]), jnp.float32)
+        wide_ref[part, 16 + points : 20 + points] = high_ref[part]
+    low_pot = jnp.concatenate([jnp.zeros((4, pot_ref.shape[1]), jnp.float32), low_ref[2]], axis=0)
+    high_pot = jnp.concatenate([high_ref[2], jnp.zeros((4, pot_ref.shape[1]), jnp.float32)], axis=0)
+    for part in range(2):
+        for first in range(0, places, piece):
+            kinetic, slope, here = stencils(
+                lambda k, part=part, first=first: wide_ref[part, 8 + first + k : 8 + first + k + piece]
+            )
+            if first == 0:
+                pot = jnp.concatenate([low_pot, pot_ref[0:8]], axis=0)
+            elif first + piece == places:
+                pot = jnp.concatenate([pot_ref[points - 8 : points], high_pot], axis=0)
+            else:
+                pot = pot_ref[first - 8 : first + 8]
+            out_ref[part, first : first + piece] = kinetic + (pot - shift) * here
+            slope_h[part, first : first + piece], slope_l[part, first : first + piece] = two(slope)
+    mix_in(out_ref, slope_h, slope_l, mix_ref, places, places // 5)
+    is_first, is_last = place_ref[2] == 1, place_ref[3] == 1
+    for part in range(2):
+        out_ref[part, 0:side_rows] = jnp.where(is_first, 0.0, out_ref[part, 0:side_rows])
+        rows = pl.ds(points + side_rows, side_rows)
+        out_ref[part, rows] = jnp.where(is_last, 0.0, out_ref[part, rows])
+
+
+def products(s, p, q):
+    return [
+        s[0] * s[0] + s[1] * s[1],
+        s[0] * p[0] + s[1] * p[1],
+        s[0] * p[1] - s[1] * p[0],
+        s[0] * q[0] + s[1] * q[1],
+        s[0] * q[1] - s[1] * q[0],
+        p[0] * p[0] + p[1] * p[1],
+        p[0] * q[0] + p[1] * q[1],
+        p[0] * q[1] - p[1] * q[0],
+        q[0] * q[0] + q[1] * q[1],
+    ]
+
+
+def folded(x):
+    columns = sum(x[:, k : k + 128] for k in range(0, x.shape[1], 128))
+    return sum(columns[k : k + 8] for k in range(0, x.shape[0], 8))
+
+
+def second_outer_kernel(wide_ref, state_ref, pot_ref, mix_ref, out_ref, gram_ref, slope_h, slope_l):
+    points = state_ref.shape[1]
+    for part in range(2):
+        for first in range(0, points, piece):
+            kinetic, slope, here = stencils(
+                lambda k, part=part, first=first: wide_ref[part, 8 + first + k : 8 + first + k + piece]
+            )
+            rows = pl.ds(first, piece)
+            out_ref[part, rows] = kinetic + (pot_ref[rows] - shift) * here
+            slope_h[part, rows], slope_l[part, rows] = two(slope)
+    mix_in(out_ref, slope_h, slope_l, mix_ref, points, points // 4)
+    gram_ref[...] = jnp.zeros_like(gram_ref)
+    for first in range(0, points, 8):
+        entries = products(
+            [state_ref[part, first : first + 8] for part in range(2)],
+            [wide_ref[part, 8 + first : 16 + first] for part in range(2)],
+            [out_ref[part, first : first + 8] for part in range(2)],
+        )
+        for k, entry in enumerate(entries):
+            if first == 0:
+                entry = jnp.where(lax.broadcasted_iota(jnp.int32, entry.shape, 0) < 4, 0.0, entry)
+            gram_ref[k] = gram_ref[k] + folded(entry)
+
+
+def block_kernel(got_ref, ham_ref, out_ref):
+    rows = ham_ref.shape[2]
+    total = jnp.zeros((16, rows), jnp.float32)
+    for strip in range(got_ref.shape[0]):
+        lhs = both_halves(got_ref[strip, 8:10])
+        for part in two(ham_ref[0, strip * rows : (strip + 1) * rows]):
+            total = total + jnp.dot(lhs, part, preferred_element_type=jnp.float32)
+    out_ref[...] = total[0:2] + total[2:4]
+
+
+def inner_result(block_ref, inner_ref, window_refs, coupling_ref, amp_ref, member, row):
+    result = block_ref[...] - shift * inner_ref[...]
+    for couple_index, window_ref in enumerate(window_refs):
+        result = result + few_rows_dot(window_ref[...], coupling_ref[0, couple_index])
+    return result + bloch_coef * few_rows_dot(row * member, amp_ref[0, 0], flipped=True)
+
+
+def unpacked(sums_ref):
+    ghosts = jnp.concatenate([sums_ref[0:4], sums_ref[4:8]], axis=1)
+    row = jnp.concatenate([sums_ref[8:10], sums_ref[10:12]], axis=1)
+    return ghosts, row
+
+
+def between_kernel(
+    place_ref, block_ref, inner_ref, window_a, window_b, sums_ref, coupling_ref, amp_ref, group_ref, wide_ref, mix_ref,
+    image_ref, chunk_ref, head_ref,
+):
+    member = member_of(group_ref, place_ref)
+    ghosts, row = unpacked(sums_ref)
+    image = inner_result(block_ref, inner_ref, (window_a, window_b), coupling_ref, amp_ref, member, row)
+    image_ref[...] = image
+    near, far = ghosts[0:2], ghosts[2:4]
+    kinetic = [kinetic_coef * (16.0 * near - far), -kinetic_coef * near]
+    slope = jnp.concatenate([slope_coef * (far - 8.0 * near), slope_coef * near], axis=0)
+    mixed = few_rows_dot(slope, mix_ref[...])
+    is_first = place_ref[2] == 1
+    rows = []
+    for part in range(2):
+        extra = [
+            kinetic[k][part : part + 1]
+            + (mixed[2 * k + 1 : 2 * k + 2] if part == 0 else -mixed[2 * k : 2 * k + 1])
+            for k in range(2)
+        ]
+        extra = jnp.concatenate(extra + [jnp.zeros((6, near.shape[1]), jnp.float32)], axis=0)
+        head = wide_ref[part, 8:16] + jnp.where(is_first, extra, 0.0)
+        head_ref[part] = head
+        rows.append(head[0:1])
+    row = jnp.where(is_first, jnp.concatenate(rows, axis=0), 0.0)
+    write_chunk(chunk_ref, image, ghost_rows(image, amp_ref, member), row)
+
+
+def last_kernel(
+    place_ref, block_ref, inner_ref, window_a, window_b, sums_ref, coupling_ref, amp_ref, group_ref, wide_ref, mix_ref,
+    head_ref, state_ref, start_ref, second_ref, pot_ref, gram_in_ref,
+    image_ref, out_ref, parts_ref, edge_ref,
+):
+    member = member_of(group_ref, place_ref)
+    ghosts, row = unpacked(sums_ref)
+    image = inner_result(block_ref, inner_ref, (window_a, window_b), coupling_ref, amp_ref, member, row)
+    image_ref[...] = image
+    is_first = place_ref[2] == 1
+    kinetic, slopes = [], []
+    for part in range(2):
+        edge_ref[part, 0:8] = wide_ref[part, 0:8]
+        ghost = jnp.concatenate([ghosts[2 + part : 3 + part], ghosts[part : part + 1]], axis=0)
+        edge_ref[part, 6:8] = jnp.where(is_first, ghost, wide_ref[part, 6:8])
+        edge_ref[part, 8:16] = head_ref[part]
+        edge_ref[part, 16:24] = wide_ref[part, 16:24]
+        inner, slope, here = stencils(lambda k, part=part: edge_ref[part, 8 + k : 16 + k])
+        kinetic.append(inner + (pot_ref[0:8] - shift) * here)
+        slopes.append(slope)
+    mixed = few_rows_dot_wide(jnp.concatenate(slopes, axis=0), mix_ref[...])
+    q = [kinetic[0] + mixed[8:16], kinetic[1] - mixed[0:8]]
+    top = lax.broadcasted_iota(jnp.int32, q[0].shape, 0) < 4
+    for part in range(2):
+        q[part] = jnp.where(top, q[part], second_ref[part, 0:8])
+        out_ref[part] = q[part]
+    edge = products([state_ref[part, 0:8] for part in range(2)], [head_ref[part] for part in range(2)], q)
+    start, inner = start_ref[...], inner_ref[...]
+    inside = products(
+        [start[0:1], start[1:2]], [inner[0:1], inner[1:2]], [image[0:1], image[1:2]]
+    )
+    lane = lax.broadcasted_iota(jnp.int32, (1, 128), 1)
+    sums = jnp.zeros((1, 128), jnp.float32)
+    for k in range(9):
+        tile = gram_in_ref[k] + folded(jnp.where(top, edge[k], 0.0))
+        line = jnp.sum(tile, axis=0, keepdims=True) + inside[k][:, :128] + inside[k][:, 128:]
+        sums = jnp.where(lane == k, jnp.sum(line, axis=1, keepdims=True), sums)
+    parts_ref[...] = jnp.broadcast_to(sums, parts_ref.shape)
+
+
+def few_rows_dot_wide(x, weights):
+    high, low = two(x)
+    weight_high, weight_low = two(weights)
+    return (
+        jnp.dot(high, weight_low, preferred_element_type=jnp.float32)
+        + jnp.dot(low, weight_high, preferred_element_type=jnp.float32)
+        + jnp.dot(high, weight_high, preferred_element_type=jnp.float32)
+    )
+
+
+def arnoldi_coefs(gram):
+    ss, spr, spi, sqr, sqi, pp, pqr, pqi, qq = gram
+    cr, ci = spr / ss, spi / ss
+    left_1 = pp - (spr * cr + spi * ci)
+    h10 = jnp.sqrt(left_1 / ss)
+    sxr = sqr - (cr * spr - ci * spi)
+    sxi = sqi - (cr * spi + ci * spr)
+    h01r, h01i = sxr / (ss * h10), sxi / (ss * h10)
+    pxr, pxi = pqr - cr * pp, pqi - ci * pp
+    yxr = pxr - (cr * sxr + ci * sxi)
+    yxi = pxi - (cr * sxi - ci * sxr)
+    scale = 1.0 / left_1
+    h11r, h11i = yxr * scale, yxi * scale
+    xx = (qq - 2.0 * (cr * pqr + ci * pqi) + (cr * cr + ci * ci) * pp) * scale
+    left_2 = xx - (h01r * h01r + h01i * h01i) - (h11r * h11r + h11i * h11i)
+    h21 = jnp.sqrt(left_2)
+    fine = (left_1 > least_left * pp) & (left_2 > least_left * xx)
+    poor = jnp.where(fine, 0.0, 1.0)
+    zero = jnp.zeros_like(ss)
+    entries = [cr + shift, h01r, h10, h11r + shift, zero, h21, ci, h01i, zero, h11i, zero, zero]
+    a = jnp.sqrt(ss)
+    coef_q = 1.0 / (a * h10 * h21)
+    coef_p = (-(cr + h11r) * coef_q, -(ci + h11i) * coef_q)
+    coef_s = (
+        (h11r * cr - h11i * ci) * coef_q - h01r / (a * h21),
+        (h11r * ci + h11i * cr) * coef_q - h01i / (a * h21),
+    )
+    return entries, (coef_q, coef_p, coef_s), poor
+
+
+def combined(coefs, s, p, q):
+    coef_q, coef_p, coef_s = coefs
+    return (
+        coef_q * q[0] + coef_p[0] * p[0] - coef_p[1] * p[1] + coef_s[0] * s[0] - coef_s[1] * s[1],
+        coef_q * q[1] + coef_p[0] * p[1] + coef_p[1] * p[0] + coef_s[0] * s[1] + coef_s[1] * s[0],
+    )
+
+
+def finish_kernel(
+    entries, parts_ref, start_ref, inner_ref, image_ref, state_ref, wide_ref, second_ref, head_ref, edge_ref,
+    inner_out, outer_out, hess_out, poor_out,
+):
+    step = pl.program_id(0)
+    count = outer_out.shape[1]
+    sums = jnp.sum(parts_ref[...], axis=0, keepdims=True) * (1.0 / entries)
+    lane = lax.broadcasted_iota(jnp.int32, sums.shape, 1)
+    gram = [jnp.sum(jnp.where(lane == k, sums, 0.0), axis=1, keepdims=True) for k in range(9)]
+    values, coefs, poor = arnoldi_coefs(gram)
+    rows = pl.ds(pl.multiple_of(step * count, 8), count)
+    wide_rows = pl.ds(pl.multiple_of(step * count + side_rows, 8), count)
+    outer_out[0], outer_out[1] = combined(
+        coefs,
+        [state_ref[part, rows] for part in range(2)],
+        [wide_ref[part, wide_rows] for part in range(2)],
+        [second_ref[part, rows] for part in range(2)],
+    )
+
+    @pl.when(step == 0)
+    def _():
+        outer_out[0, 0:8], outer_out[1, 0:8] = combined(
+            coefs,
+            [state_ref[part, 0:8] for part in range(2)],
+            [head_ref[part] for part in range(2)],
+            [edge_ref[part] for part in range(2)],
+        )
+        inner_out[0:1], inner_out[1:2] = combined(
+            coefs, *[[ref[0:1], ref[1:2]] for ref in (start_ref, inner_ref, image_ref)]
+        )
+        line = jnp.zeros((1, 128), jnp.float32)
+        for k, value in enumerate(values):
+            line = jnp.where(lane == k, value, line)
+        hess_out[...] = line
+        poor_out[...] = jnp.broadcast_to(poor, poor_out.shape)
+
+
+def across_blocks(sums, near):
+    blocks, strips = lax.axis_size("rad"), lax.axis_size("chan")
+    chips = blocks // 2
+    core = lax.rem(lax.axis_index("rad"), 2)
+    mine = jnp.concatenate([sums, near], axis=0)
+    other = lax.ppermute(mine, "rad", [(i, i ^ 1) for i in range(blocks)])
+    sums = sums + other[:12]
+    first = jnp.where(core == 0, near, other[12:])
+    second = jnp.where(core == 0, other[12:], near)
+    mine = jnp.concatenate([sums, first, second], axis=0)
+    got = [mine] + [
+        lax.ppermute(mine, "rad", [(i, (i + 2 * step) % blocks) for i in range(blocks)]) for step in range(1, chips)
+    ]
+    sums = sum(part[:12] for part in got)
+    return sums, jnp.stack([part[12 + 8 * k : 20 + 8 * k] for part in got for k in range(2)])
+
+
 def body(*inputs):
     (
         inner_state,
@@ -239,72 +553,102 @@
         band_offsets,
         channel_group,
     ) = inputs
-    block_order = inner_ham.shape[1]
+    block_order, rows = inner_ham.shape[1:]
     points, channels = outer_state.shape[1:]
     count = lax.axis_size(both)
-    entries = float(lax.axis_size("rad") * block_order + count * points * channels)
-    block_index = lax.axis_index("rad")
+    blocks, strips = lax.axis_size("rad"), lax.axis_size("chan")
+    entries = float(blocks * block_order + count * points * channels)
+    block_index, chan_index = lax.axis_index("rad"), lax.axis_index("chan")
     position = lax.axis_index(both)
-    is_first, is_last = position == 0, position == count - 1
-    member = (channel_group == block_index).astype(jnp.float32)
-    amp = surface_amp[0]
+    place = jnp.stack(
+        [block_index, chan_index, (position == 0).astype(jnp.int32), (position == count - 1).astype(jnp.int32)]
+    )
+    group = channel_group.reshape(1, channels)
     own_partners = lax.dynamic_index_in_dim(partners, block_index, 0, keepdims=False)
     own_offsets = lax.dynamic_index_in_dim(band_offsets, block_index, 0, keepdims=False)
-
-    def inner_image(own_vec, shards, first_row, inner_vec):
-        result = jnp.dot(own_vec, inner_ham[0], precision=highest) - shift * inner_vec
-        for couple_index, window in enumerate(inner_windows(shards, own_partners, own_offsets)):
-            result = result + jnp.dot(window, inner_coupling[0, couple_index], precision=highest)
-        return result + bloch_coef * jnp.einsum(
-            "pi,ki->pk", first_row * member, amp[0], precision=highest
-        )
-
-    def ghost_of(inner_vec):
-        return jnp.einsum("pk,mki->pmi", inner_vec, amp, precision=highest) * member
-
+    slots = lax.rem(block_index // 2 - own_partners // 2 + blocks // 2, blocks // 2) * 2 + lax.rem(own_partners, 2)
+    head = outer_state[:, 0:8]
+    places = points + 2 * side_rows
+
+    def exchanged(chunk):
+        got = lax.all_to_all(chunk, "chan", 0, 0)
+        sums = jnp.concatenate([jnp.sum(got[:, 0:8], axis=0), got[0, 10:14]], axis=0)
+        padded = jnp.pad(got[:, 8:10], ((2, 1), (0, 0), (0, 0)))
+        near = lax.dynamic_slice_in_dim(padded, chan_index, 4, 0).reshape(8, rows)
+        sums, shards = across_blocks(sums, near)
+        windows = inner_windows(shards.reshape(blocks, 4, 2, rows), slots, own_offsets)
+        (block_part,) = run(block_kernel, [(2, rows)], (got, inner_ham), [whole()] * 2)
+        return block_part, windows, sums
+
+    (chunk,) = run(
+        start_kernel,
+        [(strips, 16, rows)],
+        (place, inner_state, head, surface_amp, group),
+        [scalars()] + [whole()] * 4,
+    )
     carried = jnp.concatenate([outer_state, potential[None]], axis=0)
     low, high = neighbours(carried, 4)
-    wide = jnp.concatenate([low, carried, high], axis=1)
-    p_wide = outer_apply(wide[:2], wide[2, 2:-2], laser_mix, shift)
-    p_low = jnp.where(is_first, 0.0, p_wide[:, :2])
-    p_high = jnp.where(is_last, 0.0, p_wide[:, -2:])
-    p_outer = p_wide[:, 2:-2]
-    q_outer = outer_apply(jnp.concatenate([p_low, p_outer, p_high], axis=1), potential, laser_mix, shift)
-
-    s_inner = inner_state
-    own_vec, shards, ghost, first_row = exchange(
-        s_inner, ghost_of(s_inner), jnp.where(is_first, outer_state[:, 0], 0.0)
-    )
-    p_inner = inner_image(own_vec, shards, first_row, s_inner)
-    side = jnp.concatenate([ghost[:, ::-1], jnp.zeros((2, 4, channels), jnp.float32)], axis=1)
-    p_edge = p_outer[:, 0:6].at[:, 0:2].add(
-        jnp.where(is_first, outer_apply(side, jnp.zeros((2, channels)), laser_mix, 0.0), 0.0)
-    )
-    own_vec, shards, ghost, first_row = exchange(
-        p_inner, ghost_of(p_inner), jnp.where(is_first, p_edge[:, 0], 0.0)
-    )
-    q_inner = inner_image(own_vec, shards, first_row, p_inner)
-    p_low = jnp.where(is_first, ghost[:, ::-1], p_low)
-    q_edge = outer_apply(jnp.concatenate([p_low, p_edge], axis=1), potential[:4], laser_mix, shift)
-
-    parts = (
-        gram_parts(outer_state[:, 4:], p_outer[:, 4:], q_outer[:, 4:])
-        + gram_parts(outer_state[:, :4], p_edge[:, :4], q_edge)
-        + gram_parts(s_inner, p_inner, q_inner)
-    )
-    sent = jnp.broadcast_to(jnp.pad(parts, (0, 7)), (count, 16))
-    gram = jnp.sum(lax.all_to_all(sent, both, 0, 0), axis=0) / entries
-    hessenberg, coefs, poor = arnoldi_coefs(gram)
-    last_inner = combine(coefs, s_inner, p_inner, q_inner)
-    p_all = jnp.concatenate([p_edge[:, :4], p_outer[:, 4:]], axis=1)
-    q_all = jnp.concatenate([q_edge, q_outer[:, 4:]], axis=1)
-    last_outer = combine(coefs, outer_state, p_all, q_all)
+    (wide,) = run(
+        first_outer_kernel,
+        [(2, places, channels)],
+        (place, outer_state, low, high, potential, laser_mix),
+        [scalars()] + [whole()] * 5,
+        [
+            pltpu.VMEM((2, points + 32, channels), jnp.float32),
+            pltpu.VMEM((2, places, channels), jnp.bfloat16),
+            pltpu.VMEM((2, places, channels), jnp.bfloat16),
+        ],
+    )
+    block_part, windows, sums = exchanged(chunk)
+    p_inner, chunk, p_head = run(
+        between_kernel,
+        [(2, rows), (strips, 16, rows), (2, 8, channels)],
+        (place, block_part, inner_state, *windows, sums, inner_coupling, surface_amp, group, wide, laser_mix),
+        [scalars()] + [whole()] * 10,
+    )
+    second, gram = run(
+        second_outer_kernel,
+        [(2, points, channels), (9, 8, 128)],
+        (wide, outer_state, potential, laser_mix),
+        [whole()] * 4,
+        [pltpu.VMEM((2, points, channels), jnp.bfloat16)] * 2,
+    )
+    block_part, windows, sums = exchanged(chunk)
+    q_inner, q_head, parts = run(
+        last_kernel,
+        [(2, rows), (2, 8, channels), (count, 128)],
+        (
+            place, block_part, p_inner, *windows, sums, inner_coupling, surface_amp, group, wide, laser_mix,
+            p_head, head, inner_state, second, potential, gram,
+        ),
+        [scalars()] + [whole()] * 16,
+        [pltpu.VMEM((2, 24, channels), jnp.float32)],
+    )
+    parts = lax.all_to_all(parts.reshape(count, 1, 128), both, 0, 0).reshape(count, 128)
+    steps = 4
+    last_inner, last_outer, line, poor = pl.pallas_call(
+        lambda *refs: finish_kernel(entries, *refs),
+        grid=(steps,),
+        out_shape=[
+            jax.ShapeDtypeStruct(shape, jnp.float32)
+            for shape in ((2, rows), (2, points, channels), (1, 128), (1, 128))
+        ],
+        in_specs=[whole()] * 9,
+        out_specs=[
+            pl.BlockSpec((2, rows), lambda step: (0, 0)),
+            pl.BlockSpec((2, points // steps, channels), lambda step: (0, step, 0)),
+            pl.BlockSpec((1, 128), lambda step: (0, 0)),
+            pl.BlockSpec((1, 128), lambda step: (0, 0)),
+        ],
+        compiler_params=pltpu.CompilerParams(vmem_limit_bytes=vmem_bytes),
+    )(parts, inner_state, p_inner, q_inner, outer_state, wide, second, p_head, q_head)
+    hessenberg = line[0, :12].reshape(2, 3, 2)
 
     def again(state):
-        return (jnp.zeros((), jnp.bool_),) + step_by_step(*inputs)
+        return (jnp.zeros((), jnp.float32),) + step_by_step(*inputs)
 
     return lax.while_loop(
-        lambda state: state[0], again, (poor, last_inner, last_outer, hessenberg)
+        lambda state: state[0] > 0.0, again, (poor[0, 0], last_inner, last_outer, hessenberg)
     )[1:]
 
 

time: 183 us -> 107 us (0.58)
  matrix products: 36.1 us -> 0 us
  blocking collectives: 0 us -> 25.3 us
  other arithmetic: 26.8 us -> 1.84 us
  local copies, waits for them, and re-layouts: 31.1 us -> 6.92 us
  Pallas kernels: 0 us -> 24.1 us
  between operations: 22.6 us -> 7.53 us
  waiting for transfers between devices: 26.8 us -> 12 us
  starting transfers between devices: 37.6 us -> 28.2 us
    dot_general x14 -> x0, matrix products: 36.1 us -> none  [the longest x4 15.1 us: outer_apply(): jnp.einsum('prc,cd->prd', slope_rows, laser_mix, precision=highest)]
    all_to_all x0 -> x2, blocking collectives: none -> 25.3 us  [the longest x1 15.1 us: body(): lax.all_to_all(parts.reshape(count, 1, 128), both, 0, 0).reshape(count, 128)]
    pallas_call x0 -> x8, Pallas kernels: none -> 24.1 us  [the longest x7 21.5 us: run(): pl.pallas_call(kernel, out_shape=[jax.ShapeDtypeStruct(shape, jnp.float32...]
    all_to_all x5 -> x1, starting transfers between devices: 26.1 us -> 3.53 us  [exchanged(): got = lax.all_to_all(chunk, 'chan', 0, 0)]
    all_to_all x5 -> x1, waiting for transfers between devices: 26.8 us -> 7.68 us  [exchanged(): got = lax.all_to_all(chunk, 'chan', 0, 0)]
    another operation x7 -> x19, local copies, waits for them, and re-layouts: 17.5 us -> 0.27 us  [the longest x18 0.19 us: across_blocks(): jnp.stack([part[12 + 8 * k:20 + 8 * k] for part in got for k in range(2)])]
    ppermute x0 -> x8, starting transfers between devices: none -> 13.1 us  [the longest x6 8.51 us: across_blocks(): lax.ppermute(mine, 'rad', [(i, (i + 2 * step) % blocks) for i in range(bl...]
    reduce_sum x9 -> x2, other arithmetic: 7.38 us -> 0.04 us  [exchanged(): jnp.sum(got[:, 0:8], axis=0)]
  transfers between devices with their start and end apart: 7 -> 11, of which waited for: 5 -> 6; matrix products, arithmetic and copies ran while one was open for 8% -> 2% of each run, Pallas kernels for 0% -> 15%
where the time goes in v2:
time: 107 us
  starting transfers between devices  28.2 us (26%)
  blocking collectives  25.3 us (24%)
  Pallas kernels  24.1 us (23%)
  waiting for transfers between devices  12 us (11%)
  between operations  7.53 us (7%)
  local copies, waits for them, and re-layouts  6.92 us (6%)
  other arithmetic  1.84 us (2%)
    pallas_call x7, Pallas kernels, run(): pl.pallas_call(kernel, out_shape=[jax.ShapeDtypeStruct(shape, jnp.float32...  21.5 us
    all_to_all x1, blocking collectives, body(): lax.all_to_all(parts.reshape(count, 1, 128), both, 0, 0).reshape(count, 128)  15.1 us
    all_to_all x1, blocking collectives, exchanged(): got = lax.all_to_all(chunk, 'chan', 0, 0)  10.2 us
    ppermute x6, starting transfers between devices, across_blocks(): lax.ppermute(mine, 'rad', [(i, (i + 2 * step) % blocks) for i in range(bl...  8.51 us
    all_to_all x1, waiting for transfers between devices, exchanged(): got = lax.all_to_all(chunk, 'chan', 0, 0)  7.68 us
    ppermute x1, starting transfers between devices, neighbours(): high = lax.ppermute(block[:, :width], both, backward)  7.39 us
    ppermute x2, starting transfers between devices, across_blocks(): other = lax.ppermute(mine, 'rad', [(i, i ^ 1) for i in range(blocks)])  4.61 us
    ppermute x6, waiting for transfers between devices, across_blocks(): lax.ppermute(mine, 'rad', [(i, (i + 2 * step) % blocks) for i in range(bl...  4.31 us
  transfers between devices with their start and end apart: 11, of which 6 were waited for; matrix products, arithmetic and copies ran while one was open for 2% of the time, Pallas kernels for 15%

profile of v2, /device:TPU:1, one launch (start us, length us, event | category | flops | bytes accessed | tf_op | source)
XLA Modules:
  0.0 106.8 jit_solution(16087187032731629356)
XLA Ops:
  0.7 0.9 pad_maximum_fusion.13
  1.6 4.2 %collective-permute-start.8 = (f32[3,4,512]{2,1,0:T(4,128)S(1)}, f32[3,4,512]{2,1,0:T(4,128)S(1)}, u32[]{:S(2)}, u32[]{:S(2)}) collective-permute-start(f32[3,4,512]{2,1,0:T(4,128)S(1)} %get-tuple-element.317), channel_id=1, source_target_pairs={{0,1},{1,2},{2,3},{3,4},{4,5},{5,6},{6,7},{7,8},{8,9},{9,10},{10,1... | collective-permute-start | bytes 73736 | tf_op jit(solution)/shard_map/ppermute | solution.py:46
  5.8 7.4 %collective-permute-start.9 = (f32[3,4,512]{2,1,0:T(4,128)S(1)}, f32[3,4,512]{2,1,0:T(4,128)S(1)}, u32[]{:S(2)}, u32[]{:S(2)}) collective-permute-start(f32[3,4,512]{2,1,0:T(4,128)S(1)} %get-tuple-element.316), channel_id=1, source_target_pairs={{1,0},{2,1},{3,2},{4,3},{5,4},{6,5},{7,6},{8,7},{9,8},{10,9},{11,1... | collective-permute-start | bytes 73736 | tf_op jit(solution)/shard_map/ppermute | solution.py:47
  13.2 0.8 slice.476.head_ref.state_ref
  14.0 0.2 constant_dynamic-slice_fusion.13
  14.1 0.1 pad_add_fusion.place_ref
  14.2 1.6 %shard_map.121 = f32[16,16,256]{2,1,0:T(8,128)} custom-call(s32[4]{0:T(128)S(1)} %pad_add_fusion.place_ref, f32[2,256]{1,0:T(2,128)S(1)} %copy-done.27, f32[2,8,512]{2,1,0:T(8,128)S(1)} %slice.476.head_ref.state_ref, f32[1,2,256,512]{3,2,1,0:T(8,128)S(1)} %copy-done.25, s32[1,512]{1,0:T(1,128)S(1)} %bitcast.164), custom_call_target="tpu_custom_call" | custom-call | tf_op jit(solution)/shard_map/pallas_call | solution.py:184
  15.8 3.5 %all-to-all-start.4 = ((f32[16,16,256]{2,1,0:T(8,128)}), f32[16,16,256]{2,1,0:T(8,128)S(1)}, u32[]{:S(2)}, u32[]{:S(2)}) async-start(f32[16,16,256]{2,1,0:T(8,128)} %shard_map.121), calls=%async_computation.4 | async-start | bytes 524288 | tf_op jit(solution)/shard_map/all_to_all | solution.py:574
  19.3 0.6 fusion.117
  19.9 7.7 %all-to-all-done.4.got_ref = f32[16,16,256]{2,1,0:T(8,128)S(1)} async-done(((f32[16,16,256]{2,1,0:T(8,128)}), f32[16,16,256]{2,1,0:T(8,128)S(1)}, u32[]{:S(2)}, u32[]{:S(2)}) %all-to-all-start.4) | async-done | bytes 262176 | tf_op jit(solution)/shard_map/all_to_all | solution.py:574
  27.7 1.4 %collective-permute-start.4 = (f32[20,256]{1,0:T(8,128)S(1)}, f32[20,256]{1,0:T(8,128)S(1)}, u32[]{:S(2)}, u32[]{:S(2)}) collective-permute-start(f32[20,256]{1,0:T(8,128)S(1)} %pad_maximum_fusion.15), channel_id=1, source_target_pairs={{0,16},{16,0},{32,48},{48,32},{64,80},{80,64},{96,112},{112,96},{1... | collective-permute-start | bytes 61448 | tf_op jit(solution)/shard_map/ppermute | solution.py:531
  29.1 0.6 fusion.118
  36.1 5.9 %shard_map.123.wide_ref.refs_5_ = f32[2,400,512]{2,1,0:T(8,128)S(1)} custom-call(s32[4]{0:T(128)S(1)} %pad_add_fusion.place_ref, f32[2,384,512]{2,1,0:T(8,128)} %refs_4_.1, f32[3,4,512]{2,1,0:T(4,128)S(1)} %collective-permute-done.8.low_ref, f32[3,4,512]{2,1,0:T(4,128)S(1)} %collective-permute-done.9.high_ref, f32[384,512]{1,0:T(8,128)S(1)} %copy-done.21, ...), custom_call_target="tpu_custom_call" | custom-call | tf_op jit(solution)/shard_map/pallas_call | solution.py:184
  42.1 0.8 shard_map.122.block_ref
  42.9 0.0 collective-permute-done.4
  42.9 1.3 %collective-permute-start.5 = (f32[28,256]{1,0:T(8,128)S(1)}, f32[28,256]{1,0:T(8,128)S(1)}, u32[]{:S(2)}, u32[]{:S(2)}) collective-permute-start(f32[28,256]{1,0:T(8,128)S(1)} %pad_maximum_fusion.11), channel_id=1, source_target_pairs={{0,32},{16,48},{32,64},{48,80},{64,96},{80,112},{96,0},{112,16},{1... | collective-permute-start | bytes 86024 | tf_op jit(solution)/shard_map/ppermute | solution.py:537
  44.2 2.5 %collective-permute-start.6 = (f32[28,256]{1,0:T(8,128)S(1)}, f32[28,256]{1,0:T(8,128)S(1)}, u32[]{:S(2)}, u32[]{:S(2)}) collective-permute-start(f32[28,256]{1,0:T(8,128)S(1)} %pad_maximum_fusion.11), channel_id=1, source_target_pairs={{0,64},{16,80},{32,96},{48,112},{64,0},{80,16},{96,32},{112,48},{1... | collective-permute-start | bytes 86024 | tf_op jit(solution)/shard_map/ppermute | solution.py:537
  46.7 1.2 %collective-permute-start.7 = (f32[28,256]{1,0:T(8,128)S(1)}, f32[28,256]{1,0:T(8,128)S(1)}, u32[]{:S(2)}, u32[]{:S(2)}) collective-permute-start(f32[28,256]{1,0:T(8,128)S(1)} %pad_maximum_fusion.11), channel_id=1, source_target_pairs={{0,96},{16,112},{32,0},{48,16},{64,32},{80,48},{96,64},{112,80},{1... | collective-permute-start | bytes 86024 | tf_op jit(solution)/shard_map/ppermute | solution.py:537
  47.9 0.9 collective-permute-done.6
  48.9 0.7 collective-permute-done.7
  49.7 0.1 constant_dynamic-slice_fusion.12.window_a
  49.7 0.1 constant_dynamic-slice_fusion.10.window_b
  49.8 2.4 %shard_map.124 = (f32[2,256]{1,0:T(2,128)S(1)}, f32[16,16,256]{2,1,0:T(8,128)S(1)}, f32[2,8,512]{2,1,0:T(8,128)S(1)}) custom-call(s32[4]{0:T(128)S(1)} %pad_add_fusion.place_ref, f32[2,256]{1,0:T(2,128)S(1)} %shard_map.122.block_ref, f32[2,256]{1,0:T(2,128)S(1)} %copy-done.27, f32[2,512]{1,0:T(2,128)S(1)} %constant_dynamic-slice_fusion.12.window_a, ...), custom_call_target="tpu_custom_call" | custom-call | tf_op jit(solution)/shard_map/pallas_call | solution.py:184
  52.2 10.2 %all_to_all.32.got_ref = f32[16,16,256]{2,1,0:T(8,128)S(1)} all-to-all(f32[16,16,256]{2,1,0:T(8,128)S(1)} %get-tuple-element.145), channel_id=1, replica_groups=mesh['rad'=8,'chan'=16] {'chan'}, dimensions={0} | all-to-all | bytes 524288 | tf_op jit(solution)/shard_map/all_to_all | solution.py:574
  62.6 0.5 copy-done.31
  63.1 0.0 copy-done.37
  63.1 0.0 copy-done.30
  63.1 3.2 %collective-permute-start.10 = (f32[20,256]{1,0:T(8,128)S(1)}, f32[20,256]{1,0:T(8,128)S(1)}, u32[]{:S(2)}, u32[]{:S(2)}) collective-permute-start(f32[20,256]{1,0:T(8,128)S(1)} %pad_maximum_fusion.16), channel_id=1, source_target_pairs={{0,16},{16,0},{32,48},{48,32},{64,80},{80,64},{96,112},{112,96},{1... | collective-permute-start | bytes 61448 | tf_op jit(solution)/shard_map/ppermute | solution.py:531
  66.3 7.1 %shard_map.126 = (f32[2,384,512]{2,1,0:T(8,128)S(1)}, f32[9,8,128]{2,1,0:T(8,128)S(1)}) custom-call(f32[2,400,512]{2,1,0:T(8,128)S(1)} %shard_map.123.wide_ref.refs_5_, f32[2,384,512]{2,1,0:T(8,128)} %refs_4_.1, f32[384,512]{1,0:T(8,128)} %pot_ref.5, f32[512,512]{1,0:T(8,128)} %mix_ref.7), custom_call_target="tpu_custom_call" | custom-call | tf_op jit(solution)/shard_map/pallas_call | solution.py:184
  73.5 0.8 shard_map.125.block_ref
  74.3 0.0 collective-permute-done.10
  74.3 0.6 copy-done.38
  74.9 0.7 slice_add_fusion.3
  75.7 0.1 collective-permute-start.11
  75.8 3.5 %collective-permute-start.12 = (f32[28,256]{1,0:T(8,128)S(1)}, f32[28,256]{1,0:T(8,128)S(1)}, u32[]{:S(2)}, u32[]{:S(2)}) collective-permute-start(f32[28,256]{1,0:T(8,128)S(1)} %pad_maximum_fusion.12), channel_id=1, source_target_pairs={{0,64},{16,80},{32,96},{48,112},{64,0},{80,16},{96,32},{112,48},{1... | collective-permute-start | bytes 86024 | tf_op jit(solution)/shard_map/ppermute | solution.py:537
  79.3 0.4 collective-permute-done.11
  79.7 1.3 %collective-permute-done.12 = f32[28,256]{1,0:T(8,128)S(1)} collective-permute-done((f32[28,256]{1,0:T(8,128)S(1)}, f32[28,256]{1,0:T(8,128)S(1)}, u32[]{:S(2)}, u32[]{:S(2)}) %collective-permute-start.12) | collective-permute-done | bytes 28704 | tf_op jit(solution)/shard_map/ppermute | solution.py:537
  81.1 0.9 collective-permute-done.13
  82.2 0.1 constant_dynamic-slice_fusion.8.window_a
  82.3 0.1 constant_dynamic-slice_fusion.6.window_b
  82.3 0.8 copy-done.1
  83.1 3.0 %shard_map.127 = (f32[2,256]{1,0:T(2,128)S(1)}, f32[2,8,512]{2,1,0:T(8,128)S(1)}, f32[128,128]{1,0:T(8,128)S(1)}) custom-call(s32[4]{0:T(128)S(1)} %pad_add_fusion.place_ref, f32[2,256]{1,0:T(2,128)S(1)} %shard_map.125.block_ref, f32[2,256]{1,0:T(2,128)S(1)} %get-tuple-element.146.inner_ref.refs_2_, f32[2,512]{1,0:T(2,128)S(1)} %constant_dynamic-slice_fusion.8.window_a, ...), custom_call_target="tpu_custom_call" | custom-call | tf_op jit(solution)/shard_map/pallas_call | solution.py:184
  86.1 15.1 %all_to_all.33 = f32[128,1,128]{2,1,0:T(1,128)S(1)} all-to-all(f32[128,1,128]{2,1,0:T(1,128)S(1)} %bitcast.155), channel_id=1, replica_groups=mesh['rad'=8,'chan'=16] {'rad','chan'}, dimensions={0} | all-to-all | bytes 131072 | tf_op jit(solution)/shard_map/all_to_all | solution.py:627
  101.2 2.6 %shard_map.128 = (f32[2,256]{1,0:T(2,128)}, f32[2,384,512]{2,1,0:T(8,128)}, f32[1,128]{1,0:T(1,128)S(1)}, f32[1,128]{1,0:T(1,128)}) custom-call(f32[128,128]{1,0:T(8,128)S(1)} %bitcast.154, f32[2,256]{1,0:T(2,128)S(1)} %copy-done.27, f32[2,256]{1,0:T(2,128)S(1)} %get-tuple-element.146.inner_ref.refs_2_, f32[2,256]{1,0:T(2,128)S(1)} %get-tuple-element.151.refs_3_, ...), custom_call_target="tpu_custom_call" | custom-call | tf_op jit(solution)/shard_map/pallas_call | solution.py:629
  103.8 0.1 reshape_squeeze.3
  103.9 0.7 copy.27
  104.6 0.9 while.18
  105.5 1.3 %copy.28 = f32[2,3,2]{1,2,0:T(2,128)} copy(f32[2,3,2]{0,2,1:T(2,128)} %get-tuple-element.227) | data formatting | bytes 96
  (100 shorter events, 0.7 us)
Async XLA Ops:
  0.6 13.3 %copy-start.33 = (s32[8,2]{0,1:T(2,128)S(1)}, s32[8,2]{0,1:T(2,128)}, u32[]{:S(2)}) copy-start(s32[8,2]{0,1:T(2,128)} %param.30) | copy-start | bytes 196
  0.6 13.3 %copy-start.35 = (s32[8,2]{0,1:T(2,128)S(1)}, s32[8,2]{0,1:T(2,128)}, u32[]{:S(2)}) copy-start(s32[8,2]{0,1:T(2,128)} %param.29) | copy-start | bytes 196
  0.7 13.6 %copy-start.27 = (f32[2,256]{1,0:T(2,128)S(1)}, f32[2,256]{1,0:T(2,128)}, u32[]{:S(2)}) copy-start(f32[2,256]{1,0:T(2,128)} %refs_1_.1) | copy-start | bytes 6148
  0.7 13.6 %copy-start.25 = (f32[1,2,256,512]{3,2,1,0:T(8,128)S(1)}, f32[1,2,256,512]{3,2,1,0:T(8,128)}, u32[]{:S(2)}) copy-start(f32[1,2,256,512]{3,2,1,0:T(8,128)} %amp_ref.5) | copy-start | bytes 3145732
  0.7 13.6 %copy-start.28 = (s32[512]{0:T(512)S(1)}, s32[512]{0:T(512)}, u32[]{:S(2)}) copy-start(s32[512]{0:T(512)} %param.31) | copy-start | bytes 6148
  1.6 34.5 %copy-start.21 = (f32[384,512]{1,0:T(8,128)S(1)}, f32[384,512]{1,0:T(8,128)}, u32[]{:S(2)}) copy-start(f32[384,512]{1,0:T(8,128)} %pot_ref.5) | copy-start | bytes 2359300
  1.6 34.5 %collective-permute-start.8 = (f32[3,4,512]{2,1,0:T(4,128)S(1)}, f32[3,4,512]{2,1,0:T(4,128)S(1)}, u32[]{:S(2)}, u32[]{:S(2)}) collective-permute-start(f32[3,4,512]{2,1,0:T(4,128)S(1)} %get-tuple-element.317), channel_id=1, source_target_pairs={{0,1},{1,2},{2,3},{3,4},{4,5},{5,6},{6,7},{7,8},{8,9},{9,10},{10,1... | collective-permute-start | bytes 73736 | tf_op jit(solution)/shard_map/ppermute | solution.py:46
  5.8 30.3 %collective-permute-start.9 = (f32[3,4,512]{2,1,0:T(4,128)S(1)}, f32[3,4,512]{2,1,0:T(4,128)S(1)}, u32[]{:S(2)}, u32[]{:S(2)}) collective-permute-start(f32[3,4,512]{2,1,0:T(4,128)S(1)} %get-tuple-element.316), channel_id=1, source_target_pairs={{1,0},{2,1},{3,2},{4,3},{5,4},{6,5},{7,6},{8,7},{9,8},{10,9},{11,1... | collective-permute-start | bytes 73736 | tf_op jit(solution)/shard_map/ppermute | solution.py:47
  15.8 11.8 %all-to-all-start.4 = ((f32[16,16,256]{2,1,0:T(8,128)}), f32[16,16,256]{2,1,0:T(8,128)S(1)}, u32[]{:S(2)}, u32[]{:S(2)}) async-start(f32[16,16,256]{2,1,0:T(8,128)} %shard_map.121), calls=%async_computation.4 | async-start | bytes 524288 | tf_op jit(solution)/shard_map/all_to_all | solution.py:574
  27.7 15.1 %collective-permute-start.4 = (f32[20,256]{1,0:T(8,128)S(1)}, f32[20,256]{1,0:T(8,128)S(1)}, u32[]{:S(2)}, u32[]{:S(2)}) collective-permute-start(f32[20,256]{1,0:T(8,128)S(1)} %pad_maximum_fusion.15), channel_id=1, source_target_pairs={{0,16},{16,0},{32,48},{48,32},{64,80},{80,64},{96,112},{112,96},{1... | collective-permute-start | bytes 61448 | tf_op jit(solution)/shard_map/ppermute | solution.py:531
  36.1 6.0 %copy-start.7 = (f32[1,4096,256]{2,1,0:T(8,128)S(1)}, f32[1,4096,256]{2,1,0:T(8,128)}, u32[]{:S(2)}) copy-start(f32[1,4096,256]{2,1,0:T(8,128)} %ham_ref.3) | copy-start | bytes 12582916
  42.1 7.8 %copy-start.24 = (f32[1,2,512,256]{3,2,1,0:T(8,128)S(1)}, f32[1,2,512,256]{3,2,1,0:T(8,128)}, u32[]{:S(2)}) copy-start(f32[1,2,512,256]{3,2,1,0:T(8,128)} %coupling_ref.3) | copy-start | bytes 3145732
  42.9 4.9 %collective-permute-start.5 = (f32[28,256]{1,0:T(8,128)S(1)}, f32[28,256]{1,0:T(8,128)S(1)}, u32[]{:S(2)}, u32[]{:S(2)}) collective-permute-start(f32[28,256]{1,0:T(8,128)S(1)} %pad_maximum_fusion.11), channel_id=1, source_target_pairs={{0,32},{16,48},{32,64},{48,80},{64,96},{80,112},{96,0},{112,16},{1... | collective-permute-start | bytes 86024 | tf_op jit(solution)/shard_map/ppermute | solution.py:537
  44.2 4.6 %collective-permute-start.6 = (f32[28,256]{1,0:T(8,128)S(1)}, f32[28,256]{1,0:T(8,128)S(1)}, u32[]{:S(2)}, u32[]{:S(2)}) collective-permute-start(f32[28,256]{1,0:T(8,128)S(1)} %pad_maximum_fusion.11), channel_id=1, source_target_pairs={{0,64},{16,80},{32,96},{48,112},{64,0},{80,16},{96,32},{112,48},{1... | collective-permute-start | bytes 86024 | tf_op jit(solution)/shard_map/ppermute | solution.py:537
  46.7 2.9 %collective-permute-start.7 = (f32[28,256]{1,0:T(8,128)S(1)}, f32[28,256]{1,0:T(8,128)S(1)}, u32[]{:S(2)}, u32[]{:S(2)}) collective-permute-start(f32[28,256]{1,0:T(8,128)S(1)} %pad_maximum_fusion.11), channel_id=1, source_target_pairs={{0,96},{16,112},{32,0},{48,16},{64,32},{80,48},{96,64},{112,80},{1... | collective-permute-start | bytes 86024 | tf_op jit(solution)/shard_map/ppermute | solution.py:537
  62.5 0.6 copy-start.31
  62.5 0.6 copy-start.37
  62.5 0.6 copy-start.30
  63.1 10.3 %copy-start.8 = (f32[1,4096,256]{2,1,0:T(8,128)S(1)}, f32[1,4096,256]{2,1,0:T(8,128)}, u32[]{:S(2)}) copy-start(f32[1,4096,256]{2,1,0:T(8,128)} %ham_ref.3) | copy-start | bytes 12582916
  63.1 11.1 %collective-permute-start.10 = (f32[20,256]{1,0:T(8,128)S(1)}, f32[20,256]{1,0:T(8,128)S(1)}, u32[]{:S(2)}, u32[]{:S(2)}) collective-permute-start(f32[20,256]{1,0:T(8,128)S(1)} %pad_maximum_fusion.16), channel_id=1, source_target_pairs={{0,16},{16,0},{32,48},{48,32},{64,80},{80,64},{96,112},{112,96},{1... | collective-permute-start | bytes 61448 | tf_op jit(solution)/shard_map/ppermute | solution.py:531
  73.5 0.8 copy-start
  73.5 0.8 copy-start.32
  74.3 0.6 copy-start.38
  75.7 4.0 %collective-permute-start.11 = (f32[28,256]{1,0:T(8,128)S(1)}, f32[28,256]{1,0:T(8,128)S(1)}, u32[]{:S(2)}, u32[]{:S(2)}) collective-permute-start(f32[28,256]{1,0:T(8,128)S(1)} %pad_maximum_fusion.12), channel_id=1, source_target_pairs={{0,32},{16,48},{32,64},{48,80},{64,96},{80,112},{96,0},{112,16},{1... | collective-permute-start | bytes 86024 | tf_op jit(solution)/shard_map/ppermute | solution.py:537
  75.8 5.2 %collective-permute-start.12 = (f32[28,256]{1,0:T(8,128)S(1)}, f32[28,256]{1,0:T(8,128)S(1)}, u32[]{:S(2)}, u32[]{:S(2)}) collective-permute-start(f32[28,256]{1,0:T(8,128)S(1)} %pad_maximum_fusion.12), channel_id=1, source_target_pairs={{0,64},{16,80},{32,96},{48,112},{64,0},{80,16},{96,32},{112,48},{1... | collective-permute-start | bytes 86024 | tf_op jit(solution)/shard_map/ppermute | solution.py:537
  79.3 2.8 %collective-permute-start.13 = (f32[28,256]{1,0:T(8,128)S(1)}, f32[28,256]{1,0:T(8,128)S(1)}, u32[]{:S(2)}, u32[]{:S(2)}) collective-permute-start(f32[28,256]{1,0:T(8,128)S(1)} %pad_maximum_fusion.12), channel_id=1, source_target_pairs={{0,96},{16,112},{32,0},{48,16},{64,32},{80,48},{96,64},{112,80},{1... | collective-permute-start | bytes 86024 | tf_op jit(solution)/shard_map/ppermute | solution.py:537
  82.3 0.8 copy-start.1
  83.1 18.0 %copy-start.9 = (f32[2,384,512]{2,1,0:T(8,128)S(1)}, f32[2,384,512]{2,1,0:T(8,128)}, u32[]{:S(2)}) copy-start(f32[2,384,512]{2,1,0:T(8,128)} %refs_4_.1) | copy-start | bytes 4718596
  101.1 3.4 %copy-start.29 = (s32[512]{0:T(512)S(1)}, s32[512]{0:T(512)}, u32[]{:S(2)}) copy-start(s32[512]{0:T(512)} %param.31) | copy-start | bytes 6148
  101.1 3.4 %copy-start.34 = (s32[8,2]{0,1:T(2,128)S(1)}, s32[8,2]{0,1:T(2,128)}, u32[]{:S(2)}) copy-start(s32[8,2]{0,1:T(2,128)} %param.30) | copy-start | bytes 196
  101.1 3.4 %copy-start.36 = (s32[8,2]{0,1:T(2,128)S(1)}, s32[8,2]{0,1:T(2,128)}, u32[]{:S(2)}) copy-start(s32[8,2]{0,1:T(2,128)} %param.29) | copy-start | bytes 196

commit v3 on v1

v3 whole, which is shorter than its diff:
```python
import jax
import jax.numpy as jnp
from jax import lax
from jax.experimental import pallas as pl
from jax.experimental.pallas import tpu as pltpu
from jax.sharding import PartitionSpec as P

STRIP = 256
TERMS = 2

highest = lax.Precision.HIGHEST
kinetic_coef = -0.5 * 0.05 / (12.0 * 0.25 * 0.25)
slope_coef = 1.0 / (12.0 * 0.25)
bloch_coef = 2.0
shift = 1.5
least_left = 0.02
both = ("rad", "chan")


def spread(block, axis, holder):
    block = jnp.where(lax.axis_index(axis) == holder, block, jnp.zeros_like(block))
    return lax.psum(block, axis)


def local_parts(left, right):
    real_part = jnp.sum(left[0] * right[0]) + jnp.sum(left[1] * right[1])
    imag_part = jnp.sum(left[0][0] * right[0][1] - left[0][1] * right[0][0]) + jnp.sum(
        left[1][0] * right[1][1] - left[1][1] * right[1][0]
    )
    return jnp.stack([real_part, imag_part])


def rotate(vector, real_coef, imag_coef):
    return jnp.stack(
        [
            real_coef * vector[0] - imag_coef * vector[1],
            real_coef * vector[1] + imag_coef * vector[0],
        ]
    )


def neighbours(last_rows, first_rows):
    count = lax.axis_size(both)
    forward = [(i, i + 1) for i in range(count - 1)]
    backward = [(target, source) for source, target in forward]
    return lax.ppermute(last_rows, both, forward), lax.ppermute(first_rows, both, backward)


def outer_apply(extended, potential, laser_mix, moved):
    points = extended.shape[1] - 4
    far_left = extended[:, 0:points]
    near_left = extended[:, 1 : points + 1]
    centre_row = extended[:, 2 : points + 2]
    near_right = extended[:, 3 : points + 3]
    far_right = extended[:, 4 : points + 4]
    laplace = -far_left + 16.0 * near_left - 30.0 * centre_row + 16.0 * near_right - far_right
    slope_rows = slope_coef * (far_left - 8.0 * near_left + 8.0 * near_right - far_right)
    mixed_slope = jnp.einsum("prc,cd->prd", slope_rows, laser_mix, precision=highest)
    return (
        kinetic_coef * laplace
        + (potential - moved) * centre_row
        + jnp.stack([mixed_slope[1], -mixed_slope[0]])
    )


def inner_windows(shards, own_partners, own_offsets):
    windows = []
    for couple_index in range(own_partners.shape[0]):
        source = lax.dynamic_index_in_dim(shards, own_partners[couple_index], 0, keepdims=False)
        source = source.transpose(1, 0, 2).reshape(2, -1)
        band_width = source.shape[1] // 2
        windows.append(
            lax.dynamic_slice_in_dim(source, own_offsets[couple_index] + band_width, band_width, 1)
        )
    return windows


def exchange(inner_vec, ghost_part, row):
    rows = inner_vec.shape[1]
    blocks, strips = lax.axis_size("rad"), lax.axis_size("chan")
    chunk = jnp.concatenate(
        [
            inner_vec,
            ghost_part.reshape(-1, rows),
            row.reshape(-1, rows),
            jnp.zeros((2, rows), jnp.float32),
        ],
        axis=0,
    )
    got = lax.all_to_all(jnp.broadcast_to(chunk, (strips,) + chunk.shape), "chan", 0, 0)
    own = got[:, 0:2]
    ghost_sum = jnp.sum(got[:, 2:10], axis=0)
    padded = jnp.pad(own, ((2, 1), (0, 0), (0, 0)))
    near = lax.dynamic_slice_in_dim(padded, lax.axis_index("chan"), 4, 0)
    chunk = jnp.concatenate(
        [near.reshape(8, rows), ghost_sum, got[0, 10:14], jnp.zeros((4, rows), jnp.float32)],
        axis=0,
    )
    got_blocks = lax.all_to_all(jnp.broadcast_to(chunk, (blocks,) + chunk.shape), "rad", 0, 0)
    shards = got_blocks[:, 0:8].reshape(blocks, 4, 2, rows)
    ghost = jnp.sum(got_blocks[:, 8:16], axis=0).reshape(2, 2, -1)
    first_row = got_blocks[0, 16:20].reshape(2, -1)
    return own.transpose(1, 0, 2).reshape(2, -1), shards, ghost, first_row


def step_by_step(
    inner_state,
    outer_state,
    inner_ham,
    inner_coupling,
    surface_amp,
    potential,
    laser_mix,
    partners,
    band_offsets,
    channel_group,
):
    block_order = inner_ham.shape[1]
    points, channels = outer_state.shape[1:]
    entries = float(
        lax.axis_size("rad") * block_order + lax.axis_size(both) * points * channels
    )
    block_index = lax.axis_index("rad")
    is_first = lax.axis_index(both) == 0
    member = (channel_group == block_index).astype(jnp.float32)
    masked_amp = surface_amp[0] * member[None, None, :]
    own_partners = lax.dynamic_index_in_dim(partners, block_index, 0, keepdims=False)
    own_offsets = lax.dynamic_index_in_dim(band_offsets, block_index, 0, keepdims=False)

    def total(value):
        return lax.psum(value, both) / entries

    def squares(vector):
        return jnp.sum(vector[0] * vector[0]) + jnp.sum(vector[1] * vector[1])

    start_len = jnp.sqrt(total(squares((inner_state, outer_state))))
    krylov = [(inner_state / start_len, outer_state / start_len)]
    hessenberg = jnp.zeros((2, TERMS + 1, TERMS), jnp.float32)
    for term_index in range(TERMS):
        inner_vec, outer_vec = krylov[term_index]
        ghost_part = jnp.einsum("pk,mki->pmi", inner_vec, masked_amp, precision=highest)
        row = jnp.where(is_first, outer_vec[:, 0], 0.0)
        own_vec, shards, ghost, first_row = exchange(inner_vec, ghost_part, row)
        result_in = jnp.dot(own_vec, inner_ham[0], precision=highest)
        for couple_index, window in enumerate(inner_windows(shards, own_partners, own_offsets)):
            result_in = result_in + jnp.dot(window, inner_coupling[0, couple_index], precision=highest)
        result_in = result_in + bloch_coef * jnp.einsum(
            "pi,ki->pk", first_row, masked_amp[0], precision=highest
        )
        low, high = neighbours(outer_vec[:, points - 2 :], outer_vec[:, :2])
        low = jnp.where(is_first, ghost[:, ::-1], low)
        extended = jnp.concatenate([low, outer_vec, high], axis=1)
        image = (result_in, outer_apply(extended, potential, laser_mix, 0.0))
        for prior_index in range(term_index + 1):
            prior = krylov[prior_index]
            coefs = total(local_parts(prior, image))
            image = tuple(
                part - rotate(prior_part, coefs[0], coefs[1])
                for part, prior_part in zip(image, prior)
            )
            hessenberg = hessenberg.at[:, prior_index, term_index].set(coefs)
        new_length = jnp.sqrt(total(squares(image)))
        hessenberg = hessenberg.at[0, term_index + 1, term_index].set(new_length)
        krylov.append((image[0] / new_length, image[1] / new_length))
    return (krylov[-1][0], krylov[-1][1], hessenberg)


lanes = 128
margin = 8
reach = 2
vmem_bytes = 16 * 2**20


def whole():
    return pl.BlockSpec(memory_space=pltpu.VMEM)


def anywhere():
    return pl.BlockSpec(memory_space=pl.ANY)


def far():
    return pl.BlockSpec(memory_space=pltpu.HBM)


def in_one(shape):
    return pl.BlockSpec(shape, lambda i: (0,) * len(shape))


def scalars():
    return pl.BlockSpec(memory_space=pltpu.SMEM)


def run(kernel, outs, args, in_specs, scratch=()):
    return pl.pallas_call(
        kernel,
        out_shape=[jax.ShapeDtypeStruct(*out) if isinstance(out[0], tuple) else jax.ShapeDtypeStruct(out, jnp.float32) for out in outs],
        in_specs=in_specs,
        out_specs=[whole()] * len(outs),
        scratch_shapes=list(scratch),
        compiler_params=pltpu.CompilerParams(vmem_limit_bytes=vmem_bytes),
    )(*args)


def two(x):
    high = x.astype(jnp.bfloat16)
    return high, (x - high.astype(jnp.float32)).astype(jnp.bfloat16)


def both_halves(x):
    high, low = two(x)
    rest = jnp.zeros((16 - 2 * x.shape[0], x.shape[1]), jnp.float32)
    return jnp.concatenate([high.astype(jnp.float32), low.astype(jnp.float32), rest], axis=0).astype(jnp.bfloat16)


def few_rows_dot(x, weights, flipped=False):
    rows = x.shape[0]
    lhs = both_halves(x)
    dims = (((1,), (1 if flipped else 0,)), ((), ()))
    total = sum(lax.dot_general(lhs, part, dims, preferred_element_type=jnp.float32) for part in weights)
    return total[:rows] + total[rows : 2 * rows]


def mixed_with(high, low, mix_ref):
    lhs = jnp.concatenate([high, low, high], axis=1)
    return jnp.dot(lhs, mix_ref[...], preferred_element_type=jnp.float32)


def mix_parts(mix_ref):
    high, low = two(slope_coef * mix_ref[...])
    return jnp.concatenate([high, high, low], axis=0)


def write_chunk(out_ref, held_ref, written, inner_vec, ghosts, row):
    half = inner_vec.shape[1]
    held_ref[...] = jnp.concatenate(
        [
            ghosts[:, :half],
            ghosts[:, half:],
            inner_vec,
            row[:, :half],
            row[:, half:],
            jnp.zeros((2, half), jnp.float32),
        ],
        axis=0,
    )
    copies = [
        pltpu.make_async_copy(held_ref, out_ref.at[strip], written.at[strip]) for strip in range(out_ref.shape[0])
    ]
    for copy in copies:
        copy.start()
    for copy in copies:
        copy.wait()


def ghost_rows(inner_vec, amps, member):
    return jnp.concatenate([few_rows_dot(inner_vec, amp) * member for amp in amps], axis=0)


def member_of(group_ref, flags_ref):
    return jnp.where(group_ref[...] == flags_ref[0], 1.0, 0.0)


def start_kernel(
    flags_ref, inner_ref, head_ref, amp_ref, group_ref, chunk_ref, held_ref, written
):
    row = jnp.concatenate([head_ref[part, 0:1] for part in range(2)], axis=0)
    row = jnp.where(flags_ref[2] == 1, row, 0.0)
    inner_vec = inner_ref[...]
    amps = [two(amp_ref[0, radius]) for radius in range(2)]
    ghosts = ghost_rows(inner_vec, amps, member_of(group_ref, flags_ref))
    write_chunk(chunk_ref, held_ref, written, inner_vec, ghosts, row)


def stencils(window, pot):
    before_2, before_1, here, after_1, after_2 = window
    local = (pot - (30.0 * kinetic_coef + shift)) * here + (
        16.0 * kinetic_coef * (before_1 + after_1) - kinetic_coef * (before_2 + after_2)
    )
    return local, (before_2 - after_2) + 8.0 * (after_1 - before_1)


def first_outer_kernel(
    state_ref, pot_ref, mix_ref, out_ref, mix_out, first_out, last_out, wide_ref, pot_wide, slope_h, slope_l, ends_ref, written
):
    points, channels = state_ref.shape[1:]
    strips = channels // lanes
    length = points // 8
    for strip in range(strips):
        here = slice(strip * lanes, (strip + 1) * lanes)
        for part in range(3):
            source = pot_ref if part == 2 else state_ref.at[part]
            target = pot_wide.at[strip] if part == 2 else wide_ref.at[part, strip]
            target[margin : margin + points] = source[:, here]
            target[0:margin] = jnp.zeros((margin, lanes), jnp.float32)
            target[margin + points :] = jnp.zeros((margin, lanes), jnp.float32)
    for part in range(3):
        source = pot_ref if part == 2 else state_ref.at[part]
        ends_ref[0, part], ends_ref[1, part] = source[0:4], source[points - 4 : points]
    copies = [
        pltpu.make_async_copy(ends_ref.at[end], out, written.at[end]) for end, out in enumerate((first_out, last_out))
    ]
    for copy in copies:
        copy.start()

    def strip_step(step, _):
        part, strip = lax.div(step, strips), lax.rem(step, strips)

        def load(place):
            return wide_ref[part, strip, pl.ds(margin + place, 8, stride=length)]

        window = [load(place) for place in range(-2 * reach, 0)]
        columns = pl.ds(pl.multiple_of(strip * lanes, lanes), lanes)
        for first in range(-reach, length + reach, 2):
            slopes = []
            for place in (first, first + 1):
                window.append(load(place + reach))
                local, slope = stencils(window, pot_wide[strip, pl.ds(margin + place, 8, stride=length)])
                out_ref[part, strip, (place + reach) * 8 : (place + reach + 1) * 8] = local
                slopes.append(slope)
                window.pop(0)
            rows = slice((first + reach) * 8, (first + reach + 2) * 8)
            slope_h[part, rows, columns], slope_l[part, rows, columns] = two(jnp.concatenate(slopes, axis=0))
        return 0

    lax.fori_loop(0, 2 * strips, strip_step, 0)
    mix_out[...] = mix_parts(mix_ref)
    add_mixed(out_ref, slope_h, slope_l, mix_out)
    for copy in copies:
        copy.wait()


def add_mixed(out_ref, slope_h, slope_l, mix_ref):
    for part in range(2):
        mixed = mixed_with(slope_h[1 - part], slope_l[1 - part], mix_ref)
        for strip in range(out_ref.shape[1]):
            own = mixed[:, strip * lanes : (strip + 1) * lanes]
            out_ref[part, strip] = out_ref[part, strip] + (own if part == 0 else -own)


def products(s, p, q):
    return [
        s[0] * s[0] + s[1] * s[1],
        s[0] * p[0] + s[1] * p[1],
        s[0] * p[1] - s[1] * p[0],
        s[0] * q[0] + s[1] * q[1],
        s[0] * q[1] - s[1] * q[0],
        p[0] * p[0] + p[1] * p[1],
        p[0] * q[0] + p[1] * q[1],
        p[0] * q[1] - p[1] * q[0],
        q[0] * q[0] + q[1] * q[1],
    ]


def mend_edges(flags_ref, extra_ref, low_ref, high_ref, state_in, pot_in, mix_ref, wide_ref, edge_ref):
    points, channels = pot_in.shape
    strips, places = wide_ref.shape[1:3]
    local, slopes = [], []
    for part in range(2):
        for end in range(2):
            edge = edge_ref.at[part, end]
            edge[...] = jnp.zeros_like(edge)
            edge[4:8] = low_ref[part] if end == 0 else state_in[part, points - 4 : points]
            edge[8:12] = state_in[part, 0:4] if end == 0 else high_ref[part]
            if end == 0:
                pot = jnp.concatenate([low_ref[2], pot_in[0:4]], axis=0)
            else:
                pot = jnp.concatenate([pot_in[points - 4 : points], high_ref[2]], axis=0)
            inner, slope = stencils([edge[4 + k : 12 + k] for k in range(-reach, reach + 1)], pot)
            local.append(inner)
            slopes.append(slope)
    mixed = mixed_with(*two(jnp.concatenate(slopes, axis=0)), mix_ref)
    row = lax.broadcasted_iota(jnp.int32, (8, channels), 0)
    outside = [(row < 4) & (flags_ref[2] == 1), (row >= 4) & (flags_ref[3] == 1)]
    for part in range(2):
        for end in range(2):
            other = mixed[16 * (1 - part) + 8 * end : 16 * (1 - part) + 8 * end + 8]
            p = local[2 * part + end] + (other if part == 0 else -other)
            p = jnp.where(outside[end], 0.0, p)
            if end == 0:
                p = p + extra_ref[part]
            for strip in range(strips):
                first = 0 if end == 0 else places - 8 * 4 + 7
                wide_ref[part, strip, pl.ds(first, 4, stride=8)] = p[2:6, strip * lanes : (strip + 1) * lanes]


def second_outer_kernel(
    flags_ref, extra_ref, low_ref, high_ref, wide_in, state_in, pot_in, mix_ref,
    wide_ref, q_out, notes_out, slope_h, slope_l, state_ref, pot_ref, edge_ref, out_ref, notes_ref, written,
):
    mend_edges(flags_ref, extra_ref, low_ref, high_ref, state_in, pot_in, mix_ref, wide_ref, edge_ref)
    strips, places = out_ref.shape[1:3]
    length = places // 8
    for strip in range(strips):
        here = slice(strip * lanes, (strip + 1) * lanes)
        pot_ref[strip] = pot_in[:, here]
        for part in range(2):
            state_ref[part, strip] = state_in[part, :, here]

    def strip_step(step, _):
        part, strip = lax.div(step, strips), lax.rem(step, strips)

        def load(place):
            return wide_ref[part, strip, (place + reach) * 8 : (place + reach + 1) * 8]

        window = [load(place) for place in range(-reach, reach)]
        columns = pl.ds(pl.multiple_of(strip * lanes, lanes), lanes)
        for first in range(0, length, 2):
            slopes = []
            for place in (first, first + 1):
                window.append(load(place + reach))
                local, slope = stencils(window, pot_ref[strip, pl.ds(place, 8, stride=length)])
                out_ref[part, strip, place * 8 : (place + 1) * 8] = local
                slopes.append(slope)
                window.pop(0)
            rows = slice(first * 8, (first + 2) * 8)
            slope_h[part, rows, columns], slope_l[part, rows, columns] = two(jnp.concatenate(slopes, axis=0))
        return 0

    lax.fori_loop(0, 2 * strips, strip_step, 0)
    add_mixed(out_ref, slope_h, slope_l, mix_ref)
    copy = pltpu.make_async_copy(out_ref, q_out, written.at[0])
    copy.start()
    inside = lax.broadcasted_iota(jnp.int32, (8, lanes), 0) > 0

    def gram_step(strip, sums):
        for place in range(length):
            entries = products(
                [state_ref[part, strip, pl.ds(place, 8, stride=length)] for part in range(2)],
                [wide_ref[part, strip, (place + reach) * 8 : (place + reach + 1) * 8] for part in range(2)],
                [out_ref[part, strip, place * 8 : (place + 1) * 8] for part in range(2)],
            )
            if place < 4:
                entries = [jnp.where(inside, entry, 0.0) for entry in entries]
            sums = [total + entry for total, entry in zip(sums, entries)]
        return sums

    sums = lax.fori_loop(0, strips, gram_step, [jnp.zeros((8, lanes), jnp.float32)] * 9)
    for k in range(9):
        notes_ref[k] = sums[k]
    for strip in range(strips):
        here = slice(strip * lanes, (strip + 1) * lanes)
        notes_ref[9 + strip] = pot_in[0:8, here]
        for part in range(2):
            notes_ref[9 + strips * (part + 1) + strip] = state_in[part, 0:8, here]
    notes_copy = pltpu.make_async_copy(notes_ref, notes_out, written.at[1])
    notes_copy.start()
    copy.wait()
    notes_copy.wait()


def block_kernel(got_ref, ham_ref, out_ref, held_ref, arrived):
    rows = ham_ref.shape[2]
    pieces, size = held_ref.shape[:2]
    copies = [
        pltpu.make_async_copy(ham_ref.at[0, pl.ds(k * size, size)], held_ref.at[k], arrived.at[k]) for k in range(pieces)
    ]
    for copy in copies:
        copy.start()
    total = jnp.zeros((16, rows), jnp.float32)
    for k, copy in enumerate(copies):
        copy.wait()
        for part in range(size // rows):
            lhs = both_halves(got_ref[k * (size // rows) + part, 8:10])
            for weights in two(held_ref[k, part * rows : (part + 1) * rows]):
                total = total + jnp.dot(lhs, weights, preferred_element_type=jnp.float32)
    out_ref[...] = total[0:2] + total[2:4]


def gather_kernel(flags_ref, got_ref, after_ref, out_ref):
    strips = got_ref.shape[0]
    for k in range(4):
        strip = flags_ref[1] + (k - 2)
        there = (strip >= 0) & (strip < strips)
        near = got_ref[jnp.clip(strip, 0, strips - 1), 8:10]
        out_ref[2 * k : 2 * k + 2] = jnp.where(there, near, 0.0)
    out_ref[8:16] = sum(got_ref[strip, 0:8] for strip in range(strips))
    out_ref[16:20] = got_ref[0, 10:14]
    out_ref[20:24] = jnp.zeros((4, got_ref.shape[2]), jnp.float32)


def join_kernel(mine_ref, other_ref, out_ref):
    count = mine_ref.shape[0] - 16
    out_ref[0:count] = mine_ref[0:count]
    out_ref[count : 2 * count] = other_ref[0:count]
    out_ref[2 * count :] = mine_ref[count:] + other_ref[count:]


def join(mine, other):
    return run(join_kernel, [(2 * mine.shape[0] - 16, mine.shape[1])], (mine, other), [whole()] * 2)[0]


def inner_result(flags_ref, partners_ref, offsets_ref, block_ref, inner_ref, mine_ref, other_ref, coupling_ref, amp_ref, member, row):
    result = block_ref[...] - shift * inner_ref[...]
    couplings, band_width = coupling_ref.shape[1:3]
    block_index = flags_ref[0]
    for couple_index in range(couplings):
        apart = partners_ref[block_index, couple_index] ^ block_index
        far_pair = lax.shift_right_logical(apart, 2)
        slot = apart ^ (2 * far_pair)
        rows = pl.ds(pl.multiple_of(lax.rem(slot, 4) * 8, 8), 8)
        near = jnp.where(slot < 4, mine_ref[rows], other_ref[rows])
        near = jnp.concatenate([near[2 * k : 2 * k + 2] for k in range(4)], axis=1)
        near = jnp.concatenate([near, jnp.zeros((6, near.shape[1]), jnp.float32)], axis=0)
        first = offsets_ref[block_index, couple_index] + band_width
        window = pltpu.roll(near, near.shape[1] - first, 1)[0:2, :band_width]
        result = result + few_rows_dot(window, two(coupling_ref[0, couple_index]))
    return result + bloch_coef * few_rows_dot(row * member, two(amp_ref[0, 0]), flipped=True)


def unpacked(mine_ref, other_ref):
    sums = mine_ref[32:48] + other_ref[32:48]
    ghosts = jnp.concatenate([sums[0:4], sums[4:8]], axis=1)
    row = jnp.concatenate([sums[8:10], sums[10:12]], axis=1)
    return ghosts, row


def points_of(ref, part, first, count):
    return jnp.concatenate(
        [ref[part, strip, pl.ds(first * 8, count, stride=8)] for strip in range(ref.shape[1])], axis=1
    )


def between_kernel(
    flags_ref, partners_ref, offsets_ref, block_ref, inner_ref, mine_ref, other_ref, coupling_ref, amp_ref, group_ref, wide_ref, mix_ref,
    low_ref, high_ref, image_ref, chunk_ref, extra_out, held_ref, written, extra_ref, extra_written,
):
    member = member_of(group_ref, flags_ref)
    ghosts, row = unpacked(mine_ref, other_ref)
    image = inner_result(
        flags_ref, partners_ref, offsets_ref, block_ref, inner_ref, mine_ref, other_ref, coupling_ref, amp_ref, member, row
    )
    image_ref[...] = image
    near, far = ghosts[0:2], ghosts[2:4]
    kinetic = [kinetic_coef * (16.0 * near - far), -kinetic_coef * near]
    slope = jnp.concatenate([far - 8.0 * near, near, jnp.zeros((12, near.shape[1]), jnp.float32)], axis=0)
    mixed = mixed_with(*two(slope), mix_ref)
    is_first = flags_ref[2] == 1
    rows = []
    for part in range(2):
        extra = [
            kinetic[k][part : part + 1]
            + (mixed[2 * k + 1 : 2 * k + 2] if part == 0 else -mixed[2 * k : 2 * k + 1])
            for k in range(2)
        ]
        extra = jnp.concatenate(extra + [jnp.zeros((6, near.shape[1]), jnp.float32)], axis=0)
        extra = jnp.where(is_first, extra, 0.0)
        extra_ref[part] = jnp.concatenate([jnp.zeros((4, near.shape[1]), jnp.float32), extra[0:4]], axis=0)
        rows.append(points_of(wide_ref, part, reach, 8)[0:1] + extra[0:1])
    row = jnp.where(is_first, jnp.concatenate(rows, axis=0), 0.0)
    copy = pltpu.make_async_copy(extra_ref, extra_out, extra_written)
    copy.start()
    amps = [two(amp_ref[0, radius]) for radius in range(2)]
    write_chunk(chunk_ref, held_ref, written, image, ghost_rows(image, amps, member), row)
    copy.wait()


def last_kernel(
    flags_ref, partners_ref, offsets_ref, block_ref, inner_ref, mine_ref, other_ref, coupling_ref, amp_ref, group_ref, wide_ref, mix_ref,
    start_ref, second_ref, notes_ref,
    image_ref, out_ref, parts_ref, edge_ref,
):
    member = member_of(group_ref, flags_ref)
    ghosts, row = unpacked(mine_ref, other_ref)
    image = inner_result(
        flags_ref, partners_ref, offsets_ref, block_ref, inner_ref, mine_ref, other_ref, coupling_ref, amp_ref, member, row
    )
    image_ref[...] = image
    is_first = flags_ref[2] == 1
    strips = wide_ref.shape[1]
    noted = [
        jnp.concatenate([notes_ref[9 + strips * k + strip] for strip in range(strips)], axis=1) for k in range(3)
    ]
    local, slopes = [], []
    for part in range(2):
        ghost = jnp.concatenate([ghosts[2 + part : 3 + part], ghosts[part : part + 1]], axis=0)
        edge_ref[part, 0:8] = points_of(wide_ref, part, 0, 8)
        edge_ref[part, 6:8] = jnp.where(is_first, ghost, edge_ref[part, 0:2])
        edge_ref[part, 8:24] = points_of(wide_ref, part, reach, 16)
        inner, slope = stencils([edge_ref[part, 8 + k : 16 + k] for k in range(-reach, reach + 1)], noted[0])
        local.append(inner)
        slopes.append(slope)
    mixed = mixed_with(*two(jnp.concatenate(slopes, axis=0)), mix_parts(mix_ref))
    q = [local[0] + mixed[8:16], local[1] - mixed[0:8]]
    top = lax.broadcasted_iota(jnp.int32, q[0].shape, 0) < 4
    for part in range(2):
        q[part] = jnp.where(top, q[part], points_of(second_ref, part, 0, 8))
        out_ref[part] = q[part]
    edge = products(noted[1:], [edge_ref[part, 8:16] for part in range(2)], q)
    start, inner = start_ref[...], inner_ref[...]
    inside = products([start[0:1], start[1:2]], [inner[0:1], inner[1:2]], [image[0:1], image[1:2]])
    lane = lax.broadcasted_iota(jnp.int32, (1, lanes), 1)
    sums = jnp.zeros((1, lanes), jnp.float32)
    for k in range(9):
        tile = jnp.where(top, edge[k], 0.0)
        tile = notes_ref[k] + sum(tile[:, strip * lanes : (strip + 1) * lanes] for strip in range(strips))
        line = jnp.sum(tile, axis=0, keepdims=True) + inside[k][:, :lanes] + inside[k][:, lanes:]
        sums = jnp.where(lane == k, jnp.sum(line, axis=1, keepdims=True), sums)
    parts_ref[...] = jnp.broadcast_to(sums, parts_ref.shape)


def arnoldi_coefs(gram):
    ss, spr, spi, sqr, sqi, pp, pqr, pqi, qq = gram
    cr, ci = spr / ss, spi / ss
    left_1 = pp - (spr * cr + spi * ci)
    h10 = jnp.sqrt(left_1 / ss)
    sxr = sqr - (cr * spr - ci * spi)
    sxi = sqi - (cr * spi + ci * spr)
    h01r, h01i = sxr / (ss * h10), sxi / (ss * h10)
    pxr, pxi = pqr - cr * pp, pqi - ci * pp
    yxr = pxr - (cr * sxr + ci * sxi)
    yxi = pxi - (cr * sxi - ci * sxr)
    scale = 1.0 / left_1
    h11r, h11i = yxr * scale, yxi * scale
    xx = (qq - 2.0 * (cr * pqr + ci * pqi) + (cr * cr + ci * ci) * pp) * scale
    left_2 = xx - (h01r * h01r + h01i * h01i) - (h11r * h11r + h11i * h11i)
    h21 = jnp.sqrt(left_2)
    fine = (left_1 > least_left * pp) & (left_2 > least_left * xx)
    poor = jnp.where(fine, 0.0, 1.0)
    zero = jnp.zeros_like(ss)
    entries = [[[cr + shift, h10, zero], [h01r, h11r + shift, h21]], [[ci, zero, zero], [h01i, h11i, zero]]]
    a = jnp.sqrt(ss)
    coef_q = 1.0 / (a * h10 * h21)
    coef_p = (-(cr + h11r) * coef_q, -(ci + h11i) * coef_q)
    coef_s = (
        (h11r * cr - h11i * ci) * coef_q - h01r / (a * h21),
        (h11r * ci + h11i * cr) * coef_q - h01i / (a * h21),
    )
    return entries, (coef_q, coef_p, coef_s), poor


def combined(coefs, s, p, q):
    coef_q, coef_p, coef_s = coefs
    return (
        coef_q * q[0] + coef_p[0] * p[0] - coef_p[1] * p[1] + coef_s[0] * s[0] - coef_s[1] * s[1],
        coef_q * q[1] + coef_p[0] * p[1] + coef_p[1] * p[0] + coef_s[0] * s[1] + coef_s[1] * s[0],
    )


def finish_kernel(
    entries, parts_ref, start_ref, inner_ref, image_ref, state_ref, wide_ref, second_ref, edge_ref,
    inner_out, outer_out, hess_out, poor_out, coef_ref,
):
    step = pl.program_id(0)
    count = outer_out.shape[1]
    strips, places = second_ref.shape[1:3]
    length = places // 8

    @pl.when(step == 0)
    def _():
        sums = jnp.sum(parts_ref[...], axis=0, keepdims=True) * (1.0 / entries)
        lane = lax.broadcasted_iota(jnp.int32, sums.shape, 1)
        gram = [jnp.sum(jnp.where(lane == k, sums, 0.0), axis=1, keepdims=True) for k in range(9)]
        values, (coef_q, coef_p, coef_s), poor = arnoldi_coefs(gram)
        for k, coef in enumerate([coef_q, *coef_p, *coef_s]):
            coef_ref[k] = jnp.broadcast_to(coef, (8, lanes))
        lane = lax.broadcasted_iota(jnp.int32, (1, TERMS + 1), 1)
        for part in range(2):
            for column in range(TERMS):
                line = jnp.zeros((1, TERMS + 1), jnp.float32)
                for k, value in enumerate(values[part][column]):
                    line = jnp.where(lane == k, value, line)
                hess_out[part, column : column + 1] = line
        poor_out[...] = jnp.broadcast_to(poor, poor_out.shape)

    coefs = coef_ref[0], (coef_ref[1], coef_ref[2]), (coef_ref[3], coef_ref[4])
    few = count // length
    for run_index in range(few):
        own = step * few + run_index
        for first in range(0, length, 8):
            rows = pl.ds(pl.multiple_of(own * length + first, 8), 8)
            for strip in range(strips):
                result = combined(
                    coefs,
                    [state_ref[part, rows, strip * lanes : (strip + 1) * lanes] for part in range(2)],
                    [wide_ref[part, strip, pl.ds((first + reach) * 8 + own, 8, stride=8)] for part in range(2)],
                    [second_ref[part, strip, pl.ds(first * 8 + own, 8, stride=8)] for part in range(2)],
                )
                for part in range(2):
                    outer_out[
                        part,
                        run_index * length + first : run_index * length + first + 8,
                        strip * lanes : (strip + 1) * lanes,
                    ] = result[part]

    @pl.when(step == 0)
    def _():
        for strip in range(strips):
            here = slice(strip * lanes, (strip + 1) * lanes)
            result = combined(
                coefs,
                [state_ref[part, 0:8, here] for part in range(2)],
                [wide_ref[part, strip, pl.ds(reach * 8, 8, stride=8)] for part in range(2)],
                [edge_ref[part, :, here] for part in range(2)],
            )
            for part in range(2):
                outer_out[part, 0:8, here] = result[part]
        rows = inner_out.shape[1]
        for first in range(0, rows, lanes):
            here = slice(first, first + lanes)
            result = combined(
                [coefs[0][0:1], [c[0:1] for c in coefs[1]], [c[0:1] for c in coefs[2]]],
                *[[ref[0:1, here], ref[1:2, here]] for ref in (start_ref, inner_ref, image_ref)],
            )
            for part in range(2):
                inner_out[part : part + 1, here] = result[part]


def same_kernel(in_ref, out_ref):
    out_ref[...] = in_ref[...]


def across_blocks(mine):
    blocks = lax.axis_size("rad")
    last = blocks // 2 - 1
    mine = join(mine, lax.ppermute(mine, "rad", [(i, i ^ 1) for i in range(blocks)]))
    mine = join(mine, lax.ppermute(mine, "rad", [(i, i ^ 2) for i in range(blocks)]))
    return mine, lax.ppermute(mine, "rad", [(i, 2 * (last - i // 2) + i % 2) for i in range(blocks)])


def body(*inputs):
    (
        inner_state,
        outer_state,
        inner_ham,
        inner_coupling,
        surface_amp,
        potential,
        laser_mix,
        partners,
        band_offsets,
        channel_group,
    ) = inputs
    block_order, rows = inner_ham.shape[1:]
    points, channels = outer_state.shape[1:]
    count = lax.axis_size(both)
    blocks, strips = lax.axis_size("rad"), lax.axis_size("chan")
    entries = float(blocks * block_order + count * points * channels)
    block_index, chan_index = lax.axis_index("rad"), lax.axis_index("chan")
    position = lax.axis_index(both)
    flags = jnp.stack(
        [block_index, chan_index, (position == 0).astype(jnp.int32), (position == count - 1).astype(jnp.int32)]
    )
    group = channel_group.reshape(1, channels)
    f32, bf16 = jnp.float32, jnp.bfloat16
    out_strips = channels // lanes
    folded_rows = points + 2 * reach * 8

    chunk_scratch = [pltpu.VMEM((16, rows), f32), pltpu.SemaphoreType.DMA((strips,))]
    chunk = pl.pallas_call(
        start_kernel,
        grid=(1,),
        out_shape=pltpu.HBM((strips, 16, rows), f32),
        in_specs=[scalars(), whole(), in_one((2, 8, channels)), whole(), whole()],
        out_specs=far(),
        scratch_shapes=chunk_scratch,
        compiler_params=pltpu.CompilerParams(vmem_limit_bytes=vmem_bytes),
    )(flags, inner_state, outer_state, surface_amp, group)
    got = lax.all_to_all(chunk, "chan", 0, 0)
    wide, mix, first_rows, last_rows = pl.pallas_call(
        first_outer_kernel,
        out_shape=[
            jax.ShapeDtypeStruct((2, out_strips, folded_rows, lanes), f32),
            jax.ShapeDtypeStruct((3 * channels, channels), bf16),
            pltpu.HBM((3, 4, channels), f32),
            pltpu.HBM((3, 4, channels), f32),
        ],
        in_specs=[whole()] * 3,
        out_specs=[whole(), whole(), far(), far()],
        scratch_shapes=[
            pltpu.VMEM((2, out_strips, points + 2 * margin, lanes), f32),
            pltpu.VMEM((out_strips, points + 2 * margin, lanes), f32),
            pltpu.VMEM((2, folded_rows, channels), bf16),
            pltpu.VMEM((2, folded_rows, channels), bf16),
            pltpu.VMEM((2, 3, 4, channels), f32),
            pltpu.SemaphoreType.DMA((2,)),
        ],
        compiler_params=pltpu.CompilerParams(vmem_limit_bytes=vmem_bytes),
    )(outer_state, potential, laser_mix)

    def block_product(got):
        pieces = 8
        return run(
            block_kernel,
            [(2, rows)],
            (got, inner_ham),
            [whole(), anywhere()],
            [pltpu.VMEM((pieces, block_order // pieces, rows), f32), pltpu.SemaphoreType.DMA((pieces,))],
        )[0]

    (mine,) = run(gather_kernel, [(24, rows)], (flags, got, wide), [scalars(), whole(), anywhere()])
    mine, first_rows, last_rows = lax.optimization_barrier((mine, first_rows, last_rows))
    low, high = neighbours(last_rows, first_rows)
    mine, other = across_blocks(mine)
    block_part = block_product(got)
    p_inner, chunk, extra = pl.pallas_call(
        between_kernel,
        out_shape=[
            jax.ShapeDtypeStruct((2, rows), f32),
            pltpu.HBM((strips, 16, rows), f32),
            pltpu.HBM((2, 8, channels), f32),
        ],
        in_specs=[scalars()] * 3 + [whole()] * 9 + [anywhere()] * 2,
        out_specs=[whole(), far(), far()],
        scratch_shapes=chunk_scratch + [pltpu.VMEM((2, 8, channels), f32), pltpu.SemaphoreType.DMA],
        compiler_params=pltpu.CompilerParams(vmem_limit_bytes=vmem_bytes),
    )(
        flags, partners, band_offsets, block_part, inner_state, mine, other, inner_coupling, surface_amp, group, wide,
        mix, low, high,
    )
    got = lax.all_to_all(chunk, "chan", 0, 0)
    q_shape, notes_shape = (2, out_strips, points, lanes), (9 + 3 * out_strips, 8, lanes)
    wide, second, notes = pl.pallas_call(
        second_outer_kernel,
        grid=(1,),
        out_shape=[
            jax.ShapeDtypeStruct((2, out_strips, folded_rows, lanes), f32),
            pltpu.HBM(q_shape, f32),
            pltpu.HBM(notes_shape, f32),
        ],
        in_specs=[scalars(), in_one((2, 8, channels)), in_one((3, 4, channels)), in_one((3, 4, channels))]
        + [whole()] * 4,
        out_specs=[whole(), far(), far()],
        scratch_shapes=[pltpu.VMEM((2, points, channels), bf16)] * 2
        + [
            pltpu.VMEM(q_shape, f32),
            pltpu.VMEM((out_strips, points, lanes), f32),
            pltpu.VMEM((2, 2, 24, channels), f32),
            pltpu.VMEM(q_shape, f32),
            pltpu.VMEM(notes_shape, f32),
            pltpu.SemaphoreType.DMA((2,)),
        ],
        input_output_aliases={4: 0},
        compiler_params=pltpu.CompilerParams(vmem_limit_bytes=vmem_bytes),
    )(flags, pltpu.with_memory_space_constraint(extra, pltpu.HBM), low, high, wide, outer_state, potential, mix)
    (mine,) = run(
        gather_kernel, [(24, rows)], (flags, got, pltpu.with_memory_space_constraint(notes, pltpu.HBM)), [scalars(), whole(), far()]
    )
    mine, other = across_blocks(mine)
    block_part = block_product(got)
    q_inner, q_head, parts = run(
        last_kernel,
        [(2, rows), (2, 8, channels), (count, lanes)],
        (
            flags, partners, band_offsets, block_part, p_inner, mine, other, inner_coupling, surface_amp, group, wide,
            laser_mix, inner_state, second, notes,
        ),
        [scalars()] * 3 + [whole()] * 12,
        [pltpu.VMEM((2, 24, channels), f32)],
    )
    parts = lax.all_to_all(parts.reshape(count, 1, lanes), both, 0, 0).reshape(count, lanes)
    steps = 4
    last_inner, last_outer, columns, poor = pl.pallas_call(
        lambda *refs: finish_kernel(entries, *refs),
        grid=(steps,),
        out_shape=[
            jax.ShapeDtypeStruct(shape, f32)
            for shape in ((2, rows), (2, points, channels), (2, TERMS, TERMS + 1), (1, lanes))
        ],
        in_specs=[whole()] * 8,
        out_specs=[
            pl.BlockSpec((2, rows), lambda step: (0, 0)),
            pl.BlockSpec((2, points // steps, channels), lambda step: (0, step, 0)),
            pl.BlockSpec((2, TERMS, TERMS + 1), lambda step: (0, 0, 0)),
            pl.BlockSpec((1, lanes), lambda step: (0, 0)),
        ],
        scratch_shapes=[pltpu.VMEM((5, 8, lanes), f32)],
        compiler_params=pltpu.CompilerParams(vmem_limit_bytes=vmem_bytes),
    )(parts, inner_state, p_inner, q_inner, outer_state, wide, second, q_head)

    def again(state):
        last_inner, last_outer, hessenberg = step_by_step(*inputs)
        columns = hessenberg.transpose(0, 2, 1)
        (columns,) = run(same_kernel, [columns.shape], (columns,), [whole()])
        return jnp.zeros((), f32), last_inner, last_outer, columns

    _, last_inner, last_outer, columns = lax.while_loop(
        lambda state: state[0] > 0.0, again, (poor[0, 0], last_inner, last_outer, columns)
    )
    return last_inner, last_outer, columns.transpose(0, 2, 1)


def solution(mesh):
    return jax.shard_map(
        body,
        mesh=mesh,
        in_specs=(
            P(None, ("rad", "chan")),
            P(None, ("rad", "chan"), None),
            P("rad", None, "chan"),
            P("rad", None, None, "chan"),
            P("rad", None, "chan", None),
            P(("rad", "chan"), None),
            P(),
            P(),
            P(),
            P(),
        ),
        out_specs=(P(None, ("rad", "chan")), P(None, ("rad", "chan"), None), P()),
        check_vma=False,
    )
```

time: 183 us -> 89.8 us (0.49)
  matrix products: 36.1 us -> 0 us
  local copies, waits for them, and re-layouts: 31.1 us -> 0.34 us
  Pallas kernels: 0 us -> 27.6 us
  other arithmetic: 26.8 us -> 0.08 us
  between operations: 22.6 us -> 1.1 us
  blocking collectives: 0 us -> 17 us
  waiting for transfers between devices: 26.8 us -> 11.4 us
  starting transfers between devices: 37.6 us -> 31.1 us
    dot_general x14 -> x0, matrix products: 36.1 us -> none  [the longest x4 15.1 us: outer_apply(): jnp.einsum('prc,cd->prd', slope_rows, laser_mix, precision=highest)]
    pallas_call x0 -> x14, Pallas kernels: none -> 27.6 us  [the longest x9 8.61 us: run(): pl.pallas_call(kernel, out_shape=[jax.ShapeDtypeStruct(*out) if isinstanc...]
    all_to_all x5 -> x2, waiting for transfers between devices: 26.8 us -> 3.85 us  [body(): got = lax.all_to_all(chunk, 'chan', 0, 0)]
    another operation x7 -> x0, local copies, waits for them, and re-layouts: 17.5 us -> none  [the longest x3 17.2 us: gram_parts(): jnp.stack([real_of(s, s), real_of(s, p), imag_of(s, p), real_of(s, q), im...]
    all_to_all x0 -> x1, blocking collectives: none -> 17 us  [body(): lax.all_to_all(parts.reshape(count, 1, lanes), both, 0, 0)]
    all_to_all x5 -> x2, starting transfers between devices: 26.1 us -> 15.9 us  [body(): got = lax.all_to_all(chunk, 'chan', 0, 0)]
    ppermute x2 -> x8, waiting for transfers between devices: 0.01 us -> 7.52 us  [the longest x2 4.01 us: across_blocks(): lax.ppermute(mine, 'rad', [(i, i ^ 2) for i in range(blocks)])]
    add x5 -> x0, other arithmetic: 7.4 us -> none  [the longest x2 5.08 us: outer_apply(): kinetic_coef * laplace + (potential - moved) * centre_row]
  transfers between devices with their start and end apart: 7 -> 10, of which waited for: 5 -> 7; matrix products, arithmetic and copies ran while one was open for 8% -> 0% of each run, Pallas kernels for 0% -> 19%
where the time goes in v3:
time: 89.8 us; the launch traced here: 89.3 us
  starting transfers between devices  31.1 us (35%)
  Pallas kernels  27.6 us (31%)
  blocking collectives  17 us (19%)
  waiting for transfers between devices  11.4 us (13%)
  between operations  1.1 us (1%)
    all_to_all x1, blocking collectives, body(): lax.all_to_all(parts.reshape(count, 1, lanes), both, 0, 0)  17 us
    all_to_all x2, starting transfers between devices, body(): got = lax.all_to_all(chunk, 'chan', 0, 0)  15.9 us
    pallas_call x9, Pallas kernels, run(): pl.pallas_call(kernel, out_shape=[jax.ShapeDtypeStruct(*out) if isinstanc...  8.61 us
    ppermute x1, starting transfers between devices, neighbours(): lax.ppermute(first_rows, both, backward)  6.69 us
    pallas_call x1, Pallas kernels, body(): pl.pallas_call(second_outer_kernel, grid=(1,), out_shape=[jax.ShapeDtypeS...  6.42 us
    pallas_call x1, Pallas kernels, body(): pl.pallas_call(first_outer_kernel, out_shape=[jax.ShapeDtypeStruct((2, ou...  5.2 us
    ppermute x2, waiting for transfers between devices, across_blocks(): lax.ppermute(mine, 'rad', [(i, i ^ 2) for i in range(blocks)])  4.01 us
    all_to_all x2, waiting for transfers between devices, body(): got = lax.all_to_all(chunk, 'chan', 0, 0)  3.85 us
  transfers between devices with their start and end apart: 10, of which 7 were waited for; matrix products, arithmetic and copies ran while one was open for 0% of the time, Pallas kernels for 19%

profile of v3, /device:TPU:1, one launch (start us, length us, event | category | flops | bytes accessed | tf_op | source)
XLA Modules:
  0.0 89.3 jit_solution(15994670725383119783)
XLA Ops:
  0.6 0.1 pad_add_fusion.flags_ref
  0.7 2.4 %shard_map.121 = f32[16,16,256]{2,1,0:T(8,128)} custom-call(s32[4]{0:T(128)S(1)} %pad_add_fusion.flags_ref, f32[2,256]{1,0:T(2,128)} %refs_1_.1, f32[2,384,512]{2,1,0:T(8,128)} %refs_4_.1, f32[1,2,256,512]{3,2,1,0:T(8,128)} %amp_ref.5, s32[1,512]{1,0:T(1,128)} %bitcast.134), custom_call_target="tpu_custom_call" | custom-call | tf_op jit(solution)/shard_map/pallas_call | solution.py:750
  3.1 8.6 %all-to-all-start.4 = ((f32[16,16,256]{2,1,0:T(8,128)}), f32[16,16,256]{2,1,0:T(8,128)S(1)}, u32[]{:S(2)}, u32[]{:S(2)}) async-start(f32[16,16,256]{2,1,0:T(8,128)} %shard_map.121), calls=%async_computation.4 | async-start | bytes 524288 | tf_op jit(solution)/shard_map/all_to_all | solution.py:759
  11.7 5.2 %shard_map.123 = (f32[2,4,416,128]{3,2,1,0:T(8,128)S(1)}, bf16[1536,512]{1,0:T(8,128)(2,1)S(1)}, f32[3,4,512]{2,1,0:T(4,128)}, f32[3,4,512]{2,1,0:T(4,128)}) custom-call(f32[2,384,512]{2,1,0:T(8,128)} %refs_4_.1, f32[384,512]{1,0:T(8,128)} %pot_in.1, f32[512,512]{1,0:T(8,128)} %mix_ref.3), custom_call_target="tpu_custom_call" | custom-call | tf_op jit(solution)/shard_map/pallas_call | solution.py:760
  16.9 0.0 copy-start.28
  16.9 0.0 copy-start.30
  17.0 2.3 %all-to-all-done.4.got_ref = f32[16,16,256]{2,1,0:T(8,128)S(1)} async-done(((f32[16,16,256]{2,1,0:T(8,128)}), f32[16,16,256]{2,1,0:T(8,128)S(1)}, u32[]{:S(2)}, u32[]{:S(2)}) %all-to-all-start.4) | async-done | bytes 262176 | tf_op jit(solution)/shard_map/all_to_all | solution.py:759
  19.3 0.6 shard_map.124.mine_ref
  19.8 2.2 %collective-permute-start.4 = (f32[24,256]{1,0:T(8,128)S(1)}, f32[24,256]{1,0:T(8,128)S(1)}, u32[]{:S(2)}, u32[]{:S(2)}) collective-permute-start(f32[24,256]{1,0:T(8,128)S(1)} %shard_map.124.mine_ref), channel_id=1, source_target_pairs={{0,16},{16,0},{32,48},{48,32},{64,80},{80,64},{96,112},{112,96},{1... | collective-permute-start | bytes 73736 | tf_op jit(solution)/shard_map/ppermute | solution.py:716
  22.0 0.8 collective-permute-done.4.other_ref
  22.9 1.2 %collective-permute-start.5 = (f32[32,256]{1,0:T(8,128)S(1)}, f32[32,256]{1,0:T(8,128)S(1)}, u32[]{:S(2)}, u32[]{:S(2)}) collective-permute-start(f32[32,256]{1,0:T(8,128)S(1)} %shard_map.125.mine_ref), channel_id=1, source_target_pairs={{0,32},{16,48},{32,0},{48,16},{64,96},{80,112},{96,64},{112,80},{1... | collective-permute-start | bytes 98312 | tf_op jit(solution)/shard_map/ppermute | solution.py:717
  24.1 1.6 %collective-permute-done.5.other_ref = f32[32,256]{1,0:T(8,128)S(1)} collective-permute-done((f32[32,256]{1,0:T(8,128)S(1)}, f32[32,256]{1,0:T(8,128)S(1)}, u32[]{:S(2)}, u32[]{:S(2)}) %collective-permute-start.5) | collective-permute-done | bytes 32800 | tf_op jit(solution)/shard_map/ppermute | solution.py:717
  25.6 0.6 shard_map.126.mine_ref
  26.3 2.5 %collective-permute-start.6 = (f32[48,256]{1,0:T(8,128)}, f32[48,256]{1,0:T(8,128)}, u32[]{:S(2)}, u32[]{:S(2)}) collective-permute-start(f32[48,256]{1,0:T(8,128)} %shard_map.126.mine_ref), channel_id=1, source_target_pairs={{0,96},{16,112},{32,64},{48,80},{64,32},{80,48},{96,0},{112,16},{1... | collective-permute-start | bytes 147464 | tf_op jit(solution)/shard_map/ppermute | solution.py:718
  28.8 2.2 %collective-permute-start.7 = (f32[3,4,512]{2,1,0:T(4,128)}, f32[3,4,512]{2,1,0:T(4,128)}, u32[]{:S(2)}, u32[]{:S(2)}) collective-permute-start(f32[3,4,512]{2,1,0:T(4,128)} %get-tuple-element.158), channel_id=1, source_target_pairs={{0,1},{1,2},{2,3},{3,4},{4,5},{5,6},{6,7},{7,8},{8,9},{9,10},{10,1... | collective-permute-start | bytes 73736 | tf_op jit(solution)/shard_map/ppermute | solution.py:46
  30.9 6.7 %collective-permute-start.8 = (f32[3,4,512]{2,1,0:T(4,128)}, f32[3,4,512]{2,1,0:T(4,128)}, u32[]{:S(2)}, u32[]{:S(2)}) collective-permute-start(f32[3,4,512]{2,1,0:T(4,128)} %get-tuple-element.159), channel_id=1, source_target_pairs={{1,0},{2,1},{3,2},{4,3},{5,4},{6,5},{7,6},{8,7},{9,8},{10,9},{11,1... | collective-permute-start | bytes 73736 | tf_op jit(solution)/shard_map/ppermute | solution.py:46
  37.6 0.0 copy-done.28
  37.7 0.1 copy.47.partners_ref
  37.7 0.1 copy.48.offsets_ref
  37.8 2.7 %shard_map.122.block_ref = f32[2,256]{1,0:T(2,128)S(1)} custom-call(f32[16,16,256]{2,1,0:T(8,128)S(1)} %all-to-all-done.4.got_ref, f32[1,4096,256]{2,1,0:T(8,128)} %ham_ref.3), custom_call_target="tpu_custom_call" | custom-call | tf_op jit(solution)/shard_map/pallas_call | solution.py:195
  40.5 0.0 collective-permute-done.7.low_ref
  40.5 0.0 collective-permute-done.8.high_ref
  40.5 0.0 collective-permute-done.6.other_ref
  40.5 0.1 copy-done.19
  40.6 0.0 copy-done.22
  40.6 2.6 %shard_map.127 = (f32[2,256]{1,0:T(2,128)S(1)}, f32[16,16,256]{2,1,0:T(8,128)}, f32[2,8,512]{2,1,0:T(8,128)}) custom-call(s32[4]{0:T(128)S(1)} %pad_add_fusion.flags_ref, s32[8,2]{1,0:T(8,128)S(1)} %copy.47.partners_ref, s32[8,2]{1,0:T(8,128)S(1)} %copy.48.offsets_ref, f32[2,256]{1,0:T(2,128)S(1)} %shard_map.122.block_ref, f32[2,256]{1,0:T(2,128)S(1)} %copy-done.22, ...), custom_call_target="tpu_custom_call" | custom-call | tf_op jit(solution)/shard_map/pallas_call | solution.py:796
  43.2 7.3 %all-to-all-start.5 = ((f32[16,16,256]{2,1,0:T(8,128)}), f32[16,16,256]{2,1,0:T(8,128)S(1)}, u32[]{:S(2)}, u32[]{:S(2)}) async-start(f32[16,16,256]{2,1,0:T(8,128)} %get-tuple-element.160), calls=%async_computation.5 | async-start | bytes 524288 | tf_op jit(solution)/shard_map/all_to_all | solution.py:811
  50.5 6.4 %shard_map.129 = (f32[2,4,416,128]{3,2,1,0:T(8,128)S(1)}, f32[2,4,384,128]{3,2,1,0:T(8,128)}, f32[21,8,128]{2,1,0:T(8,128)}) custom-call(s32[4]{0:T(128)S(1)} %pad_add_fusion.flags_ref, f32[2,8,512]{2,1,0:T(8,128)} %get-tuple-element.162.extra_ref, f32[3,4,512]{2,1,0:T(4,128)} %collective-permute-done.7.low_ref, ...), custom_call_target="tpu_custom_call", output_to_operand_aliasing={{0}: (4, {})} | custom-call | tf_op jit(solution)/shard_map/pallas_call | solution.py:813
  56.9 1.5 %all-to-all-done.5.got_ref = f32[16,16,256]{2,1,0:T(8,128)S(1)} async-done(((f32[16,16,256]{2,1,0:T(8,128)}), f32[16,16,256]{2,1,0:T(8,128)S(1)}, u32[]{:S(2)}, u32[]{:S(2)}) %all-to-all-start.5) | async-done | bytes 262176 | tf_op jit(solution)/shard_map/all_to_all | solution.py:811
  58.4 0.6 shard_map.130.mine_ref
  59.0 0.1 collective-permute-start.9
  59.1 1.2 %collective-permute-done.9.other_ref = f32[24,256]{1,0:T(8,128)S(1)} collective-permute-done((f32[24,256]{1,0:T(8,128)S(1)}, f32[24,256]{1,0:T(8,128)S(1)}, u32[]{:S(2)}, u32[]{:S(2)}) %collective-permute-start.9) | collective-permute-done | bytes 24608 | tf_op jit(solution)/shard_map/ppermute | solution.py:716
  60.3 0.3 collective-permute-start.10
  60.6 2.5 %collective-permute-done.10.other_ref = f32[32,256]{1,0:T(8,128)S(1)} collective-permute-done((f32[32,256]{1,0:T(8,128)S(1)}, f32[32,256]{1,0:T(8,128)S(1)}, u32[]{:S(2)}, u32[]{:S(2)}) %collective-permute-start.10) | collective-permute-done | bytes 32800 | tf_op jit(solution)/shard_map/ppermute | solution.py:717
  63.1 0.0 copy-start.16
  63.1 0.0 copy-start.20
  63.1 0.0 copy-start.23
  63.1 0.0 copy-start.26
  63.1 0.1 collective-permute-start.11
  63.2 2.7 %shard_map.128.block_ref = f32[2,256]{1,0:T(2,128)S(1)} custom-call(f32[16,16,256]{2,1,0:T(8,128)S(1)} %all-to-all-done.5.got_ref, f32[1,4096,256]{2,1,0:T(8,128)} %ham_ref.3), custom_call_target="tpu_custom_call" | custom-call | tf_op jit(solution)/shard_map/pallas_call | solution.py:195
  65.9 1.5 %collective-permute-done.11.other_ref = f32[48,256]{1,0:T(8,128)S(1)} collective-permute-done((f32[48,256]{1,0:T(8,128)S(1)}, f32[48,256]{1,0:T(8,128)S(1)}, u32[]{:S(2)}, u32[]{:S(2)}) %collective-permute-start.11) | collective-permute-done | bytes 49184 | tf_op jit(solution)/shard_map/ppermute | solution.py:718
  67.4 0.0 copy-done
  67.4 0.0 copy-start.4
  67.4 1.5 %shard_map.133 = (f32[2,256]{1,0:T(2,128)S(1)}, f32[2,8,512]{2,1,0:T(8,128)S(1)}, f32[128,128]{1,0:T(8,128)S(1)}) custom-call(s32[4]{0:T(128)S(1)} %pad_add_fusion.flags_ref, s32[8,2]{1,0:T(8,128)S(1)} %copy.47.partners_ref, s32[8,2]{1,0:T(8,128)S(1)} %copy.48.offsets_ref, f32[2,256]{1,0:T(2,128)S(1)} %shard_map.128.block_ref, ...), custom_call_target="tpu_custom_call" | custom-call | tf_op jit(solution)/shard_map/pallas_call | solution.py:195
  69.0 17.0 %all_to_all.31 = f32[128,1,128]{2,1,0:T(1,128)S(1)} all-to-all(f32[128,1,128]{2,1,0:T(1,128)S(1)} %bitcast.127), channel_id=1, replica_groups=mesh['rad'=8,'chan'=16] {'rad','chan'}, dimensions={0} | all-to-all | bytes 131072 | tf_op jit(solution)/shard_map/all_to_all | solution.py:851
  85.9 0.0 copy-start.31
  85.9 2.4 %shard_map.134 = (f32[2,256]{1,0:T(2,128)}, f32[2,384,512]{2,1,0:T(8,128)}, f32[2,2,3]{2,1,0:T(2,128)}, f32[1,128]{1,0:T(1,128)}) custom-call(f32[128,128]{1,0:T(8,128)S(1)} %bitcast.125, f32[2,256]{1,0:T(2,128)S(1)} %copy-done.23, f32[2,256]{1,0:T(2,128)S(1)} %get-tuple-element.161.inner_ref.refs_2_, f32[2,256]{1,0:T(2,128)S(1)} %get-tuple-element.167.refs_3_, ...), custom_call_target="tpu_custom_call" | custom-call | tf_op jit(solution)/shard_map/pallas_call | solution.py:853
  88.4 0.7 while.18
  (27 shorter events, 0.1 us)
Async XLA Ops:
  3.1 16.2 %all-to-all-start.4 = ((f32[16,16,256]{2,1,0:T(8,128)}), f32[16,16,256]{2,1,0:T(8,128)S(1)}, u32[]{:S(2)}, u32[]{:S(2)}) async-start(f32[16,16,256]{2,1,0:T(8,128)} %shard_map.121), calls=%async_computation.4 | async-start | bytes 524288 | tf_op jit(solution)/shard_map/all_to_all | solution.py:759
  16.9 20.7 %copy-start.28 = (s32[8,2]{0,1:T(2,128)S(1)}, s32[8,2]{0,1:T(2,128)}, u32[]{:S(2)}) copy-start(s32[8,2]{0,1:T(2,128)} %param.29) | copy-start | bytes 196
  16.9 20.8 %copy-start.30 = (s32[8,2]{0,1:T(2,128)S(1)}, s32[8,2]{0,1:T(2,128)}, u32[]{:S(2)}) copy-start(s32[8,2]{0,1:T(2,128)} %param.30) | copy-start | bytes 196
  19.8 3.0 %collective-permute-start.4 = (f32[24,256]{1,0:T(8,128)S(1)}, f32[24,256]{1,0:T(8,128)S(1)}, u32[]{:S(2)}, u32[]{:S(2)}) collective-permute-start(f32[24,256]{1,0:T(8,128)S(1)} %shard_map.124.mine_ref), channel_id=1, source_target_pairs={{0,16},{16,0},{32,48},{48,32},{64,80},{80,64},{96,112},{112,96},{1... | collective-permute-start | bytes 73736 | tf_op jit(solution)/shard_map/ppermute | solution.py:716
  22.9 2.8 %collective-permute-start.5 = (f32[32,256]{1,0:T(8,128)S(1)}, f32[32,256]{1,0:T(8,128)S(1)}, u32[]{:S(2)}, u32[]{:S(2)}) collective-permute-start(f32[32,256]{1,0:T(8,128)S(1)} %shard_map.125.mine_ref), channel_id=1, source_target_pairs={{0,32},{16,48},{32,0},{48,16},{64,96},{80,112},{96,64},{112,80},{1... | collective-permute-start | bytes 98312 | tf_op jit(solution)/shard_map/ppermute | solution.py:717
  26.3 14.2 %collective-permute-start.6 = (f32[48,256]{1,0:T(8,128)}, f32[48,256]{1,0:T(8,128)}, u32[]{:S(2)}, u32[]{:S(2)}) collective-permute-start(f32[48,256]{1,0:T(8,128)} %shard_map.126.mine_ref), channel_id=1, source_target_pairs={{0,96},{16,112},{32,64},{48,80},{64,32},{80,48},{96,0},{112,16},{1... | collective-permute-start | bytes 147464 | tf_op jit(solution)/shard_map/ppermute | solution.py:718
  28.8 11.7 %collective-permute-start.7 = (f32[3,4,512]{2,1,0:T(4,128)}, f32[3,4,512]{2,1,0:T(4,128)}, u32[]{:S(2)}, u32[]{:S(2)}) collective-permute-start(f32[3,4,512]{2,1,0:T(4,128)} %get-tuple-element.158), channel_id=1, source_target_pairs={{0,1},{1,2},{2,3},{3,4},{4,5},{5,6},{6,7},{7,8},{8,9},{9,10},{10,1... | collective-permute-start | bytes 73736 | tf_op jit(solution)/shard_map/ppermute | solution.py:46
  30.9 9.6 %collective-permute-start.8 = (f32[3,4,512]{2,1,0:T(4,128)}, f32[3,4,512]{2,1,0:T(4,128)}, u32[]{:S(2)}, u32[]{:S(2)}) collective-permute-start(f32[3,4,512]{2,1,0:T(4,128)} %get-tuple-element.159), channel_id=1, source_target_pairs={{1,0},{2,1},{3,2},{4,3},{5,4},{6,5},{7,6},{8,7},{9,8},{10,9},{11,1... | collective-permute-start | bytes 73736 | tf_op jit(solution)/shard_map/ppermute | solution.py:46
  37.8 2.7 %copy-start.15 = (f32[1,2,512,256]{3,2,1,0:T(8,128)S(1)}, f32[1,2,512,256]{3,2,1,0:T(8,128)}, u32[]{:S(2)}) copy-start(f32[1,2,512,256]{3,2,1,0:T(8,128)} %coupling_ref.3) | copy-start | bytes 3145732
  37.8 2.8 %copy-start.19 = (f32[1,2,256,512]{3,2,1,0:T(8,128)S(1)}, f32[1,2,256,512]{3,2,1,0:T(8,128)}, u32[]{:S(2)}) copy-start(f32[1,2,256,512]{3,2,1,0:T(8,128)} %amp_ref.5) | copy-start | bytes 3145732
  37.8 2.8 %copy-start.22 = (f32[2,256]{1,0:T(2,128)S(1)}, f32[2,256]{1,0:T(2,128)}, u32[]{:S(2)}) copy-start(f32[2,256]{1,0:T(2,128)} %refs_1_.1) | copy-start | bytes 6148
  37.8 2.8 %copy-start.25 = (s32[512]{0:T(512)S(1)}, s32[512]{0:T(512)}, u32[]{:S(2)}) copy-start(s32[512]{0:T(512)} %param.31) | copy-start | bytes 6148
  43.2 15.2 %all-to-all-start.5 = ((f32[16,16,256]{2,1,0:T(8,128)}), f32[16,16,256]{2,1,0:T(8,128)S(1)}, u32[]{:S(2)}, u32[]{:S(2)}) async-start(f32[16,16,256]{2,1,0:T(8,128)} %get-tuple-element.160), calls=%async_computation.5 | async-start | bytes 524288 | tf_op jit(solution)/shard_map/all_to_all | solution.py:811
  58.4 8.9 %copy-start.21 = (f32[512,512]{1,0:T(8,128)S(1)}, f32[512,512]{1,0:T(8,128)}, u32[]{:S(2)}) copy-start(f32[512,512]{1,0:T(8,128)} %mix_ref.3) | copy-start | bytes 3145732
  59.0 1.3 %collective-permute-start.9 = (f32[24,256]{1,0:T(8,128)S(1)}, f32[24,256]{1,0:T(8,128)S(1)}, u32[]{:S(2)}, u32[]{:S(2)}) collective-permute-start(f32[24,256]{1,0:T(8,128)S(1)} %shard_map.130.mine_ref), channel_id=1, source_target_pairs={{0,16},{16,0},{32,48},{48,32},{64,80},{80,64},{96,112},{112,96},{1... | collective-permute-start | bytes 73736 | tf_op jit(solution)/shard_map/ppermute | solution.py:716
  60.3 2.8 %collective-permute-start.10 = (f32[32,256]{1,0:T(8,128)S(1)}, f32[32,256]{1,0:T(8,128)S(1)}, u32[]{:S(2)}, u32[]{:S(2)}) collective-permute-start(f32[32,256]{1,0:T(8,128)S(1)} %shard_map.131.mine_ref), channel_id=1, source_target_pairs={{0,32},{16,48},{32,0},{48,16},{64,96},{80,112},{96,64},{112,80},{1... | collective-permute-start | bytes 98312 | tf_op jit(solution)/shard_map/ppermute | solution.py:717
  63.1 4.3 %copy-start = (f32[2,4,384,128]{3,2,1,0:T(8,128)S(1)}, f32[2,4,384,128]{3,2,1,0:T(8,128)}, u32[]{:S(2)}) copy-start(f32[2,4,384,128]{3,2,1,0:T(8,128)} %get-tuple-element.165.second_ref.refs_6_) | copy-start | bytes 4718596
  63.1 4.3 %copy-start.1 = (f32[21,8,128]{2,1,0:T(8,128)S(1)}, f32[21,8,128]{2,1,0:T(8,128)}, u32[]{:S(2)}) copy-start(f32[21,8,128]{2,1,0:T(8,128)} %get-tuple-element.163.after_ref.notes_ref) | copy-start | bytes 258052
  63.1 4.3 %copy-start.16 = (f32[1,2,512,256]{3,2,1,0:T(8,128)S(1)}, f32[1,2,512,256]{3,2,1,0:T(8,128)}, u32[]{:S(2)}) copy-start(f32[1,2,512,256]{3,2,1,0:T(8,128)} %coupling_ref.3) | copy-start | bytes 3145732
  63.1 4.3 %copy-start.20 = (f32[1,2,256,512]{3,2,1,0:T(8,128)S(1)}, f32[1,2,256,512]{3,2,1,0:T(8,128)}, u32[]{:S(2)}) copy-start(f32[1,2,256,512]{3,2,1,0:T(8,128)} %amp_ref.5) | copy-start | bytes 3145732
  63.1 4.3 %copy-start.23 = (f32[2,256]{1,0:T(2,128)S(1)}, f32[2,256]{1,0:T(2,128)}, u32[]{:S(2)}) copy-start(f32[2,256]{1,0:T(2,128)} %refs_1_.1) | copy-start | bytes 6148
  63.1 4.3 %copy-start.26 = (s32[512]{0:T(512)S(1)}, s32[512]{0:T(512)}, u32[]{:S(2)}) copy-start(s32[512]{0:T(512)} %param.31) | copy-start | bytes 6148
  63.1 4.2 %collective-permute-start.11 = (f32[48,256]{1,0:T(8,128)S(1)}, f32[48,256]{1,0:T(8,128)S(1)}, u32[]{:S(2)}, u32[]{:S(2)}) collective-permute-start(f32[48,256]{1,0:T(8,128)S(1)} %shard_map.132.mine_ref), channel_id=1, source_target_pairs={{0,96},{16,112},{32,64},{48,80},{64,32},{80,48},{96,0},{112,16},{1... | collective-permute-start | bytes 147464 | tf_op jit(solution)/shard_map/ppermute | solution.py:718
  67.4 18.5 %copy-start.4 = (f32[2,384,512]{2,1,0:T(8,128)S(1)}, f32[2,384,512]{2,1,0:T(8,128)}, u32[]{:S(2)}) copy-start(f32[2,384,512]{2,1,0:T(8,128)} %refs_4_.1) | copy-start | bytes 4718596
  85.9 2.4 %copy-start.24 = (f32[2,256]{1,0:T(2,128)S(1)}, f32[2,256]{1,0:T(2,128)}, u32[]{:S(2)}) copy-start(f32[2,256]{1,0:T(2,128)} %refs_1_.1) | copy-start | bytes 6148
  85.9 2.4 %copy-start.27 = (s32[512]{0:T(512)S(1)}, s32[512]{0:T(512)}, u32[]{:S(2)}) copy-start(s32[512]{0:T(512)} %param.31) | copy-start | bytes 6148
  85.9 2.4 %copy-start.29 = (s32[8,2]{0,1:T(2,128)S(1)}, s32[8,2]{0,1:T(2,128)}, u32[]{:S(2)}) copy-start(s32[8,2]{0,1:T(2,128)} %param.29) | copy-start | bytes 196
  85.9 2.4 %copy-start.31 = (s32[8,2]{0,1:T(2,128)S(1)}, s32[8,2]{0,1:T(2,128)}, u32[]{:S(2)}) copy-start(s32[8,2]{0,1:T(2,128)} %param.30) | copy-start | bytes 196

commit v4 on v3

--- a/solution.py
+++ b/solution.py
@@ -222,16 +222,12 @@
 
 
 def mixed_with(high, low, mix_ref):
-    lhs = jnp.concatenate([high, low, high], axis=1)
-    return jnp.dot(lhs, mix_ref[...], preferred_element_type=jnp.float32)
-
-
-def mix_parts(mix_ref):
-    high, low = two(slope_coef * mix_ref[...])
-    return jnp.concatenate([high, high, low], axis=0)
-
-
-def write_chunk(out_ref, held_ref, written, inner_vec, ghosts, row):
+    count = high.shape[0]
+    first = jnp.dot(jnp.concatenate([high, low], axis=0), mix_ref[0], preferred_element_type=jnp.float32)
+    return first[:count] + first[count:] + jnp.dot(high, mix_ref[1], preferred_element_type=jnp.float32)
+
+
+def write_chunk(out_ref, held_ref, written, inner_vec, ghosts, row, others=()):
     half = inner_vec.shape[1]
     held_ref[...] = jnp.concatenate(
         [
@@ -245,11 +241,12 @@
         axis=0,
     )
     copies = [
-        pltpu.make_async_copy(held_ref, out_ref.at[strip], written.at[strip]) for strip in range(out_ref.shape[0])
+        pltpu.make_async_copy(held_ref, out_ref.at[strip, pl.ds(0, 16)], written.at[strip])
+        for strip in range(out_ref.shape[0])
     ]
     for copy in copies:
         copy.start()
-    for copy in copies:
+    for copy in [*others, *copies]:
         copy.wait()
 
 
@@ -257,19 +254,51 @@
     return jnp.concatenate([few_rows_dot(inner_vec, amp) * member for amp in amps], axis=0)
 
 
-def member_of(group_ref, flags_ref):
-    return jnp.where(group_ref[...] == flags_ref[0], 1.0, 0.0)
+def member_of(group_ref):
+    return jnp.where(group_ref[...] == lax.axis_index("rad"), 1.0, 0.0)
+
+
+def at_first():
+    return (lax.axis_index("rad") == 0) & (lax.axis_index("chan") == 0)
+
+
+def at_last():
+    last = [lax.axis_index(axis) == lax.axis_size(axis) - 1 for axis in both]
+    return last[0] & last[1]
+
+
+def send_ends(chunk_ref, ends_ref, written, first_rows, last_rows):
+    half = ends_ref.shape[2]
+    for end, points in enumerate((last_rows, first_rows)):
+        for k in range(2):
+            for part in range(2):
+                ends_ref[end, 4 * k + 2 * part : 4 * k + 2 * part + 2] = points[part][:, k * half : (k + 1) * half]
+    strips = chunk_ref.shape[0]
+    copies = [
+        pltpu.make_async_copy(
+            ends_ref.at[end],
+            chunk_ref.at[lax.rem(lax.axis_index("chan") + there, strips), pl.ds(16, 8)],
+            written.at[end],
+        )
+        for end, there in enumerate((1, strips - 1))
+    ]
+    for copy in copies:
+        copy.start()
+    return copies
 
 
 def start_kernel(
-    flags_ref, inner_ref, head_ref, amp_ref, group_ref, chunk_ref, held_ref, written
+    inner_ref, head_ref, tail_ref, amp_ref, group_ref, chunk_ref, held_ref, written, ends_ref, ends_written
 ):
+    ends = send_ends(
+        chunk_ref, ends_ref, ends_written, [head_ref[part, 0:2] for part in range(2)], [tail_ref[part, 6:8] for part in range(2)]
+    )
     row = jnp.concatenate([head_ref[part, 0:1] for part in range(2)], axis=0)
-    row = jnp.where(flags_ref[2] == 1, row, 0.0)
+    row = jnp.where(at_first(), row, 0.0)
     inner_vec = inner_ref[...]
     amps = [two(amp_ref[0, radius]) for radius in range(2)]
-    ghosts = ghost_rows(inner_vec, amps, member_of(group_ref, flags_ref))
-    write_chunk(chunk_ref, held_ref, written, inner_vec, ghosts, row)
+    ghosts = ghost_rows(inner_vec, amps, member_of(group_ref))
+    write_chunk(chunk_ref, held_ref, written, inner_vec, ghosts, row, ends)
 
 
 def stencils(window, pot):
@@ -281,7 +310,7 @@
 
 
 def first_outer_kernel(
-    state_ref, pot_ref, mix_ref, out_ref, mix_out, first_out, last_out, wide_ref, pot_wide, slope_h, slope_l, ends_ref, written
+    state_ref, pot_ref, mix_ref, out_ref, mix_out, edges_ref, wide_ref, pot_wide, slope_h, slope_l
 ):
     points, channels = state_ref.shape[1:]
     strips = channels // lanes
@@ -296,12 +325,7 @@
             target[margin + points :] = jnp.zeros((margin, lanes), jnp.float32)
     for part in range(3):
         source = pot_ref if part == 2 else state_ref.at[part]
-        ends_ref[0, part], ends_ref[1, part] = source[0:4], source[points - 4 : points]
-    copies = [
-        pltpu.make_async_copy(ends_ref.at[end], out, written.at[end]) for end, out in enumerate((first_out, last_out))
-    ]
-    for copy in copies:
-        copy.start()
+        edges_ref[0, part], edges_ref[1, part] = source[0:8], source[points - 8 : points]
 
     def strip_step(step, _):
         part, strip = lax.div(step, strips), lax.rem(step, strips)
@@ -324,10 +348,8 @@
         return 0
 
     lax.fori_loop(0, 2 * strips, strip_step, 0)
-    mix_out[...] = mix_parts(mix_ref)
+    mix_out[0], mix_out[1] = two(slope_coef * mix_ref[...])
     add_mixed(out_ref, slope_h, slope_l, mix_out)
-    for copy in copies:
-        copy.wait()
 
 
 def add_mixed(out_ref, slope_h, slope_l, mix_ref):
@@ -352,45 +374,17 @@
     ]
 
 
-def mend_edges(flags_ref, extra_ref, low_ref, high_ref, state_in, pot_in, mix_ref, wide_ref, edge_ref):
-    points, channels = pot_in.shape
-    strips, places = wide_ref.shape[1:3]
-    local, slopes = [], []
-    for part in range(2):
-        for end in range(2):
-            edge = edge_ref.at[part, end]
-            edge[...] = jnp.zeros_like(edge)
-            edge[4:8] = low_ref[part] if end == 0 else state_in[part, points - 4 : points]
-            edge[8:12] = state_in[part, 0:4] if end == 0 else high_ref[part]
-            if end == 0:
-                pot = jnp.concatenate([low_ref[2], pot_in[0:4]], axis=0)
-            else:
-                pot = jnp.concatenate([pot_in[points - 4 : points], high_ref[2]], axis=0)
-            inner, slope = stencils([edge[4 + k : 12 + k] for k in range(-reach, reach + 1)], pot)
-            local.append(inner)
-            slopes.append(slope)
-    mixed = mixed_with(*two(jnp.concatenate(slopes, axis=0)), mix_ref)
-    row = lax.broadcasted_iota(jnp.int32, (8, channels), 0)
-    outside = [(row < 4) & (flags_ref[2] == 1), (row >= 4) & (flags_ref[3] == 1)]
-    for part in range(2):
-        for end in range(2):
-            other = mixed[16 * (1 - part) + 8 * end : 16 * (1 - part) + 8 * end + 8]
-            p = local[2 * part + end] + (other if part == 0 else -other)
-            p = jnp.where(outside[end], 0.0, p)
-            if end == 0:
-                p = p + extra_ref[part]
-            for strip in range(strips):
-                first = 0 if end == 0 else places - 8 * 4 + 7
-                wide_ref[part, strip, pl.ds(first, 4, stride=8)] = p[2:6, strip * lanes : (strip + 1) * lanes]
-
-
 def second_outer_kernel(
-    flags_ref, extra_ref, low_ref, high_ref, wide_in, state_in, pot_in, mix_ref,
-    wide_ref, q_out, notes_out, slope_h, slope_l, state_ref, pot_ref, edge_ref, out_ref, notes_ref, written,
+    patch_ref, wide_in, state_in, pot_in, mix_ref,
+    wide_ref, q_out, notes_out, slope_h, slope_l, state_ref, pot_ref, out_ref, notes_ref, written,
 ):
-    mend_edges(flags_ref, extra_ref, low_ref, high_ref, state_in, pot_in, mix_ref, wide_ref, edge_ref)
     strips, places = out_ref.shape[1:3]
     length = places // 8
+    for part in range(2):
+        for strip in range(strips):
+            here = slice(strip * lanes, (strip + 1) * lanes)
+            wide_ref[part, strip, pl.ds(reach * 8, 2, stride=8)] = patch_ref[part, 0:2, here]
+            wide_ref[part, strip, pl.ds(length * 8 + 7, 2, stride=8)] = patch_ref[part, 2:4, here]
     for strip in range(strips):
         here = slice(strip * lanes, (strip + 1) * lanes)
         pot_ref[strip] = pot_in[:, here]
@@ -421,7 +415,7 @@
     add_mixed(out_ref, slope_h, slope_l, mix_ref)
     copy = pltpu.make_async_copy(out_ref, q_out, written.at[0])
     copy.start()
-    inside = lax.broadcasted_iota(jnp.int32, (8, lanes), 0) > 0
+    run_of = lax.broadcasted_iota(jnp.int32, (8, lanes), 0)
 
     def gram_step(strip, sums):
         for place in range(length):
@@ -430,7 +424,8 @@
                 [wide_ref[part, strip, (place + reach) * 8 : (place + reach + 1) * 8] for part in range(2)],
                 [out_ref[part, strip, place * 8 : (place + 1) * 8] for part in range(2)],
             )
-            if place < 4:
+            if place < 4 or place >= length - 4:
+                inside = run_of > 0 if place < 4 else run_of < 7
                 entries = [jnp.where(inside, entry, 0.0) for entry in entries]
             sums = [total + entry for total, entry in zip(sums, entries)]
         return sums
@@ -440,20 +435,22 @@
         notes_ref[k] = sums[k]
     for strip in range(strips):
         here = slice(strip * lanes, (strip + 1) * lanes)
-        notes_ref[9 + strip] = pot_in[0:8, here]
-        for part in range(2):
-            notes_ref[9 + strips * (part + 1) + strip] = state_in[part, 0:8, here]
+        for end, rows in enumerate((slice(0, 8), slice(places - 8, places))):
+            notes_ref[9 + strips * 3 * end + strip] = pot_in[rows, here]
+            for part in range(2):
+                notes_ref[9 + strips * (3 * end + part + 1) + strip] = state_in[part, rows, here]
     notes_copy = pltpu.make_async_copy(notes_ref, notes_out, written.at[1])
     notes_copy.start()
     copy.wait()
     notes_copy.wait()
 
 
-def block_kernel(got_ref, ham_ref, out_ref, held_ref, arrived):
+def block_kernel(first, got_ref, ham_ref, out_ref, held_ref, arrived):
     rows = ham_ref.shape[2]
     pieces, size = held_ref.shape[:2]
     copies = [
-        pltpu.make_async_copy(ham_ref.at[0, pl.ds(k * size, size)], held_ref.at[k], arrived.at[k]) for k in range(pieces)
+        pltpu.make_async_copy(ham_ref.at[0, pl.ds((first + k) * size, size)], held_ref.at[k], arrived.at[k])
+        for k in range(pieces)
     ]
     for copy in copies:
         copy.start()
@@ -461,48 +458,56 @@
     for k, copy in enumerate(copies):
         copy.wait()
         for part in range(size // rows):
-            lhs = both_halves(got_ref[k * (size // rows) + part, 8:10])
+            lhs = both_halves(got_ref[(first + k) * (size // rows) + part, 8:10])
             for weights in two(held_ref[k, part * rows : (part + 1) * rows]):
                 total = total + jnp.dot(lhs, weights, preferred_element_type=jnp.float32)
     out_ref[...] = total[0:2] + total[2:4]
 
 
-def gather_kernel(flags_ref, got_ref, after_ref, out_ref):
+def gather_kernel(got_ref, after_ref, out_ref, ends_ref):
     strips = got_ref.shape[0]
+    own = lax.axis_index("chan")
     for k in range(4):
-        strip = flags_ref[1] + (k - 2)
+        strip = own + (k - 2)
         there = (strip >= 0) & (strip < strips)
         near = got_ref[jnp.clip(strip, 0, strips - 1), 8:10]
         out_ref[2 * k : 2 * k + 2] = jnp.where(there, near, 0.0)
     out_ref[8:16] = sum(got_ref[strip, 0:8] for strip in range(strips))
     out_ref[16:20] = got_ref[0, 10:14]
     out_ref[20:24] = jnp.zeros((4, got_ref.shape[2]), jnp.float32)
-
-
-def join_kernel(mine_ref, other_ref, out_ref):
-    count = mine_ref.shape[0] - 16
+    before = got_ref[lax.rem(own + strips - 1, strips), 16:24]
+    after = got_ref[lax.rem(own + 1, strips), 16:24]
+    ends_ref[0], ends_ref[1] = before, after
+    out_ref[24:32] = jnp.where(own == 0, before, after)
+
+
+def join_kernel(mine_ref, other_ref, after_ref, out_ref):
+    count = mine_ref.shape[0] - 24
     out_ref[0:count] = mine_ref[0:count]
     out_ref[count : 2 * count] = other_ref[0:count]
-    out_ref[2 * count :] = mine_ref[count:] + other_ref[count:]
-
-
-def join(mine, other):
-    return run(join_kernel, [(2 * mine.shape[0] - 16, mine.shape[1])], (mine, other), [whole()] * 2)[0]
-
-
-def inner_result(flags_ref, partners_ref, offsets_ref, block_ref, inner_ref, mine_ref, other_ref, coupling_ref, amp_ref, member, row):
-    result = block_ref[...] - shift * inner_ref[...]
+    out_ref[2 * count : 2 * count + 16] = mine_ref[count : count + 16] + other_ref[count : count + 16]
+    keep = (count > 8) | ((lax.rem(lax.axis_index("rad"), 2) == 1) == (lax.axis_index("chan") == 0))
+    out_ref[2 * count + 16 :] = jnp.where(keep, mine_ref[count + 16 :], other_ref[count + 16 :])
+
+
+def join(mine, other, after):
+    shape = (2 * mine.shape[0] - 24, mine.shape[1])
+    return run(join_kernel, [shape], (mine, other, after), [whole()] * 2 + [anywhere()])[0]
+
+
+def inner_result(partners_ref, offsets_ref, block_a, block_b, block_c, inner_ref, mine_ref, other_ref, coupling_ref, amp_ref, member, row):
+    result = block_a[...] + block_b[...] + block_c[...] - shift * inner_ref[...]
     couplings, band_width = coupling_ref.shape[1:3]
-    block_index = flags_ref[0]
+    block_index = lax.axis_index("rad")
     for couple_index in range(couplings):
-        apart = partners_ref[block_index, couple_index] ^ block_index
+        apart = partners_ref[couple_index, block_index] ^ block_index
         far_pair = lax.shift_right_logical(apart, 2)
         slot = apart ^ (2 * far_pair)
         rows = pl.ds(pl.multiple_of(lax.rem(slot, 4) * 8, 8), 8)
         near = jnp.where(slot < 4, mine_ref[rows], other_ref[rows])
         near = jnp.concatenate([near[2 * k : 2 * k + 2] for k in range(4)], axis=1)
         near = jnp.concatenate([near, jnp.zeros((6, near.shape[1]), jnp.float32)], axis=0)
-        first = offsets_ref[block_index, couple_index] + band_width
+        first = offsets_ref[couple_index, block_index] + band_width
         window = pltpu.roll(near, near.shape[1] - first, 1)[0:2, :band_width]
         result = result + few_rows_dot(window, two(coupling_ref[0, couple_index]))
     return result + bloch_coef * few_rows_dot(row * member, two(amp_ref[0, 0]), flipped=True)
@@ -515,86 +520,137 @@
     return ghosts, row
 
 
-def points_of(ref, part, first, count):
+def points_of(ref, part, first, count, run_index=0):
     return jnp.concatenate(
-        [ref[part, strip, pl.ds(first * 8, count, stride=8)] for strip in range(ref.shape[1])], axis=1
-    )
+        [ref[part, strip, pl.ds(first * 8 + run_index, count, stride=8)] for strip in range(ref.shape[1])], axis=1
+    )
+
+
+def mend(edge_ref, pots, mix_ref, more=None):
+    local, slopes = [], []
+    for part in range(2):
+        for end in range(2):
+            inner, slope = stencils([edge_ref[part, end, 8 + k : 16 + k] for k in range(-reach, reach + 1)], pots[end])
+            local.append(inner)
+            slopes.append(slope)
+    mixed = mixed_with(*two(jnp.concatenate(slopes + ([] if more is None else [more]), axis=0)), mix_ref)
+    image = [
+        [
+            local[2 * part + end] + (mixed[16 + 8 * end : 24 + 8 * end] if part == 0 else -mixed[8 * end : 8 * end + 8])
+            for end in range(2)
+        ]
+        for part in range(2)
+    ]
+    return image, mixed[32:]
+
+
+def pick_ends(ends_ref, core_ref, near_ref, far_ref):
+    block, strip = lax.axis_index("rad"), lax.axis_index("chan")
+    core, chip = lax.rem(block, 2), lax.div(block, 2)
+    is_low, is_high = strip == 0, strip == lax.axis_size("chan") - 1
+    from_core = (core == 1) == is_low
+    from_near = (lax.rem(chip, 2) == 1) == is_low
+    came = jnp.where(from_core, core_ref[24:32], jnp.where(from_near, near_ref[32:40], far_ref[48:56]))
+    before = jnp.where(at_first(), 0.0, jnp.where(is_low, came, ends_ref[0]))
+    after = jnp.where(at_last(), 0.0, jnp.where(is_high, came, ends_ref[1]))
+    return [
+        [jnp.concatenate([x[2 * part : 2 * part + 2], x[4 + 2 * part : 6 + 2 * part]], axis=1) for part in range(2)]
+        for x in (before, after)
+    ]
 
 
 def between_kernel(
-    flags_ref, partners_ref, offsets_ref, block_ref, inner_ref, mine_ref, other_ref, coupling_ref, amp_ref, group_ref, wide_ref, mix_ref,
-    low_ref, high_ref, image_ref, chunk_ref, extra_out, held_ref, written, extra_ref, extra_written,
+    partners_ref, offsets_ref, block_a, block_b, block_c, inner_ref, mine_ref, other_ref, coupling_ref, amp_ref, group_ref,
+    edges_ref, mix_ref, ends_ref, core_ref, near_ref,
+    image_ref, chunk_ref, patch_out, held_ref, written, send_ref, ends_written, patch_ref, patch_written, edge_ref,
 ):
-    member = member_of(group_ref, flags_ref)
+    member = member_of(group_ref)
+    ghosts, row = unpacked(mine_ref, other_ref)
+    before, after = pick_ends(ends_ref, core_ref, near_ref, other_ref)
+    edge_ref[...] = jnp.zeros_like(edge_ref)
+    for part in range(2):
+        edge_ref[part, 0, 6:8] = before[part]
+        edge_ref[part, 1, 16:18] = after[part]
+        for end in range(2):
+            edge_ref[part, end, 8:16] = edges_ref[end, part]
+    near, far_off = ghosts[0:2], ghosts[2:4]
+    kinetic = [kinetic_coef * (16.0 * near - far_off), -kinetic_coef * near]
+    slope = jnp.concatenate([far_off - 8.0 * near, near, jnp.zeros((12, near.shape[1]), jnp.float32)], axis=0)
+    p, mixed = mend(edge_ref, [edges_ref[end, 2] for end in range(2)], mix_ref, slope)
+    first_rows, last_rows = [], []
+    for part in range(2):
+        extra = jnp.concatenate(
+            [
+                kinetic[k][part : part + 1]
+                + (mixed[2 * k + 1 : 2 * k + 2] if part == 0 else -mixed[2 * k : 2 * k + 1])
+                for k in range(2)
+            ],
+            axis=0,
+        )
+        first_rows.append(p[part][0][0:2] + jnp.where(at_first(), extra, 0.0))
+        last_rows.append(p[part][1][6:8])
+        patch_ref[part] = jnp.concatenate(
+            [first_rows[part], last_rows[part], jnp.zeros((4, near.shape[1]), jnp.float32)], axis=0
+        )
+    copy = pltpu.make_async_copy(patch_ref, patch_out, patch_written)
+    copy.start()
+    copies = [copy] + send_ends(chunk_ref, send_ref, ends_written, first_rows, last_rows)
+    image = inner_result(
+        partners_ref, offsets_ref, block_a, block_b, block_c, inner_ref, mine_ref, other_ref, coupling_ref, amp_ref, member, row
+    )
+    image_ref[...] = image
+    row = jnp.where(at_first(), jnp.concatenate([rows[0:1] for rows in first_rows], axis=0), 0.0)
+    amps = [two(amp_ref[0, radius]) for radius in range(2)]
+    write_chunk(chunk_ref, held_ref, written, image, ghost_rows(image, amps, member), row, copies)
+
+
+def last_kernel(
+    partners_ref, offsets_ref, block_a, block_b, block_c, inner_ref, mine_ref, other_ref, coupling_ref, amp_ref, group_ref,
+    wide_ref, mix_ref, ends_ref, core_ref, near_ref, start_ref, second_ref, notes_ref,
+    image_ref, out_ref, parts_ref, edge_ref,
+):
+    member = member_of(group_ref)
     ghosts, row = unpacked(mine_ref, other_ref)
     image = inner_result(
-        flags_ref, partners_ref, offsets_ref, block_ref, inner_ref, mine_ref, other_ref, coupling_ref, amp_ref, member, row
+        partners_ref, offsets_ref, block_a, block_b, block_c, inner_ref, mine_ref, other_ref, coupling_ref, amp_ref, member, row
     )
     image_ref[...] = image
-    near, far = ghosts[0:2], ghosts[2:4]
-    kinetic = [kinetic_coef * (16.0 * near - far), -kinetic_coef * near]
-    slope = jnp.concatenate([far - 8.0 * near, near, jnp.zeros((12, near.shape[1]), jnp.float32)], axis=0)
-    mixed = mixed_with(*two(slope), mix_ref)
-    is_first = flags_ref[2] == 1
-    rows = []
-    for part in range(2):
-        extra = [
-            kinetic[k][part : part + 1]
-            + (mixed[2 * k + 1 : 2 * k + 2] if part == 0 else -mixed[2 * k : 2 * k + 1])
-            for k in range(2)
+    strips = wide_ref.shape[1]
+    length = second_ref.shape[2] // 8
+    noted = [
+        [
+            jnp.concatenate([notes_ref[9 + strips * (3 * end + k) + strip] for strip in range(strips)], axis=1)
+            for k in range(3)
         ]
-        extra = jnp.concatenate(extra + [jnp.zeros((6, near.shape[1]), jnp.float32)], axis=0)
-        extra = jnp.where(is_first, extra, 0.0)
-        extra_ref[part] = jnp.concatenate([jnp.zeros((4, near.shape[1]), jnp.float32), extra[0:4]], axis=0)
-        rows.append(points_of(wide_ref, part, reach, 8)[0:1] + extra[0:1])
-    row = jnp.where(is_first, jnp.concatenate(rows, axis=0), 0.0)
-    copy = pltpu.make_async_copy(extra_ref, extra_out, extra_written)
-    copy.start()
-    amps = [two(amp_ref[0, radius]) for radius in range(2)]
-    write_chunk(chunk_ref, held_ref, written, image, ghost_rows(image, amps, member), row)
-    copy.wait()
-
-
-def last_kernel(
-    flags_ref, partners_ref, offsets_ref, block_ref, inner_ref, mine_ref, other_ref, coupling_ref, amp_ref, group_ref, wide_ref, mix_ref,
-    start_ref, second_ref, notes_ref,
-    image_ref, out_ref, parts_ref, edge_ref,
-):
-    member = member_of(group_ref, flags_ref)
-    ghosts, row = unpacked(mine_ref, other_ref)
-    image = inner_result(
-        flags_ref, partners_ref, offsets_ref, block_ref, inner_ref, mine_ref, other_ref, coupling_ref, amp_ref, member, row
-    )
-    image_ref[...] = image
-    is_first = flags_ref[2] == 1
-    strips = wide_ref.shape[1]
-    noted = [
-        jnp.concatenate([notes_ref[9 + strips * k + strip] for strip in range(strips)], axis=1) for k in range(3)
+        for end in range(2)
     ]
-    local, slopes = [], []
+    before, after = pick_ends(ends_ref, core_ref, near_ref, other_ref)
+    edge_ref[...] = jnp.zeros_like(edge_ref)
     for part in range(2):
         ghost = jnp.concatenate([ghosts[2 + part : 3 + part], ghosts[part : part + 1]], axis=0)
-        edge_ref[part, 0:8] = points_of(wide_ref, part, 0, 8)
-        edge_ref[part, 6:8] = jnp.where(is_first, ghost, edge_ref[part, 0:2])
-        edge_ref[part, 8:24] = points_of(wide_ref, part, reach, 16)
-        inner, slope = stencils([edge_ref[part, 8 + k : 16 + k] for k in range(-reach, reach + 1)], noted[0])
-        local.append(inner)
-        slopes.append(slope)
-    mixed = mixed_with(*two(jnp.concatenate(slopes, axis=0)), mix_parts(mix_ref))
-    q = [local[0] + mixed[8:16], local[1] - mixed[0:8]]
-    top = lax.broadcasted_iota(jnp.int32, q[0].shape, 0) < 4
-    for part in range(2):
-        q[part] = jnp.where(top, q[part], points_of(second_ref, part, 0, 8))
-        out_ref[part] = q[part]
-    edge = products(noted[1:], [edge_ref[part, 8:16] for part in range(2)], q)
+        edge_ref[part, 0, 6:8] = jnp.where(at_first(), ghost, before[part])
+        edge_ref[part, 0, 8:24] = points_of(wide_ref, part, reach, 16)
+        edge_ref[part, 1, 0:16] = points_of(wide_ref, part, length + reach - 16, 16, 7)
+        edge_ref[part, 1, 16:18] = after[part]
+    q, _ = mend(edge_ref, [noted[end][0] for end in range(2)], mix_ref)
+    row_of = lax.broadcasted_iota(jnp.int32, q[0][0].shape, 0)
+    mended = [row_of < 4, row_of >= 4]
+    totals = [notes_ref[k] for k in range(9)]
+    for end in range(2):
+        for part in range(2):
+            there = points_of(second_ref, part, 0 if end == 0 else length - 8, 8, 7 * end)
+            q[part][end] = jnp.where(mended[end], q[part][end], there)
+            out_ref[end, part] = q[part][end]
+        entries = products(noted[end][1:], [edge_ref[part, end, 8:16] for part in range(2)], [q[part][end] for part in range(2)])
+        for k, entry in enumerate(entries):
+            entry = jnp.where(mended[end], entry, 0.0)
+            totals[k] = totals[k] + sum(entry[:, strip * lanes : (strip + 1) * lanes] for strip in range(strips))
     start, inner = start_ref[...], inner_ref[...]
     inside = products([start[0:1], start[1:2]], [inner[0:1], inner[1:2]], [image[0:1], image[1:2]])
     lane = lax.broadcasted_iota(jnp.int32, (1, lanes), 1)
     sums = jnp.zeros((1, lanes), jnp.float32)
     for k in range(9):
-        tile = jnp.where(top, edge[k], 0.0)
-        tile = notes_ref[k] + sum(tile[:, strip * lanes : (strip + 1) * lanes] for strip in range(strips))
-        line = jnp.sum(tile, axis=0, keepdims=True) + inside[k][:, :lanes] + inside[k][:, lanes:]
+        line = jnp.sum(totals[k], axis=0, keepdims=True) + inside[k][:, :lanes] + inside[k][:, lanes:]
         sums = jnp.where(lane == k, jnp.sum(line, axis=1, keepdims=True), sums)
     parts_ref[...] = jnp.broadcast_to(sums, parts_ref.shape)
 
@@ -683,18 +739,27 @@
                         strip * lanes : (strip + 1) * lanes,
                     ] = result[part]
 
-    @pl.when(step == 0)
-    def _():
+    def put_end(end):
+        first = 0 if end == 0 else length - 8
+        rows = slice(0, 8) if end == 0 else slice(count - 8, count)
         for strip in range(strips):
             here = slice(strip * lanes, (strip + 1) * lanes)
             result = combined(
                 coefs,
-                [state_ref[part, 0:8, here] for part in range(2)],
-                [wide_ref[part, strip, pl.ds(reach * 8, 8, stride=8)] for part in range(2)],
-                [edge_ref[part, :, here] for part in range(2)],
+                [state_ref[part, 0:8, here] if end == 0 else state_ref[part, places - 8 : places, here] for part in range(2)],
+                [wide_ref[part, strip, pl.ds((first + reach) * 8 + 7 * end, 8, stride=8)] for part in range(2)],
+                [edge_ref[end, part, :, here] for part in range(2)],
             )
             for part in range(2):
-                outer_out[part, 0:8, here] = result[part]
+                outer_out[part, rows, here] = result[part]
+
+    @pl.when(step == pl.num_programs(0) - 1)
+    def _():
+        put_end(1)
+
+    @pl.when(step == 0)
+    def _():
+        put_end(0)
         rows = inner_out.shape[1]
         for first in range(0, rows, lanes):
             here = slice(first, first + lanes)
@@ -710,12 +775,14 @@
     out_ref[...] = in_ref[...]
 
 
-def across_blocks(mine):
+def across_blocks(mine, after):
     blocks = lax.axis_size("rad")
     last = blocks // 2 - 1
-    mine = join(mine, lax.ppermute(mine, "rad", [(i, i ^ 1) for i in range(blocks)]))
-    mine = join(mine, lax.ppermute(mine, "rad", [(i, i ^ 2) for i in range(blocks)]))
-    return mine, lax.ppermute(mine, "rad", [(i, 2 * (last - i // 2) + i % 2) for i in range(blocks)])
+    core = lax.ppermute(mine, "rad", [(i, i ^ 1) for i in range(blocks)])
+    mine = join(mine, core, after[0])
+    near = lax.ppermute(mine, "rad", [(i, i ^ 2) for i in range(blocks)])
+    mine = join(mine, near, after[1])
+    return mine, (core, near, lax.ppermute(mine, "rad", [(i, 2 * (last - i // 2) + i % 2) for i in range(blocks)]))
 
 
 def body(*inputs):
@@ -736,80 +803,84 @@
     count = lax.axis_size(both)
     blocks, strips = lax.axis_size("rad"), lax.axis_size("chan")
     entries = float(blocks * block_order + count * points * channels)
-    block_index, chan_index = lax.axis_index("rad"), lax.axis_index("chan")
-    position = lax.axis_index(both)
-    flags = jnp.stack(
-        [block_index, chan_index, (position == 0).astype(jnp.int32), (position == count - 1).astype(jnp.int32)]
-    )
     group = channel_group.reshape(1, channels)
+    by_coupling = partners.T, band_offsets.T
     f32, bf16 = jnp.float32, jnp.bfloat16
     out_strips = channels // lanes
     folded_rows = points + 2 * reach * 8
 
+    ends_scratch = [pltpu.VMEM((2, 8, rows), f32), pltpu.SemaphoreType.DMA((2,))]
     chunk_scratch = [pltpu.VMEM((16, rows), f32), pltpu.SemaphoreType.DMA((strips,))]
     chunk = pl.pallas_call(
         start_kernel,
         grid=(1,),
-        out_shape=pltpu.HBM((strips, 16, rows), f32),
-        in_specs=[scalars(), whole(), in_one((2, 8, channels)), whole(), whole()],
+        out_shape=pltpu.HBM((strips, 24, rows), f32),
+        in_specs=[
+            whole(),
+            in_one((2, 8, channels)),
+            pl.BlockSpec((2, 8, channels), lambda i: (0, points // 8 - 1, 0)),
+            whole(),
+            whole(),
+        ],
         out_specs=far(),
-        scratch_shapes=chunk_scratch,
+        scratch_shapes=chunk_scratch + ends_scratch,
         compiler_params=pltpu.CompilerParams(vmem_limit_bytes=vmem_bytes),
-    )(flags, inner_state, outer_state, surface_amp, group)
+    )(inner_state, outer_state, outer_state, surface_amp, group)
     got = lax.all_to_all(chunk, "chan", 0, 0)
-    wide, mix, first_rows, last_rows = pl.pallas_call(
+    wide, mix, edges = pl.pallas_call(
         first_outer_kernel,
         out_shape=[
             jax.ShapeDtypeStruct((2, out_strips, folded_rows, lanes), f32),
-            jax.ShapeDtypeStruct((3 * channels, channels), bf16),
-            pltpu.HBM((3, 4, channels), f32),
-            pltpu.HBM((3, 4, channels), f32),
+            jax.ShapeDtypeStruct((2, channels, channels), bf16),
+            jax.ShapeDtypeStruct((2, 3, 8, channels), f32),
         ],
         in_specs=[whole()] * 3,
-        out_specs=[whole(), whole(), far(), far()],
+        out_specs=[whole()] * 3,
         scratch_shapes=[
             pltpu.VMEM((2, out_strips, points + 2 * margin, lanes), f32),
             pltpu.VMEM((out_strips, points + 2 * margin, lanes), f32),
             pltpu.VMEM((2, folded_rows, channels), bf16),
             pltpu.VMEM((2, folded_rows, channels), bf16),
-            pltpu.VMEM((2, 3, 4, channels), f32),
-            pltpu.SemaphoreType.DMA((2,)),
         ],
         compiler_params=pltpu.CompilerParams(vmem_limit_bytes=vmem_bytes),
     )(outer_state, potential, laser_mix)
 
     def block_product(got):
-        pieces = 8
-        return run(
-            block_kernel,
-            [(2, rows)],
-            (got, inner_ham),
-            [whole(), anywhere()],
-            [pltpu.VMEM((pieces, block_order // pieces, rows), f32), pltpu.SemaphoreType.DMA((pieces,))],
-        )[0]
-
-    (mine,) = run(gather_kernel, [(24, rows)], (flags, got, wide), [scalars(), whole(), anywhere()])
-    mine, first_rows, last_rows = lax.optimization_barrier((mine, first_rows, last_rows))
-    low, high = neighbours(last_rows, first_rows)
-    mine, other = across_blocks(mine)
-    block_part = block_product(got)
-    p_inner, chunk, extra = pl.pallas_call(
+        size = 2 * rows
+        parts = []
+        for first, last in ((0, 2), (2, 5), (5, 8)):
+            parts += run(
+                lambda *refs, first=first: block_kernel(first, *refs),
+                [(2, rows)],
+                (got, inner_ham),
+                [whole(), anywhere()],
+                [pltpu.VMEM((last - first, size, rows), f32), pltpu.SemaphoreType.DMA((last - first,))],
+            )
+        return parts
+
+    gathered = [(32, rows), (2, 8, rows)]
+    mine, ends = run(gather_kernel, gathered, (got, wide), [whole(), anywhere()])
+    block_parts = block_product(got)
+    mine, came = across_blocks(mine, block_parts)
+    p_inner, chunk, patch = pl.pallas_call(
         between_kernel,
         out_shape=[
             jax.ShapeDtypeStruct((2, rows), f32),
-            pltpu.HBM((strips, 16, rows), f32),
+            pltpu.HBM((strips, 24, rows), f32),
             pltpu.HBM((2, 8, channels), f32),
         ],
-        in_specs=[scalars()] * 3 + [whole()] * 9 + [anywhere()] * 2,
-        out_specs=[whole(), far(), far()],
-        scratch_shapes=chunk_scratch + [pltpu.VMEM((2, 8, channels), f32), pltpu.SemaphoreType.DMA],
+        in_specs=[scalars()] * 2 + [whole()] * 14,
+        out_specs=[whole()] + [far()] * 2,
+        scratch_shapes=chunk_scratch
+        + ends_scratch
+        + [pltpu.VMEM((2, 8, channels), f32), pltpu.SemaphoreType.DMA, pltpu.VMEM((2, 2, 24, channels), f32)],
         compiler_params=pltpu.CompilerParams(vmem_limit_bytes=vmem_bytes),
     )(
-        flags, partners, band_offsets, block_part, inner_state, mine, other, inner_coupling, surface_amp, group, wide,
-        mix, low, high,
+        *by_coupling, *block_parts, inner_state, mine, came[2], inner_coupling, surface_amp, group,
+        edges, mix, ends, came[0], came[1],
     )
     got = lax.all_to_all(chunk, "chan", 0, 0)
-    q_shape, notes_shape = (2, out_strips, points, lanes), (9 + 3 * out_strips, 8, lanes)
+    q_shape, notes_shape = (2, out_strips, points, lanes), (9 + 6 * out_strips, 8, lanes)
     wide, second, notes = pl.pallas_call(
         second_outer_kernel,
         grid=(1,),
@@ -818,35 +889,33 @@
             pltpu.HBM(q_shape, f32),
             pltpu.HBM(notes_shape, f32),
         ],
-        in_specs=[scalars(), in_one((2, 8, channels)), in_one((3, 4, channels)), in_one((3, 4, channels))]
-        + [whole()] * 4,
+        in_specs=[in_one((2, 8, channels))] + [whole()] * 4,
         out_specs=[whole(), far(), far()],
         scratch_shapes=[pltpu.VMEM((2, points, channels), bf16)] * 2
         + [
             pltpu.VMEM(q_shape, f32),
             pltpu.VMEM((out_strips, points, lanes), f32),
-            pltpu.VMEM((2, 2, 24, channels), f32),
             pltpu.VMEM(q_shape, f32),
             pltpu.VMEM(notes_shape, f32),
             pltpu.SemaphoreType.DMA((2,)),
         ],
-        input_output_aliases={4: 0},
+        input_output_aliases={1: 0},
         compiler_params=pltpu.CompilerParams(vmem_limit_bytes=vmem_bytes),
-    )(flags, pltpu.with_memory_space_constraint(extra, pltpu.HBM), low, high, wide, outer_state, potential, mix)
-    (mine,) = run(
-        gather_kernel, [(24, rows)], (flags, got, pltpu.with_memory_space_constraint(notes, pltpu.HBM)), [scalars(), whole(), far()]
-    )
-    mine, other = across_blocks(mine)
-    block_part = block_product(got)
-    q_inner, q_head, parts = run(
+    )(pltpu.with_memory_space_constraint(patch, pltpu.HBM), wide, outer_state, potential, mix)
+    mine, ends = run(
+        gather_kernel, gathered, (got, pltpu.with_memory_space_constraint(notes, pltpu.HBM)), [whole(), far()]
+    )
+    block_parts = block_product(got)
+    mine, came = across_blocks(mine, block_parts)
+    q_inner, q_ends, parts = run(
         last_kernel,
-        [(2, rows), (2, 8, channels), (count, lanes)],
+        [(2, rows), (2, 2, 8, channels), (count, lanes)],
         (
-            flags, partners, band_offsets, block_part, p_inner, mine, other, inner_coupling, surface_amp, group, wide,
-            laser_mix, inner_state, second, notes,
+            *by_coupling, *block_parts, p_inner, mine, came[2], inner_coupling, surface_amp, group,
+            wide, mix, ends, came[0], came[1], inner_state, second, notes,
         ),
-        [scalars()] * 3 + [whole()] * 12,
-        [pltpu.VMEM((2, 24, channels), f32)],
+        [scalars()] * 2 + [whole()] * 17,
+        [pltpu.VMEM((2, 2, 24, channels), f32)],
     )
     parts = lax.all_to_all(parts.reshape(count, 1, lanes), both, 0, 0).reshape(count, lanes)
     steps = 4
@@ -866,7 +935,7 @@
         ],
         scratch_shapes=[pltpu.VMEM((5, 8, lanes), f32)],
         compiler_params=pltpu.CompilerParams(vmem_limit_bytes=vmem_bytes),
-    )(parts, inner_state, p_inner, q_inner, outer_state, wide, second, q_head)
+    )(parts, inner_state, p_inner, q_inner, outer_state, wide, second, q_ends)
 
     def again(state):
         last_inner, last_outer, hessenberg = step_by_step(*inputs)

time: 89.8 us -> 81.5 us (0.908)
  starting transfers between devices: 31.1 us -> 24.3 us
  Pallas kernels: 27.6 us -> 26 us
    ppermute x6 -> x4, starting transfers between devices: 12.7 us -> 7.02 us  [the longest x2 5.64 us: across_blocks(): core = lax.ppermute(mine, 'rad', [(i, i ^ 1) for i in range(blocks)])]
    all_to_all x2, starting transfers between devices: 15.9 us -> 12.2 us  [body(): got = lax.all_to_all(chunk, 'chan', 0, 0)]
    ppermute x6 -> x4, waiting for transfers between devices: 6.05 us -> 3.02 us  [the longest x2 3.02 us: across_blocks(): near = lax.ppermute(mine, 'rad', [(i, i ^ 2) for i in range(blocks)])]
    ppermute x2, starting transfers between devices: 2.56 us -> 5.12 us  [across_blocks(): lax.ppermute(mine, 'rad', [(i, 2 * (last - i // 2) + i % 2) for i in rang...]
    all_to_all x2, waiting for transfers between devices: 3.85 us -> 6.14 us  [body(): got = lax.all_to_all(chunk, 'chan', 0, 0)]
    pallas_call x9 -> x13, Pallas kernels: 8.61 us -> 7.42 us  [run(): pl.pallas_call(kernel, out_shape=[jax.ShapeDtypeStruct(*out) if isinstanc...]
  transfers between devices with their start and end apart: 10 -> 8, of which waited for: 7 -> 6; matrix products, arithmetic and copies ran while one was open for 0% -> 0% of each run, Pallas kernels for 19% -> 21%
where the time goes in v4:
time: 81.5 us; the launch traced here: 81.1 us
  Pallas kernels  26 us (32%)
  starting transfers between devices  24.3 us (30%)
  blocking collectives  17.7 us (22%)
  waiting for transfers between devices  11.2 us (14%)
  between operations  1.09 us (1%)
    all_to_all x1, blocking collectives, body(): lax.all_to_all(parts.reshape(count, 1, lanes), both, 0, 0)  17.7 us
    all_to_all x2, starting transfers between devices, body(): got = lax.all_to_all(chunk, 'chan', 0, 0)  12.2 us
    pallas_call x13, Pallas kernels, run(): pl.pallas_call(kernel, out_shape=[jax.ShapeDtypeStruct(*out) if isinstanc...  7.42 us
    all_to_all x2, waiting for transfers between devices, body(): got = lax.all_to_all(chunk, 'chan', 0, 0)  6.14 us
    pallas_call x1, Pallas kernels, body(): pl.pallas_call(second_outer_kernel, grid=(1,), out_shape=[jax.ShapeDtypeS...  6.09 us
    ppermute x2, starting transfers between devices, across_blocks(): core = lax.ppermute(mine, 'rad', [(i, i ^ 1) for i in range(blocks)])  5.64 us
    pallas_call x1, Pallas kernels, body(): pl.pallas_call(first_outer_kernel, out_shape=[jax.ShapeDtypeStruct((2, ou...  5.14 us
    ppermute x2, starting transfers between devices, across_blocks(): lax.ppermute(mine, 'rad', [(i, 2 * (last - i // 2) + i % 2) for i in rang...  5.12 us
  transfers between devices with their start and end apart: 8, of which 6 were waited for; matrix products, arithmetic and copies ran while one was open for 0% of the time, Pallas kernels for 21%

profile of v4, /device:TPU:1, one launch (start us, length us, event | category | flops | bytes accessed | tf_op | source)
XLA Modules:
  0.0 81.1 jit_solution(2459670367758781470)
XLA Ops:
  0.6 2.4 %shard_map.121 = f32[16,24,256]{2,1,0:T(8,128)} custom-call(f32[2,256]{1,0:T(2,128)} %refs_1_.13, f32[2,384,512]{2,1,0:T(8,128)} %refs_4_.1, f32[2,384,512]{2,1,0:T(8,128)} %refs_4_.1, f32[1,2,256,512]{3,2,1,0:T(8,128)} %amp_ref.5, s32[1,512]{1,0:T(1,128)} %bitcast.132), custom_call_target="tpu_custom_call" | custom-call | tf_op jit(solution)/shard_map/pallas_call | solution.py:814
  3.0 8.6 %all-to-all-start.4 = ((f32[16,24,256]{2,1,0:T(8,128)}), f32[16,24,256]{2,1,0:T(8,128)S(1)}, u32[]{:S(2)}, u32[]{:S(2)}) async-start(f32[16,24,256]{2,1,0:T(8,128)} %shard_map.121), calls=%async_computation.4 | async-start | bytes 786432 | tf_op jit(solution)/shard_map/all_to_all | solution.py:829
  11.6 5.1 %shard_map.125 = (f32[2,4,416,128]{3,2,1,0:T(8,128)S(1)}, bf16[2,512,512]{2,1,0:T(8,128)(2,1)S(1)}, f32[2,3,8,512]{3,2,1,0:T(8,128)S(1)}) custom-call(f32[2,384,512]{2,1,0:T(8,128)} %refs_4_.1, f32[384,512]{1,0:T(8,128)} %pot_in.1, f32[512,512]{1,0:T(8,128)} %mix_ref.1), custom_call_target="tpu_custom_call" | custom-call | tf_op jit(solution)/shard_map/pallas_call | solution.py:830
  16.8 4.0 %all-to-all-done.4.refs_0_.got_ref = f32[16,24,256]{2,1,0:T(8,128)S(1)} async-done(((f32[16,24,256]{2,1,0:T(8,128)}), f32[16,24,256]{2,1,0:T(8,128)S(1)}, u32[]{:S(2)}, u32[]{:S(2)}) %all-to-all-start.4) | async-done | bytes 393248 | tf_op jit(solution)/shard_map/all_to_all | solution.py:829
  20.8 0.0 copy-start.2
  20.9 1.9 %collective-permute-start.4 = (f32[32,256]{1,0:T(8,128)S(1)}, f32[32,256]{1,0:T(8,128)S(1)}, u32[]{:S(2)}, u32[]{:S(2)}) collective-permute-start(f32[32,256]{1,0:T(8,128)S(1)} %get-tuple-element.154.mine_ref), channel_id=1, source_target_pairs={{0,16},{16,0},{32,48},{48,32},{64,80},{80,64},{96,112},{112,96},{1... | collective-permute-start | bytes 98312 | tf_op jit(solution)/shard_map/ppermute | solution.py:781
  22.8 1.6 %shard_map.122.after_ref.block_a = f32[2,256]{1,0:T(2,128)S(1)} custom-call(f32[16,24,256]{2,1,0:T(8,128)S(1)} %all-to-all-done.4.refs_0_.got_ref, f32[1,4096,256]{2,1,0:T(8,128)} %refs_1_.12), custom_call_target="tpu_custom_call" | custom-call | tf_op jit(solution)/shard_map/pallas_call | solution.py:195
  24.4 0.0 collective-permute-done.4.other_ref.core_ref
  24.4 1.3 %collective-permute-start.5 = (f32[40,256]{1,0:T(8,128)S(1)}, f32[40,256]{1,0:T(8,128)S(1)}, u32[]{:S(2)}, u32[]{:S(2)}) collective-permute-start(f32[40,256]{1,0:T(8,128)S(1)} %shard_map.127.mine_ref), channel_id=1, source_target_pairs={{0,32},{16,48},{32,0},{48,16},{64,96},{80,112},{96,64},{112,80},{1... | collective-permute-start | bytes 122888 | tf_op jit(solution)/shard_map/ppermute | solution.py:783
  25.7 0.0 copy-done.2
  25.7 0.7 shard_map.123.after_ref.block_b
  26.4 0.9 %collective-permute-done.5.other_ref.near_ref = f32[40,256]{1,0:T(8,128)S(1)} collective-permute-done((f32[40,256]{1,0:T(8,128)S(1)}, f32[40,256]{1,0:T(8,128)S(1)}, u32[]{:S(2)}, u32[]{:S(2)}) %collective-permute-start.5) | collective-permute-done | bytes 40992 | tf_op jit(solution)/shard_map/ppermute | solution.py:783
  27.4 0.0 copy-start.26
  27.4 0.0 copy-start.28
  27.4 0.0 copy-start.29
  27.4 0.0 copy-start.30
  27.4 0.0 copy-start.31
  27.4 2.6 %collective-permute-start.6 = (f32[56,256]{1,0:T(8,128)S(1)}, f32[56,256]{1,0:T(8,128)S(1)}, u32[]{:S(2)}, u32[]{:S(2)}) collective-permute-start(f32[56,256]{1,0:T(8,128)S(1)} %shard_map.128.mine_ref), channel_id=1, source_target_pairs={{0,96},{16,112},{32,64},{48,80},{64,32},{80,48},{96,0},{112,16},{1... | collective-permute-start | bytes 172040 | tf_op jit(solution)/shard_map/ppermute | solution.py:785
  30.0 0.7 shard_map.124.block_c
  30.7 1.0 %collective-permute-done.6.other_ref = f32[56,256]{1,0:T(8,128)S(1)} collective-permute-done((f32[56,256]{1,0:T(8,128)S(1)}, f32[56,256]{1,0:T(8,128)S(1)}, u32[]{:S(2)}, u32[]{:S(2)}) %collective-permute-start.6) | collective-permute-done | bytes 57376 | tf_op jit(solution)/shard_map/ppermute | solution.py:785
  31.7 0.0 copy-done.22
  31.7 0.0 copy-done.26
  31.7 0.0 copy-done.28
  31.7 0.0 copy-done.29
  31.8 0.0 copy-done.30
  31.8 0.0 copy-done.31
  31.8 2.6 %shard_map.129 = (f32[2,256]{1,0:T(2,128)S(1)}, f32[16,24,256]{2,1,0:T(8,128)}, f32[2,8,512]{2,1,0:T(8,128)}) custom-call(s32[2,8]{1,0:T(2,128)S(1)} %bitcast.135, s32[2,8]{1,0:T(2,128)S(1)} %bitcast.137, f32[2,256]{1,0:T(2,128)S(1)} %shard_map.122.after_ref.block_a, f32[2,256]{1,0:T(2,128)S(1)} %shard_map.123.after_ref.block_b, ...), custom_call_target="tpu_custom_call" | custom-call | tf_op jit(solution)/shard_map/pallas_call | solution.py:865
  34.4 3.6 %all-to-all-start.5 = ((f32[16,24,256]{2,1,0:T(8,128)}), f32[16,24,256]{2,1,0:T(8,128)S(1)}, u32[]{:S(2)}, u32[]{:S(2)}) async-start(f32[16,24,256]{2,1,0:T(8,128)} %get-tuple-element.158), calls=%async_computation.5 | async-start | bytes 786432 | tf_op jit(solution)/shard_map/all_to_all | solution.py:882
  37.9 6.1 %shard_map.133 = (f32[2,4,416,128]{3,2,1,0:T(8,128)S(1)}, f32[2,4,384,128]{3,2,1,0:T(8,128)}, f32[33,8,128]{2,1,0:T(8,128)}) custom-call(f32[2,8,512]{2,1,0:T(8,128)} %get-tuple-element.160.patch_ref, f32[2,4,416,128]{3,2,1,0:T(8,128)S(1)} %get-tuple-element.153.after_ref.wide_in, f32[2,384,512]{2,1,0:T(8,128)} %refs_4_.1, ...), custom_call_target="tpu_custom_call", output_to_operand_aliasing={{0}: (1, {})} | custom-call | tf_op jit(solution)/shard_map/pallas_call | solution.py:884
  44.0 2.1 %all-to-all-done.5.refs_0_.got_ref = f32[16,24,256]{2,1,0:T(8,128)S(1)} async-done(((f32[16,24,256]{2,1,0:T(8,128)}), f32[16,24,256]{2,1,0:T(8,128)S(1)}, u32[]{:S(2)}, u32[]{:S(2)}) %all-to-all-start.5) | async-done | bytes 393248 | tf_op jit(solution)/shard_map/all_to_all | solution.py:882
  46.2 0.0 copy-start.3
  46.2 3.7 %collective-permute-start.7 = (f32[32,256]{1,0:T(8,128)S(1)}, f32[32,256]{1,0:T(8,128)S(1)}, u32[]{:S(2)}, u32[]{:S(2)}) collective-permute-start(f32[32,256]{1,0:T(8,128)S(1)} %get-tuple-element.162.mine_ref), channel_id=1, source_target_pairs={{0,16},{16,0},{32,48},{48,32},{64,80},{80,64},{96,112},{112,96},{1... | collective-permute-start | bytes 98312 | tf_op jit(solution)/shard_map/ppermute | solution.py:781
  49.9 1.6 %shard_map.130.after_ref.block_a = f32[2,256]{1,0:T(2,128)S(1)} custom-call(f32[16,24,256]{2,1,0:T(8,128)S(1)} %all-to-all-done.5.refs_0_.got_ref, f32[1,4096,256]{2,1,0:T(8,128)} %refs_1_.12), custom_call_target="tpu_custom_call" | custom-call | tf_op jit(solution)/shard_map/pallas_call | solution.py:195
  51.5 0.0 collective-permute-done.7.other_ref.core_ref
  51.5 0.1 collective-permute-start.8
  51.6 0.7 shard_map.131.after_ref.block_b
  52.3 2.1 %collective-permute-done.8.other_ref.near_ref = f32[40,256]{1,0:T(8,128)S(1)} collective-permute-done((f32[40,256]{1,0:T(8,128)S(1)}, f32[40,256]{1,0:T(8,128)S(1)}, u32[]{:S(2)}, u32[]{:S(2)}) %collective-permute-start.8) | collective-permute-done | bytes 40992 | tf_op jit(solution)/shard_map/ppermute | solution.py:783
  54.5 0.0 copy-start.23
  54.5 0.0 copy-start.27
  54.5 2.6 %collective-permute-start.9 = (f32[56,256]{1,0:T(8,128)S(1)}, f32[56,256]{1,0:T(8,128)S(1)}, u32[]{:S(2)}, u32[]{:S(2)}) collective-permute-start(f32[56,256]{1,0:T(8,128)S(1)} %shard_map.136.mine_ref), channel_id=1, source_target_pairs={{0,96},{16,112},{32,64},{48,80},{64,32},{80,48},{96,0},{112,16},{1... | collective-permute-start | bytes 172040 | tf_op jit(solution)/shard_map/ppermute | solution.py:785
  57.0 0.7 shard_map.132.block_c
  57.8 1.0 %collective-permute-done.9.other_ref = f32[56,256]{1,0:T(8,128)S(1)} collective-permute-done((f32[56,256]{1,0:T(8,128)S(1)}, f32[56,256]{1,0:T(8,128)S(1)}, u32[]{:S(2)}, u32[]{:S(2)}) %collective-permute-start.9) | collective-permute-done | bytes 57376 | tf_op jit(solution)/shard_map/ppermute | solution.py:785
  58.8 0.0 copy-done
  58.8 0.0 copy-start.11
  58.8 1.3 %shard_map.137 = (f32[2,256]{1,0:T(2,128)S(1)}, f32[2,2,8,512]{3,2,1,0:T(8,128)S(1)}, f32[128,128]{1,0:T(8,128)S(1)}) custom-call(s32[2,8]{1,0:T(2,128)S(1)} %bitcast.136, s32[2,8]{1,0:T(2,128)S(1)} %bitcast.138, f32[2,256]{1,0:T(2,128)S(1)} %shard_map.130.after_ref.block_a, f32[2,256]{1,0:T(2,128)S(1)} %shard_map.131.after_ref.block_b, ...), custom_call_target="tpu_custom_call" | custom-call | tf_op jit(solution)/shard_map/pallas_call | solution.py:195
  60.2 17.7 %all_to_all.31 = f32[128,1,128]{2,1,0:T(1,128)S(1)} all-to-all(f32[128,1,128]{2,1,0:T(1,128)S(1)} %bitcast.125), channel_id=1, replica_groups=mesh['rad'=8,'chan'=16] {'rad','chan'}, dimensions={0} | all-to-all | bytes 131072 | tf_op jit(solution)/shard_map/all_to_all | solution.py:920
  77.8 2.4 %shard_map.138 = (f32[2,256]{1,0:T(2,128)}, f32[2,384,512]{2,1,0:T(8,128)}, f32[2,2,3]{2,1,0:T(2,128)}, f32[1,128]{1,0:T(1,128)}) custom-call(f32[128,128]{1,0:T(8,128)S(1)} %bitcast.123, f32[2,256]{1,0:T(2,128)S(1)} %copy-done.28, f32[2,256]{1,0:T(2,128)S(1)} %get-tuple-element.159.inner_ref.refs_2_, f32[2,256]{1,0:T(2,128)S(1)} %get-tuple-element.167.refs_3_, ...), custom_call_target="tpu_custom_call" | custom-call | tf_op jit(solution)/shard_map/pallas_call | solution.py:922
  80.2 0.7 while.18
  (14 shorter events, 0.1 us)
Async XLA Ops:
  3.0 17.8 %all-to-all-start.4 = ((f32[16,24,256]{2,1,0:T(8,128)}), f32[16,24,256]{2,1,0:T(8,128)S(1)}, u32[]{:S(2)}, u32[]{:S(2)}) async-start(f32[16,24,256]{2,1,0:T(8,128)} %shard_map.121), calls=%async_computation.4 | async-start | bytes 786432 | tf_op jit(solution)/shard_map/all_to_all | solution.py:829
  20.8 4.9 %copy-start.2 = (f32[1,4096,256]{2,1,0:T(8,128)S(1)}, f32[1,4096,256]{2,1,0:T(8,128)}, u32[]{:S(2)}) copy-start(f32[1,4096,256]{2,1,0:T(8,128)} %refs_1_.12) | copy-start | bytes 12582916
  20.9 3.5 %collective-permute-start.4 = (f32[32,256]{1,0:T(8,128)S(1)}, f32[32,256]{1,0:T(8,128)S(1)}, u32[]{:S(2)}, u32[]{:S(2)}) collective-permute-start(f32[32,256]{1,0:T(8,128)S(1)} %get-tuple-element.154.mine_ref), channel_id=1, source_target_pairs={{0,16},{16,0},{32,48},{48,32},{64,80},{80,64},{96,112},{112,96},{1... | collective-permute-start | bytes 98312 | tf_op jit(solution)/shard_map/ppermute | solution.py:781
  24.4 2.9 %collective-permute-start.5 = (f32[40,256]{1,0:T(8,128)S(1)}, f32[40,256]{1,0:T(8,128)S(1)}, u32[]{:S(2)}, u32[]{:S(2)}) collective-permute-start(f32[40,256]{1,0:T(8,128)S(1)} %shard_map.127.mine_ref), channel_id=1, source_target_pairs={{0,32},{16,48},{32,0},{48,16},{64,96},{80,112},{96,64},{112,80},{1... | collective-permute-start | bytes 122888 | tf_op jit(solution)/shard_map/ppermute | solution.py:783
  27.4 4.4 %copy-start.22 = (f32[1,2,512,256]{3,2,1,0:T(8,128)S(1)}, f32[1,2,512,256]{3,2,1,0:T(8,128)}, u32[]{:S(2)}) copy-start(f32[1,2,512,256]{3,2,1,0:T(8,128)} %coupling_ref.3) | copy-start | bytes 3145732
  27.4 4.4 %copy-start.26 = (f32[1,2,256,512]{3,2,1,0:T(8,128)S(1)}, f32[1,2,256,512]{3,2,1,0:T(8,128)}, u32[]{:S(2)}) copy-start(f32[1,2,256,512]{3,2,1,0:T(8,128)} %amp_ref.5) | copy-start | bytes 3145732
  27.4 4.4 %copy-start.28 = (f32[2,256]{1,0:T(2,128)S(1)}, f32[2,256]{1,0:T(2,128)}, u32[]{:S(2)}) copy-start(f32[2,256]{1,0:T(2,128)} %refs_1_.13) | copy-start | bytes 6148
  27.4 4.4 %copy-start.29 = (s32[512]{0:T(512)S(1)}, s32[512]{0:T(512)}, u32[]{:S(2)}) copy-start(s32[512]{0:T(512)} %param.31) | copy-start | bytes 6148
  27.4 4.4 %copy-start.30 = (s32[8,2]{0,1:T(2,128)S(1)}, s32[8,2]{0,1:T(2,128)}, u32[]{:S(2)}) copy-start(s32[8,2]{0,1:T(2,128)} %param.29) | copy-start | bytes 196
  27.4 4.4 %copy-start.31 = (s32[8,2]{0,1:T(2,128)S(1)}, s32[8,2]{0,1:T(2,128)}, u32[]{:S(2)}) copy-start(s32[8,2]{0,1:T(2,128)} %param.30) | copy-start | bytes 196
  27.4 4.3 %collective-permute-start.6 = (f32[56,256]{1,0:T(8,128)S(1)}, f32[56,256]{1,0:T(8,128)S(1)}, u32[]{:S(2)}, u32[]{:S(2)}) collective-permute-start(f32[56,256]{1,0:T(8,128)S(1)} %shard_map.128.mine_ref), channel_id=1, source_target_pairs={{0,96},{16,112},{32,64},{48,80},{64,32},{80,48},{96,0},{112,16},{1... | collective-permute-start | bytes 172040 | tf_op jit(solution)/shard_map/ppermute | solution.py:785
  34.4 11.8 %all-to-all-start.5 = ((f32[16,24,256]{2,1,0:T(8,128)}), f32[16,24,256]{2,1,0:T(8,128)S(1)}, u32[]{:S(2)}, u32[]{:S(2)}) async-start(f32[16,24,256]{2,1,0:T(8,128)} %get-tuple-element.158), calls=%async_computation.5 | async-start | bytes 786432 | tf_op jit(solution)/shard_map/all_to_all | solution.py:882
  46.2 5.4 %copy-start.3 = (f32[1,4096,256]{2,1,0:T(8,128)S(1)}, f32[1,4096,256]{2,1,0:T(8,128)}, u32[]{:S(2)}) copy-start(f32[1,4096,256]{2,1,0:T(8,128)} %refs_1_.12) | copy-start | bytes 12582916
  46.2 5.3 %collective-permute-start.7 = (f32[32,256]{1,0:T(8,128)S(1)}, f32[32,256]{1,0:T(8,128)S(1)}, u32[]{:S(2)}, u32[]{:S(2)}) collective-permute-start(f32[32,256]{1,0:T(8,128)S(1)} %get-tuple-element.162.mine_ref), channel_id=1, source_target_pairs={{0,16},{16,0},{32,48},{48,32},{64,80},{80,64},{96,112},{112,96},{1... | collective-permute-start | bytes 98312 | tf_op jit(solution)/shard_map/ppermute | solution.py:781
  51.5 2.9 %collective-permute-start.8 = (f32[40,256]{1,0:T(8,128)S(1)}, f32[40,256]{1,0:T(8,128)S(1)}, u32[]{:S(2)}, u32[]{:S(2)}) collective-permute-start(f32[40,256]{1,0:T(8,128)S(1)} %shard_map.135.mine_ref), channel_id=1, source_target_pairs={{0,32},{16,48},{32,0},{48,16},{64,96},{80,112},{96,64},{112,80},{1... | collective-permute-start | bytes 122888 | tf_op jit(solution)/shard_map/ppermute | solution.py:783
  54.4 4.4 %copy-start = (f32[2,4,384,128]{3,2,1,0:T(8,128)S(1)}, f32[2,4,384,128]{3,2,1,0:T(8,128)}, u32[]{:S(2)}) copy-start(f32[2,4,384,128]{3,2,1,0:T(8,128)} %get-tuple-element.165.second_ref.refs_6_) | copy-start | bytes 4718596
  54.4 4.4 %copy-start.1 = (f32[33,8,128]{2,1,0:T(8,128)S(1)}, f32[33,8,128]{2,1,0:T(8,128)}, u32[]{:S(2)}) copy-start(f32[33,8,128]{2,1,0:T(8,128)} %get-tuple-element.161.after_ref.notes_ref) | copy-start | bytes 405508
  54.5 4.4 %copy-start.23 = (f32[1,2,512,256]{3,2,1,0:T(8,128)S(1)}, f32[1,2,512,256]{3,2,1,0:T(8,128)}, u32[]{:S(2)}) copy-start(f32[1,2,512,256]{3,2,1,0:T(8,128)} %coupling_ref.3) | copy-start | bytes 3145732
  54.5 4.3 %copy-start.27 = (f32[1,2,256,512]{3,2,1,0:T(8,128)S(1)}, f32[1,2,256,512]{3,2,1,0:T(8,128)}, u32[]{:S(2)}) copy-start(f32[1,2,256,512]{3,2,1,0:T(8,128)} %amp_ref.5) | copy-start | bytes 3145732
  54.5 4.3 %collective-permute-start.9 = (f32[56,256]{1,0:T(8,128)S(1)}, f32[56,256]{1,0:T(8,128)S(1)}, u32[]{:S(2)}, u32[]{:S(2)}) collective-permute-start(f32[56,256]{1,0:T(8,128)S(1)} %shard_map.136.mine_ref), channel_id=1, source_target_pairs={{0,96},{16,112},{32,64},{48,80},{64,32},{80,48},{96,0},{112,16},{1... | collective-permute-start | bytes 172040 | tf_op jit(solution)/shard_map/ppermute | solution.py:785
  58.8 19.0 %copy-start.11 = (f32[2,384,512]{2,1,0:T(8,128)S(1)}, f32[2,384,512]{2,1,0:T(8,128)}, u32[]{:S(2)}) copy-start(f32[2,384,512]{2,1,0:T(8,128)} %refs_4_.1) | copy-start | bytes 4718596

commit v5 on v4

--- a/solution.py
+++ b/solution.py
@@ -227,9 +227,9 @@
     return first[:count] + first[count:] + jnp.dot(high, mix_ref[1], preferred_element_type=jnp.float32)
 
 
-def write_chunk(out_ref, held_ref, written, inner_vec, ghosts, row, others=()):
+def write_chunk(out_ref, inner_vec, ghosts, row, held_ref=None, written=None):
     half = inner_vec.shape[1]
-    held_ref[...] = jnp.concatenate(
+    chunk = jnp.concatenate(
         [
             ghosts[:, :half],
             ghosts[:, half:],
@@ -240,14 +240,18 @@
         ],
         axis=0,
     )
+    if held_ref is None:
+        for strip in range(out_ref.shape[0]):
+            out_ref[strip, 0:16] = chunk
+        return []
+    held_ref[...] = chunk
     copies = [
         pltpu.make_async_copy(held_ref, out_ref.at[strip, pl.ds(0, 16)], written.at[strip])
         for strip in range(out_ref.shape[0])
     ]
     for copy in copies:
         copy.start()
-    for copy in [*others, *copies]:
-        copy.wait()
+    return copies
 
 
 def ghost_rows(inner_vec, amps, member):
@@ -267,38 +271,30 @@
     return last[0] & last[1]
 
 
-def send_ends(chunk_ref, ends_ref, written, first_rows, last_rows):
-    half = ends_ref.shape[2]
-    for end, points in enumerate((last_rows, first_rows)):
-        for k in range(2):
-            for part in range(2):
-                ends_ref[end, 4 * k + 2 * part : 4 * k + 2 * part + 2] = points[part][:, k * half : (k + 1) * half]
-    strips = chunk_ref.shape[0]
-    copies = [
-        pltpu.make_async_copy(
-            ends_ref.at[end],
-            chunk_ref.at[lax.rem(lax.axis_index("chan") + there, strips), pl.ds(16, 8)],
-            written.at[end],
-        )
-        for end, there in enumerate((1, strips - 1))
-    ]
-    for copy in copies:
-        copy.start()
+def send_ends(out_ref, first_rows, last_rows, held_ref=None, written=None):
+    strips, _, half = out_ref.shape
+    copies = []
+    for end, (there, points) in enumerate(((1, last_rows), (strips - 1, first_rows))):
+        both_parts = jnp.concatenate(points, axis=0)
+        rows = jnp.concatenate([both_parts[:, :half], both_parts[:, half:]], axis=0)
+        strip = lax.rem(lax.axis_index("chan") + there, strips)
+        if held_ref is None:
+            out_ref[strip, 16:24] = rows
+        else:
+            held_ref[end] = rows
+            copies.append(pltpu.make_async_copy(held_ref.at[end], out_ref.at[strip, pl.ds(16, 8)], written.at[end]))
+            copies[-1].start()
     return copies
 
 
-def start_kernel(
-    inner_ref, head_ref, tail_ref, amp_ref, group_ref, chunk_ref, held_ref, written, ends_ref, ends_written
-):
-    ends = send_ends(
-        chunk_ref, ends_ref, ends_written, [head_ref[part, 0:2] for part in range(2)], [tail_ref[part, 6:8] for part in range(2)]
-    )
+def start_kernel(inner_ref, head_ref, tail_ref, amp_ref, group_ref, chunk_ref):
+    send_ends(chunk_ref, [head_ref[part, 0:2] for part in range(2)], [tail_ref[part, 6:8] for part in range(2)])
     row = jnp.concatenate([head_ref[part, 0:1] for part in range(2)], axis=0)
     row = jnp.where(at_first(), row, 0.0)
     inner_vec = inner_ref[...]
     amps = [two(amp_ref[0, radius]) for radius in range(2)]
     ghosts = ghost_rows(inner_vec, amps, member_of(group_ref))
-    write_chunk(chunk_ref, held_ref, written, inner_vec, ghosts, row, ends)
+    write_chunk(chunk_ref, inner_vec, ghosts, row)
 
 
 def stencils(window, pot):
@@ -464,7 +460,15 @@
     out_ref[...] = total[0:2] + total[2:4]
 
 
-def gather_kernel(got_ref, after_ref, out_ref, ends_ref):
+def chip_index():
+    return lax.div(lax.axis_index("rad"), 2)
+
+
+def core_index():
+    return lax.rem(lax.axis_index("rad"), 2)
+
+
+def gather_kernel(got_ref, after_ref, out_ref, kept_ref, ends_ref):
     strips = got_ref.shape[0]
     own = lax.axis_index("chan")
     for k in range(4):
@@ -472,37 +476,55 @@
         there = (strip >= 0) & (strip < strips)
         near = got_ref[jnp.clip(strip, 0, strips - 1), 8:10]
         out_ref[2 * k : 2 * k + 2] = jnp.where(there, near, 0.0)
-    out_ref[8:16] = sum(got_ref[strip, 0:8] for strip in range(strips))
-    out_ref[16:20] = got_ref[0, 10:14]
-    out_ref[20:24] = jnp.zeros((4, got_ref.shape[2]), jnp.float32)
+    kept_ref[0:8] = sum(got_ref[strip, 0:8] for strip in range(strips))
+    kept_ref[8:12] = got_ref[0, 10:14]
+    kept_ref[12:16] = jnp.zeros((4, got_ref.shape[2]), jnp.float32)
+    out_ref[8:16] = jnp.where(chip_index() == 0, kept_ref[8:16], kept_ref[0:8])
     before = got_ref[lax.rem(own + strips - 1, strips), 16:24]
     after = got_ref[lax.rem(own + 1, strips), 16:24]
     ends_ref[0], ends_ref[1] = before, after
-    out_ref[24:32] = jnp.where(own == 0, before, after)
-
-
-def join_kernel(mine_ref, other_ref, after_ref, out_ref):
-    count = mine_ref.shape[0] - 24
-    out_ref[0:count] = mine_ref[0:count]
-    out_ref[count : 2 * count] = other_ref[0:count]
-    out_ref[2 * count : 2 * count + 16] = mine_ref[count : count + 16] + other_ref[count : count + 16]
-    keep = (count > 8) | ((lax.rem(lax.axis_index("rad"), 2) == 1) == (lax.axis_index("chan") == 0))
-    out_ref[2 * count + 16 :] = jnp.where(keep, mine_ref[count + 16 :], other_ref[count + 16 :])
-
-
-def join(mine, other, after):
-    shape = (2 * mine.shape[0] - 24, mine.shape[1])
-    return run(join_kernel, [shape], (mine, other, after), [whole()] * 2 + [anywhere()])[0]
-
-
-def inner_result(partners_ref, offsets_ref, block_a, block_b, block_c, inner_ref, mine_ref, other_ref, coupling_ref, amp_ref, member, row):
-    result = block_a[...] + block_b[...] + block_c[...] - shift * inner_ref[...]
+    out_ref[16:24] = jnp.where(own == 0, before, after)
+
+
+def joined(kept_ref, came, add_ghosts, take_row):
+    ghosts = kept_ref[0:8] + jnp.where(add_ghosts, came, 0.0)
+    return ghosts, jnp.where(take_row, came, kept_ref[8:16])
+
+
+def join_kernel(mine_ref, other_ref, kept_ref, after_ref, out_ref, kept_out):
+    chip = chip_index()
+    out_ref[0:8], out_ref[8:16] = mine_ref[0:8], other_ref[0:8]
+    ghosts, row = joined(kept_ref, other_ref[8:16], (chip == 0) | (chip == 3), chip == 1)
+    kept_out[0:8], kept_out[8:16] = ghosts, row
+    out_ref[16:24] = jnp.where(chip <= 1, row, ghosts)
+    out_ref[24:32] = mine_ref[16:24]
+
+
+def last_join_kernel(mine_ref, other_ref, kept_ref, near_ref, after_ref, out_ref, kept_out):
+    chip, core = chip_index(), core_index()
+    out_ref[0:16], out_ref[16:32] = mine_ref[0:16], other_ref[0:16]
+    ghosts, row = joined(kept_ref, other_ref[16:24], chip == 0, chip >= 2)
+    kept_out[0:8], kept_out[8:16] = ghosts, row
+    out_ref[32:40] = jnp.where(core == 0, row, ghosts)
+    is_low = lax.axis_index("chan") == 0
+    from_own = (core == 0) == is_low
+    from_near = (lax.rem(chip, 2) == 1) == is_low
+    out_ref[40:48] = jnp.where(from_own, mine_ref[24:32], jnp.where(from_near, near_ref[16:24], other_ref[24:32]))
+
+
+def join(kernel, count, *args):
+    width = args[0].shape[1]
+    return run(kernel, [(count, width), (16, width)], args, [whole()] * (len(args) - 1) + [anywhere()])
+
+
+def inner_result(partners_ref, offsets_ref, block_a, block_b, inner_ref, mine_ref, other_ref, coupling_ref, amp_ref, member, row):
+    result = block_a[...] + block_b[...] - shift * inner_ref[...]
     couplings, band_width = coupling_ref.shape[1:3]
     block_index = lax.axis_index("rad")
     for couple_index in range(couplings):
         apart = partners_ref[couple_index, block_index] ^ block_index
         far_pair = lax.shift_right_logical(apart, 2)
-        slot = apart ^ (2 * far_pair)
+        slot = 4 * (apart & 1) + lax.shift_right_logical(apart ^ (2 * far_pair), 1)
         rows = pl.ds(pl.multiple_of(lax.rem(slot, 4) * 8, 8), 8)
         near = jnp.where(slot < 4, mine_ref[rows], other_ref[rows])
         near = jnp.concatenate([near[2 * k : 2 * k + 2] for k in range(4)], axis=1)
@@ -513,11 +535,9 @@
     return result + bloch_coef * few_rows_dot(row * member, two(amp_ref[0, 0]), flipped=True)
 
 
-def unpacked(mine_ref, other_ref):
-    sums = mine_ref[32:48] + other_ref[32:48]
-    ghosts = jnp.concatenate([sums[0:4], sums[4:8]], axis=1)
-    row = jnp.concatenate([sums[8:10], sums[10:12]], axis=1)
-    return ghosts, row
+def unpacked(kept_ref, other_ref):
+    ghosts, row = joined(kept_ref, other_ref[32:40], True, core_index() == 1)
+    return jnp.concatenate([ghosts[0:4], ghosts[4:8]], axis=1), jnp.concatenate([row[0:2], row[2:4]], axis=1)
 
 
 def points_of(ref, part, first, count, run_index=0):
@@ -544,13 +564,10 @@
     return image, mixed[32:]
 
 
-def pick_ends(ends_ref, core_ref, near_ref, far_ref):
-    block, strip = lax.axis_index("rad"), lax.axis_index("chan")
-    core, chip = lax.rem(block, 2), lax.div(block, 2)
+def pick_ends(ends_ref, other_ref):
+    strip = lax.axis_index("chan")
     is_low, is_high = strip == 0, strip == lax.axis_size("chan") - 1
-    from_core = (core == 1) == is_low
-    from_near = (lax.rem(chip, 2) == 1) == is_low
-    came = jnp.where(from_core, core_ref[24:32], jnp.where(from_near, near_ref[32:40], far_ref[48:56]))
+    came = other_ref[40:48]
     before = jnp.where(at_first(), 0.0, jnp.where(is_low, came, ends_ref[0]))
     after = jnp.where(at_last(), 0.0, jnp.where(is_high, came, ends_ref[1]))
     return [
@@ -560,13 +577,13 @@
 
 
 def between_kernel(
-    partners_ref, offsets_ref, block_a, block_b, block_c, inner_ref, mine_ref, other_ref, coupling_ref, amp_ref, group_ref,
-    edges_ref, mix_ref, ends_ref, core_ref, near_ref,
-    image_ref, chunk_ref, patch_out, held_ref, written, send_ref, ends_written, patch_ref, patch_written, edge_ref,
+    partners_ref, offsets_ref, block_a, block_b, inner_ref, mine_ref, other_ref, coupling_ref, amp_ref, group_ref,
+    edges_ref, mix_ref, ends_ref, kept_ref,
+    image_ref, chunk_ref, patch_out, held_ref, written, ends_held, ends_written, patch_ref, patch_written, edge_ref,
 ):
     member = member_of(group_ref)
-    ghosts, row = unpacked(mine_ref, other_ref)
-    before, after = pick_ends(ends_ref, core_ref, near_ref, other_ref)
+    ghosts, row = unpacked(kept_ref, other_ref)
+    before, after = pick_ends(ends_ref, other_ref)
     edge_ref[...] = jnp.zeros_like(edge_ref)
     for part in range(2):
         edge_ref[part, 0, 6:8] = before[part]
@@ -594,25 +611,27 @@
         )
     copy = pltpu.make_async_copy(patch_ref, patch_out, patch_written)
     copy.start()
-    copies = [copy] + send_ends(chunk_ref, send_ref, ends_written, first_rows, last_rows)
+    copies = [copy] + send_ends(chunk_ref, first_rows, last_rows, ends_held, ends_written)
     image = inner_result(
-        partners_ref, offsets_ref, block_a, block_b, block_c, inner_ref, mine_ref, other_ref, coupling_ref, amp_ref, member, row
+        partners_ref, offsets_ref, block_a, block_b, inner_ref, mine_ref, other_ref, coupling_ref, amp_ref, member, row
     )
     image_ref[...] = image
     row = jnp.where(at_first(), jnp.concatenate([rows[0:1] for rows in first_rows], axis=0), 0.0)
     amps = [two(amp_ref[0, radius]) for radius in range(2)]
-    write_chunk(chunk_ref, held_ref, written, image, ghost_rows(image, amps, member), row, copies)
+    copies += write_chunk(chunk_ref, image, ghost_rows(image, amps, member), row, held_ref, written)
+    for copy in copies:
+        copy.wait()
 
 
 def last_kernel(
-    partners_ref, offsets_ref, block_a, block_b, block_c, inner_ref, mine_ref, other_ref, coupling_ref, amp_ref, group_ref,
-    wide_ref, mix_ref, ends_ref, core_ref, near_ref, start_ref, second_ref, notes_ref,
+    partners_ref, offsets_ref, block_a, block_b, inner_ref, mine_ref, other_ref, coupling_ref, amp_ref, group_ref,
+    wide_ref, mix_ref, ends_ref, kept_ref, start_ref, second_ref, notes_ref,
     image_ref, out_ref, parts_ref, edge_ref,
 ):
     member = member_of(group_ref)
-    ghosts, row = unpacked(mine_ref, other_ref)
+    ghosts, row = unpacked(kept_ref, other_ref)
     image = inner_result(
-        partners_ref, offsets_ref, block_a, block_b, block_c, inner_ref, mine_ref, other_ref, coupling_ref, amp_ref, member, row
+        partners_ref, offsets_ref, block_a, block_b, inner_ref, mine_ref, other_ref, coupling_ref, amp_ref, member, row
     )
     image_ref[...] = image
     strips = wide_ref.shape[1]
@@ -624,7 +643,7 @@
         ]
         for end in range(2)
     ]
-    before, after = pick_ends(ends_ref, core_ref, near_ref, other_ref)
+    before, after = pick_ends(ends_ref, other_ref)
     edge_ref[...] = jnp.zeros_like(edge_ref)
     for part in range(2):
         ghost = jnp.concatenate([ghosts[2 + part : 3 + part], ghosts[part : part + 1]], axis=0)
@@ -695,94 +714,77 @@
 
 def finish_kernel(
     entries, parts_ref, start_ref, inner_ref, image_ref, state_ref, wide_ref, second_ref, edge_ref,
-    inner_out, outer_out, hess_out, poor_out, coef_ref,
+    inner_out, result_out, hess_out, poor_out, outer_out, written,
 ):
-    step = pl.program_id(0)
-    count = outer_out.shape[1]
     strips, places = second_ref.shape[1:3]
     length = places // 8
-
-    @pl.when(step == 0)
-    def _():
-        sums = jnp.sum(parts_ref[...], axis=0, keepdims=True) * (1.0 / entries)
-        lane = lax.broadcasted_iota(jnp.int32, sums.shape, 1)
-        gram = [jnp.sum(jnp.where(lane == k, sums, 0.0), axis=1, keepdims=True) for k in range(9)]
-        values, (coef_q, coef_p, coef_s), poor = arnoldi_coefs(gram)
-        for k, coef in enumerate([coef_q, *coef_p, *coef_s]):
-            coef_ref[k] = jnp.broadcast_to(coef, (8, lanes))
-        lane = lax.broadcasted_iota(jnp.int32, (1, TERMS + 1), 1)
-        for part in range(2):
-            for column in range(TERMS):
-                line = jnp.zeros((1, TERMS + 1), jnp.float32)
-                for k, value in enumerate(values[part][column]):
-                    line = jnp.where(lane == k, value, line)
-                hess_out[part, column : column + 1] = line
-        poor_out[...] = jnp.broadcast_to(poor, poor_out.shape)
-
-    coefs = coef_ref[0], (coef_ref[1], coef_ref[2]), (coef_ref[3], coef_ref[4])
-    few = count // length
-    for run_index in range(few):
-        own = step * few + run_index
-        for first in range(0, length, 8):
-            rows = pl.ds(pl.multiple_of(own * length + first, 8), 8)
-            for strip in range(strips):
-                result = combined(
-                    coefs,
-                    [state_ref[part, rows, strip * lanes : (strip + 1) * lanes] for part in range(2)],
-                    [wide_ref[part, strip, pl.ds((first + reach) * 8 + own, 8, stride=8)] for part in range(2)],
-                    [second_ref[part, strip, pl.ds(first * 8 + own, 8, stride=8)] for part in range(2)],
-                )
-                for part in range(2):
-                    outer_out[
-                        part,
-                        run_index * length + first : run_index * length + first + 8,
-                        strip * lanes : (strip + 1) * lanes,
-                    ] = result[part]
-
-    def put_end(end):
-        first = 0 if end == 0 else length - 8
-        rows = slice(0, 8) if end == 0 else slice(count - 8, count)
+    sums = jnp.sum(parts_ref[...], axis=0, keepdims=True) * (1.0 / entries)
+    lane = lax.broadcasted_iota(jnp.int32, sums.shape, 1)
+    gram = [jnp.sum(jnp.where(lane == k, sums, 0.0), axis=1, keepdims=True) for k in range(9)]
+    values, (coef_q, coef_p, coef_s), poor = arnoldi_coefs(gram)
+    tile = lambda coef: jnp.broadcast_to(coef, (8, lanes))
+    coefs = tile(coef_q), [tile(coef) for coef in coef_p], [tile(coef) for coef in coef_s]
+
+    def put(rows, p_first, q_first, run_index, edge=None):
         for strip in range(strips):
             here = slice(strip * lanes, (strip + 1) * lanes)
             result = combined(
                 coefs,
-                [state_ref[part, 0:8, here] if end == 0 else state_ref[part, places - 8 : places, here] for part in range(2)],
-                [wide_ref[part, strip, pl.ds((first + reach) * 8 + 7 * end, 8, stride=8)] for part in range(2)],
-                [edge_ref[end, part, :, here] for part in range(2)],
+                [state_ref[part, rows, here] for part in range(2)],
+                [wide_ref[part, strip, pl.ds(p_first * 8 + run_index, 8, stride=8)] for part in range(2)],
+                [
+                    second_ref[part, strip, pl.ds(q_first * 8 + run_index, 8, stride=8)]
+                    if edge is None
+                    else edge_ref[edge, part, :, here]
+                    for part in range(2)
+                ],
             )
             for part in range(2):
                 outer_out[part, rows, here] = result[part]
 
-    @pl.when(step == pl.num_programs(0) - 1)
-    def _():
-        put_end(1)
-
-    @pl.when(step == 0)
-    def _():
-        put_end(0)
-        rows = inner_out.shape[1]
-        for first in range(0, rows, lanes):
-            here = slice(first, first + lanes)
-            result = combined(
-                [coefs[0][0:1], [c[0:1] for c in coefs[1]], [c[0:1] for c in coefs[2]]],
-                *[[ref[0:1, here], ref[1:2, here]] for ref in (start_ref, inner_ref, image_ref)],
-            )
-            for part in range(2):
-                inner_out[part : part + 1, here] = result[part]
+    copies = []
+    for run_index in range(8):
+        for first in range(0, length, 8):
+            row = run_index * length + first
+            edge = 0 if row == 0 else 1 if row == places - 8 else None
+            put(slice(row, row + 8), first + reach, first, run_index, edge)
+        rows = pl.ds(run_index * length, length)
+        copies.append(
+            pltpu.make_async_copy(outer_out.at[:, rows], result_out.at[:, rows], written.at[run_index])
+        )
+        copies[-1].start()
+    for first in range(0, inner_out.shape[1], lanes):
+        here = slice(first, first + lanes)
+        result = combined(
+            [coefs[0][0:1], [c[0:1] for c in coefs[1]], [c[0:1] for c in coefs[2]]],
+            *[[ref[0:1, here], ref[1:2, here]] for ref in (start_ref, inner_ref, image_ref)],
+        )
+        for part in range(2):
+            inner_out[part : part + 1, here] = result[part]
+    lane = lax.broadcasted_iota(jnp.int32, (1, TERMS + 1), 1)
+    for part in range(2):
+        for column in range(TERMS):
+            line = jnp.zeros((1, TERMS + 1), jnp.float32)
+            for k, value in enumerate(values[part][column]):
+                line = jnp.where(lane == k, value, line)
+            hess_out[part, column : column + 1] = line
+    poor_out[...] = jnp.broadcast_to(poor, poor_out.shape)
+    for copy in copies:
+        copy.wait()
 
 
 def same_kernel(in_ref, out_ref):
     out_ref[...] = in_ref[...]
 
 
-def across_blocks(mine, after):
+def across_blocks(mine, kept, after):
     blocks = lax.axis_size("rad")
     last = blocks // 2 - 1
-    core = lax.ppermute(mine, "rad", [(i, i ^ 1) for i in range(blocks)])
-    mine = join(mine, core, after[0])
     near = lax.ppermute(mine, "rad", [(i, i ^ 2) for i in range(blocks)])
-    mine = join(mine, near, after[1])
-    return mine, (core, near, lax.ppermute(mine, "rad", [(i, 2 * (last - i // 2) + i % 2) for i in range(blocks)]))
+    mine, kept = join(join_kernel, 32, mine, near, kept, after[0])
+    other = lax.ppermute(mine, "rad", [(i, 2 * (last - i // 2) + i % 2) for i in range(blocks)])
+    mine, kept = join(last_join_kernel, 48, mine, other, kept, near, after[1])
+    return mine, lax.ppermute(mine, "rad", [(i, i ^ 1) for i in range(blocks)]), kept
 
 
 def body(*inputs):
@@ -809,12 +811,10 @@
     out_strips = channels // lanes
     folded_rows = points + 2 * reach * 8
 
-    ends_scratch = [pltpu.VMEM((2, 8, rows), f32), pltpu.SemaphoreType.DMA((2,))]
-    chunk_scratch = [pltpu.VMEM((16, rows), f32), pltpu.SemaphoreType.DMA((strips,))]
     chunk = pl.pallas_call(
         start_kernel,
         grid=(1,),
-        out_shape=pltpu.HBM((strips, 24, rows), f32),
+        out_shape=jax.ShapeDtypeStruct((strips, 24, rows), f32),
         in_specs=[
             whole(),
             in_one((2, 8, channels)),
@@ -822,8 +822,7 @@
             whole(),
             whole(),
         ],
-        out_specs=far(),
-        scratch_shapes=chunk_scratch + ends_scratch,
+        out_specs=whole(),
         compiler_params=pltpu.CompilerParams(vmem_limit_bytes=vmem_bytes),
     )(inner_state, outer_state, outer_state, surface_amp, group)
     got = lax.all_to_all(chunk, "chan", 0, 0)
@@ -848,20 +847,20 @@
     def block_product(got):
         size = 2 * rows
         parts = []
-        for first, last in ((0, 2), (2, 5), (5, 8)):
+        for first, last in ((0, 4), (4, 8)):
             parts += run(
                 lambda *refs, first=first: block_kernel(first, *refs),
                 [(2, rows)],
-                (got, inner_ham),
-                [whole(), anywhere()],
+                (got, pltpu.with_memory_space_constraint(inner_ham, pltpu.HBM)),
+                [whole(), far()],
                 [pltpu.VMEM((last - first, size, rows), f32), pltpu.SemaphoreType.DMA((last - first,))],
             )
         return parts
 
-    gathered = [(32, rows), (2, 8, rows)]
-    mine, ends = run(gather_kernel, gathered, (got, wide), [whole(), anywhere()])
+    gathered = [(24, rows), (16, rows), (2, 8, rows)]
+    mine, kept, ends = run(gather_kernel, gathered, (got, wide), [whole(), anywhere()])
     block_parts = block_product(got)
-    mine, came = across_blocks(mine, block_parts)
+    mine, other, kept = across_blocks(mine, kept, block_parts)
     p_inner, chunk, patch = pl.pallas_call(
         between_kernel,
         out_shape=[
@@ -869,15 +868,19 @@
             pltpu.HBM((strips, 24, rows), f32),
             pltpu.HBM((2, 8, channels), f32),
         ],
-        in_specs=[scalars()] * 2 + [whole()] * 14,
+        in_specs=[scalars()] * 2 + [whole()] * 12,
         out_specs=[whole()] + [far()] * 2,
-        scratch_shapes=chunk_scratch
-        + ends_scratch
+        scratch_shapes=[
+            pltpu.VMEM((16, rows), f32),
+            pltpu.SemaphoreType.DMA((strips,)),
+            pltpu.VMEM((2, 8, rows), f32),
+            pltpu.SemaphoreType.DMA((2,)),
+        ]
         + [pltpu.VMEM((2, 8, channels), f32), pltpu.SemaphoreType.DMA, pltpu.VMEM((2, 2, 24, channels), f32)],
         compiler_params=pltpu.CompilerParams(vmem_limit_bytes=vmem_bytes),
     )(
-        *by_coupling, *block_parts, inner_state, mine, came[2], inner_coupling, surface_amp, group,
-        edges, mix, ends, came[0], came[1],
+        *by_coupling, *block_parts, inner_state, mine, other, inner_coupling, surface_amp, group,
+        edges, mix, ends, kept,
     )
     got = lax.all_to_all(chunk, "chan", 0, 0)
     q_shape, notes_shape = (2, out_strips, points, lanes), (9 + 6 * out_strips, 8, lanes)
@@ -902,38 +905,33 @@
         input_output_aliases={1: 0},
         compiler_params=pltpu.CompilerParams(vmem_limit_bytes=vmem_bytes),
     )(pltpu.with_memory_space_constraint(patch, pltpu.HBM), wide, outer_state, potential, mix)
-    mine, ends = run(
+    mine, kept, ends = run(
         gather_kernel, gathered, (got, pltpu.with_memory_space_constraint(notes, pltpu.HBM)), [whole(), far()]
     )
     block_parts = block_product(got)
-    mine, came = across_blocks(mine, block_parts)
+    mine, other, kept = across_blocks(mine, kept, block_parts)
     q_inner, q_ends, parts = run(
         last_kernel,
         [(2, rows), (2, 2, 8, channels), (count, lanes)],
         (
-            *by_coupling, *block_parts, p_inner, mine, came[2], inner_coupling, surface_amp, group,
-            wide, mix, ends, came[0], came[1], inner_state, second, notes,
+            *by_coupling, *block_parts, p_inner, mine, other, inner_coupling, surface_amp, group,
+            wide, mix, ends, kept, inner_state, second, notes,
         ),
-        [scalars()] * 2 + [whole()] * 17,
+        [scalars()] * 2 + [whole()] * 15,
         [pltpu.VMEM((2, 2, 24, channels), f32)],
     )
     parts = lax.all_to_all(parts.reshape(count, 1, lanes), both, 0, 0).reshape(count, lanes)
-    steps = 4
     last_inner, last_outer, columns, poor = pl.pallas_call(
         lambda *refs: finish_kernel(entries, *refs),
-        grid=(steps,),
         out_shape=[
-            jax.ShapeDtypeStruct(shape, f32)
-            for shape in ((2, rows), (2, points, channels), (2, TERMS, TERMS + 1), (1, lanes))
+            jax.ShapeDtypeStruct((2, rows), f32),
+            pltpu.HBM((2, points, channels), f32),
+            jax.ShapeDtypeStruct((2, TERMS, TERMS + 1), f32),
+            jax.ShapeDtypeStruct((1, lanes), f32),
         ],
         in_specs=[whole()] * 8,
-        out_specs=[
-            pl.BlockSpec((2, rows), lambda step: (0, 0)),
-            pl.BlockSpec((2, points // steps, channels), lambda step: (0, step, 0)),
-            pl.BlockSpec((2, TERMS, TERMS + 1), lambda step: (0, 0, 0)),
-            pl.BlockSpec((1, lanes), lambda step: (0, 0)),
-        ],
-        scratch_shapes=[pltpu.VMEM((5, 8, lanes), f32)],
+        out_specs=[whole(), far(), whole(), whole()],
+        scratch_shapes=[pltpu.VMEM((2, points, channels), f32), pltpu.SemaphoreType.DMA((8,))],
         compiler_params=pltpu.CompilerParams(vmem_limit_bytes=vmem_bytes),
     )(parts, inner_state, p_inner, q_inner, outer_state, wide, second, q_ends)
 

time: 81.5 us -> 80 us (0.982)
  blocking collectives: 17.7 us -> 14.7 us
  Pallas kernels: 26 us -> 27.4 us
  waiting for transfers between devices: 11.2 us -> 10 us
  starting transfers between devices: 24.3 us -> 25.4 us
    all_to_all x1, blocking collectives: 17.7 us -> 14.7 us  [body(): lax.all_to_all(parts.reshape(count, 1, lanes), both, 0, 0)]
    ppermute x2, waiting for transfers between devices: 3.02 us -> 0.78 us  [across_blocks(): near = lax.ppermute(mine, 'rad', [(i, i ^ 2) for i in range(blocks)])]
    ppermute x2, waiting for transfers between devices: 2.07 us -> 0.07 us  [across_blocks(): lax.ppermute(mine, 'rad', [(i, 2 * (last - i // 2) + i % 2) for i in rang...]
    ppermute x2, waiting for transfers between devices: 0.01 us -> 1.76 us  [across_blocks(): lax.ppermute(mine, 'rad', [(i, i ^ 1) for i in range(blocks)])]
    ppermute x2, starting transfers between devices: 5.64 us -> 7.23 us  [across_blocks(): lax.ppermute(mine, 'rad', [(i, i ^ 1) for i in range(blocks)])]
    pallas_call x13 -> x11, Pallas kernels: 7.42 us -> 8.95 us  [run(): pl.pallas_call(kernel, out_shape=[jax.ShapeDtypeStruct(*out) if isinstanc...]
    all_to_all x2, waiting for transfers between devices: 6.14 us -> 7.44 us  [body(): got = lax.all_to_all(chunk, 'chan', 0, 0)]
  transfers between devices with their start and end apart: 8 -> 8, of which waited for: 6 -> 6; matrix products, arithmetic and copies ran while one was open for 0% -> 0% of each run, Pallas kernels for 21% -> 24%
where the time goes in v5:
time: 80 us; the launch traced here: 79.5 us
  Pallas kernels  27.4 us (34%)
  starting transfers between devices  25.4 us (32%)
  blocking collectives  14.7 us (18%)
  waiting for transfers between devices  10 us (12%)
  between operations  1.05 us (1%)
  loops' own time  0.81 us (1%)
    all_to_all x1, blocking collectives, body(): lax.all_to_all(parts.reshape(count, 1, lanes), both, 0, 0)  14.7 us
    all_to_all x2, starting transfers between devices, body(): got = lax.all_to_all(chunk, 'chan', 0, 0)  12.2 us
    pallas_call x11, Pallas kernels, run(): pl.pallas_call(kernel, out_shape=[jax.ShapeDtypeStruct(*out) if isinstanc...  8.95 us
    all_to_all x2, waiting for transfers between devices, body(): got = lax.all_to_all(chunk, 'chan', 0, 0)  7.44 us
    ppermute x2, starting transfers between devices, across_blocks(): lax.ppermute(mine, 'rad', [(i, i ^ 1) for i in range(blocks)])  7.23 us
    pallas_call x1, Pallas kernels, body(): pl.pallas_call(second_outer_kernel, grid=(1,), out_shape=[jax.ShapeDtypeS...  6.11 us
    pallas_call x1, Pallas kernels, body(): pl.pallas_call(first_outer_kernel, out_shape=[jax.ShapeDtypeStruct((2, ou...  5.14 us
    ppermute x2, starting transfers between devices, across_blocks(): lax.ppermute(mine, 'rad', [(i, 2 * (last - i // 2) + i % 2) for i in rang...  4.66 us
  transfers between devices with their start and end apart: 8, of which 6 were waited for; matrix products, arithmetic and copies ran while one was open for 0% of the time, Pallas kernels for 24%

profile of v5, /device:TPU:1, one launch (start us, length us, event | category | flops | bytes accessed | tf_op | source)
XLA Modules:
  0.0 79.5 jit_solution(3646453980190669902)
XLA Ops:
  0.6 2.3 %shard_map.121 = f32[16,24,256]{2,1,0:T(8,128)} custom-call(f32[2,256]{1,0:T(2,128)} %refs_1_.9, f32[2,384,512]{2,1,0:T(8,128)} %refs_4_.1, f32[2,384,512]{2,1,0:T(8,128)} %refs_4_.1, f32[1,2,256,512]{3,2,1,0:T(8,128)} %amp_ref.5, s32[1,512]{1,0:T(1,128)} %bitcast.132), custom_call_target="tpu_custom_call" | custom-call | tf_op jit(solution)/shard_map/pallas_call | solution.py:814
  2.9 8.6 %all-to-all-start.4 = ((f32[16,24,256]{2,1,0:T(8,128)}), f32[16,24,256]{2,1,0:T(8,128)S(1)}, u32[]{:S(2)}, u32[]{:S(2)}) async-start(f32[16,24,256]{2,1,0:T(8,128)} %shard_map.121), calls=%async_computation.4 | async-start | bytes 786432 | tf_op jit(solution)/shard_map/all_to_all | solution.py:828
  11.5 5.1 %shard_map.124 = (f32[2,4,416,128]{3,2,1,0:T(8,128)S(1)}, bf16[2,512,512]{2,1,0:T(8,128)(2,1)S(1)}, f32[2,3,8,512]{3,2,1,0:T(8,128)S(1)}) custom-call(f32[2,384,512]{2,1,0:T(8,128)} %refs_4_.1, f32[384,512]{1,0:T(8,128)} %pot_in.1, f32[512,512]{1,0:T(8,128)} %mix_ref.1), custom_call_target="tpu_custom_call" | custom-call | tf_op jit(solution)/shard_map/pallas_call | solution.py:829
  16.7 4.0 %all-to-all-done.4.refs_0_.got_ref = f32[16,24,256]{2,1,0:T(8,128)S(1)} async-done(((f32[16,24,256]{2,1,0:T(8,128)}), f32[16,24,256]{2,1,0:T(8,128)S(1)}, u32[]{:S(2)}, u32[]{:S(2)}) %all-to-all-start.4) | async-done | bytes 393248 | tf_op jit(solution)/shard_map/all_to_all | solution.py:828
  20.7 1.3 %collective-permute-start.4 = (f32[24,256]{1,0:T(8,128)S(1)}, f32[24,256]{1,0:T(8,128)S(1)}, u32[]{:S(2)}, u32[]{:S(2)}) collective-permute-start(f32[24,256]{1,0:T(8,128)S(1)} %get-tuple-element.164.mine_ref), channel_id=1, source_target_pairs={{0,32},{16,48},{32,0},{48,16},{64,96},{80,112},{96,64},{112,80},{1... | collective-permute-start | bytes 73736 | tf_op jit(solution)/shard_map/ppermute | solution.py:783
  22.0 1.9 %shard_map.122.after_ref.block_a = f32[2,256]{1,0:T(2,128)S(1)} custom-call(f32[16,24,256]{2,1,0:T(8,128)S(1)} %all-to-all-done.4.refs_0_.got_ref, f32[1,4096,256]{2,1,0:T(8,128)} %refs_1_.8), custom_call_target="tpu_custom_call" | custom-call | tf_op jit(solution)/shard_map/pallas_call | solution.py:195
  23.9 0.0 collective-permute-done.4.other_ref.near_ref
  24.0 0.0 copy-start.20
  24.0 0.0 copy-start.24
  24.0 0.0 copy-start.26
  24.0 0.0 copy-start.27
  24.0 0.0 copy-start.28
  24.0 0.0 copy-start.29
  24.0 2.1 %collective-permute-start.5 = (f32[32,256]{1,0:T(8,128)S(1)}, f32[32,256]{1,0:T(8,128)S(1)}, u32[]{:S(2)}, u32[]{:S(2)}) collective-permute-start(f32[32,256]{1,0:T(8,128)S(1)} %get-tuple-element.166.mine_ref), channel_id=1, source_target_pairs={{0,96},{16,112},{32,64},{48,80},{64,32},{80,48},{96,0},{112,16},{1... | collective-permute-start | bytes 98312 | tf_op jit(solution)/shard_map/ppermute | solution.py:785
  26.1 1.9 %shard_map.123.after_ref.block_b = f32[2,256]{1,0:T(2,128)S(1)} custom-call(f32[16,24,256]{2,1,0:T(8,128)S(1)} %all-to-all-done.4.refs_0_.got_ref, f32[1,4096,256]{2,1,0:T(8,128)} %refs_1_.8), custom_call_target="tpu_custom_call" | custom-call | tf_op jit(solution)/shard_map/pallas_call | solution.py:195
  28.0 0.1 collective-permute-done.5.other_ref
  28.1 3.8 %collective-permute-start.6 = (f32[48,256]{1,0:T(8,128)S(1)}, f32[48,256]{1,0:T(8,128)S(1)}, u32[]{:S(2)}, u32[]{:S(2)}) collective-permute-start(f32[48,256]{1,0:T(8,128)S(1)} %get-tuple-element.168.mine_ref), channel_id=1, source_target_pairs={{0,16},{16,0},{32,48},{48,32},{64,80},{80,64},{96,112},{112,96},{1... | collective-permute-start | bytes 147464 | tf_op jit(solution)/shard_map/ppermute | solution.py:787
  31.9 0.9 %collective-permute-done.6.other_ref = f32[48,256]{1,0:T(8,128)S(1)} collective-permute-done((f32[48,256]{1,0:T(8,128)S(1)}, f32[48,256]{1,0:T(8,128)S(1)}, u32[]{:S(2)}, u32[]{:S(2)}) %collective-permute-start.6) | collective-permute-done | bytes 49184 | tf_op jit(solution)/shard_map/ppermute | solution.py:787
  32.8 0.0 copy-done.20
  32.8 0.0 copy-done.24
  32.8 0.0 copy-done.26
  32.8 0.0 copy-done.27
  32.8 0.0 copy-done.28
  32.8 0.0 copy-done.29
  32.8 2.6 %shard_map.128 = (f32[2,256]{1,0:T(2,128)S(1)}, f32[16,24,256]{2,1,0:T(8,128)}, f32[2,8,512]{2,1,0:T(8,128)}) custom-call(s32[2,8]{1,0:T(2,128)S(1)} %bitcast.135, s32[2,8]{1,0:T(2,128)S(1)} %bitcast.137, f32[2,256]{1,0:T(2,128)S(1)} %shard_map.122.after_ref.block_a, f32[2,256]{1,0:T(2,128)S(1)} %shard_map.123.after_ref.block_b, f32[2,256]{1,0:T(2,128)S(1)} %copy-done.26, ...), custom_call_target="tpu_custom_call" | custom-call | tf_op jit(solution)/shard_map/pallas_call | solution.py:864
  35.4 3.6 %all-to-all-start.5 = ((f32[16,24,256]{2,1,0:T(8,128)}), f32[16,24,256]{2,1,0:T(8,128)S(1)}, u32[]{:S(2)}, u32[]{:S(2)}) async-start(f32[16,24,256]{2,1,0:T(8,128)} %get-tuple-element.173), calls=%async_computation.5 | async-start | bytes 786432 | tf_op jit(solution)/shard_map/all_to_all | solution.py:885
  39.0 6.1 %shard_map.131 = (f32[2,4,416,128]{3,2,1,0:T(8,128)S(1)}, f32[2,4,384,128]{3,2,1,0:T(8,128)}, f32[33,8,128]{2,1,0:T(8,128)}) custom-call(f32[2,8,512]{2,1,0:T(8,128)} %get-tuple-element.175.patch_ref, f32[2,4,416,128]{3,2,1,0:T(8,128)S(1)} %get-tuple-element.163.after_ref.wide_in, f32[2,384,512]{2,1,0:T(8,128)} %refs_4_.1, ...), custom_call_target="tpu_custom_call", output_to_operand_aliasing={{0}: (1, {})} | custom-call | tf_op jit(solution)/shard_map/pallas_call | solution.py:887
  45.1 3.4 %all-to-all-done.5.refs_0_.got_ref = f32[16,24,256]{2,1,0:T(8,128)S(1)} async-done(((f32[16,24,256]{2,1,0:T(8,128)}), f32[16,24,256]{2,1,0:T(8,128)S(1)}, u32[]{:S(2)}, u32[]{:S(2)}) %all-to-all-start.5) | async-done | bytes 393248 | tf_op jit(solution)/shard_map/all_to_all | solution.py:885
  48.5 0.1 collective-permute-start.7
  48.6 1.9 %shard_map.129.after_ref.block_a = f32[2,256]{1,0:T(2,128)S(1)} custom-call(f32[16,24,256]{2,1,0:T(8,128)S(1)} %all-to-all-done.5.refs_0_.got_ref, f32[1,4096,256]{2,1,0:T(8,128)} %refs_1_.8), custom_call_target="tpu_custom_call" | custom-call | tf_op jit(solution)/shard_map/pallas_call | solution.py:195
  50.5 0.8 collective-permute-done.7.other_ref.near_ref
  51.3 0.0 copy-start.1
  51.3 0.0 copy-start.21
  51.3 0.0 copy-start.25
  51.3 2.6 %collective-permute-start.8 = (f32[32,256]{1,0:T(8,128)S(1)}, f32[32,256]{1,0:T(8,128)S(1)}, u32[]{:S(2)}, u32[]{:S(2)}) collective-permute-start(f32[32,256]{1,0:T(8,128)S(1)} %get-tuple-element.179.mine_ref), channel_id=1, source_target_pairs={{0,96},{16,112},{32,64},{48,80},{64,32},{80,48},{96,0},{112,16},{1... | collective-permute-start | bytes 98312 | tf_op jit(solution)/shard_map/ppermute | solution.py:785
  53.9 1.9 %shard_map.130.after_ref.block_b = f32[2,256]{1,0:T(2,128)S(1)} custom-call(f32[16,24,256]{2,1,0:T(8,128)S(1)} %all-to-all-done.5.refs_0_.got_ref, f32[1,4096,256]{2,1,0:T(8,128)} %refs_1_.8), custom_call_target="tpu_custom_call" | custom-call | tf_op jit(solution)/shard_map/pallas_call | solution.py:195
  55.8 0.0 collective-permute-done.8.other_ref
  55.8 3.4 %collective-permute-start.9 = (f32[48,256]{1,0:T(8,128)S(1)}, f32[48,256]{1,0:T(8,128)S(1)}, u32[]{:S(2)}, u32[]{:S(2)}) collective-permute-start(f32[48,256]{1,0:T(8,128)S(1)} %get-tuple-element.181.mine_ref), channel_id=1, source_target_pairs={{0,16},{16,0},{32,48},{48,32},{64,80},{80,64},{96,112},{112,96},{1... | collective-permute-start | bytes 147464 | tf_op jit(solution)/shard_map/ppermute | solution.py:787
  59.3 0.9 %collective-permute-done.9.other_ref = f32[48,256]{1,0:T(8,128)S(1)} collective-permute-done((f32[48,256]{1,0:T(8,128)S(1)}, f32[48,256]{1,0:T(8,128)S(1)}, u32[]{:S(2)}, u32[]{:S(2)}) %collective-permute-start.9) | collective-permute-done | bytes 49184 | tf_op jit(solution)/shard_map/ppermute | solution.py:787
  60.2 0.0 copy-done
  60.2 0.0 copy-done.1
  60.2 0.0 copy-done.21
  60.2 0.0 copy-done.25
  60.2 0.0 copy-start.9
  60.2 1.3 %shard_map.135 = (f32[2,256]{1,0:T(2,128)S(1)}, f32[2,2,8,512]{3,2,1,0:T(8,128)S(1)}, f32[128,128]{1,0:T(8,128)S(1)}) custom-call(s32[2,8]{1,0:T(2,128)S(1)} %bitcast.136, s32[2,8]{1,0:T(2,128)S(1)} %bitcast.138, f32[2,256]{1,0:T(2,128)S(1)} %shard_map.129.after_ref.block_a, f32[2,256]{1,0:T(2,128)S(1)} %shard_map.130.after_ref.block_b, ...), custom_call_target="tpu_custom_call" | custom-call | tf_op jit(solution)/shard_map/pallas_call | solution.py:195
  61.5 14.7 %all_to_all.31 = f32[128,1,128]{2,1,0:T(1,128)S(1)} all-to-all(f32[128,1,128]{2,1,0:T(1,128)S(1)} %bitcast.125), channel_id=1, replica_groups=mesh['rad'=8,'chan'=16] {'rad','chan'}, dimensions={0} | all-to-all | bytes 131072 | tf_op jit(solution)/shard_map/all_to_all | solution.py:923
  76.2 2.3 %shard_map.136 = (f32[2,256]{1,0:T(2,128)}, f32[2,384,512]{2,1,0:T(8,128)}, f32[2,2,3]{2,1,0:T(2,128)}, f32[1,128]{1,0:T(1,128)}) custom-call(f32[128,128]{1,0:T(8,128)S(1)} %bitcast.123, f32[2,256]{1,0:T(2,128)S(1)} %copy-done.26, f32[2,256]{1,0:T(2,128)S(1)} %get-tuple-element.174.inner_ref.refs_2_, f32[2,256]{1,0:T(2,128)S(1)} %get-tuple-element.187.refs_3_, ...), custom_call_target="tpu_custom_call" | custom-call | tf_op jit(solution)/shard_map/pallas_call | solution.py:924
  78.6 0.8 %while.18 = (f32[]{:T(128)}, f32[2,256]{1,0:T(2,128)}, f32[2,384,512]{2,1,0:T(8,128)}, f32[2,2,3]{2,1,0:T(2,128)}, f32[2,256]{1,0:T(2,128)S(1)}, /*index=5*/f32[...) while((f32[]{:T(128)}, f32[2,256]{1,0:T(2,128)}, ...), condition=%region_29.30_spmd, body=%region_0.29_spmd | while | flops 4953002496 | bytes 191500976 | solution.py:944
  (8 shorter events, 0.1 us)
Async XLA Ops:
  2.9 17.8 %all-to-all-start.4 = ((f32[16,24,256]{2,1,0:T(8,128)}), f32[16,24,256]{2,1,0:T(8,128)S(1)}, u32[]{:S(2)}, u32[]{:S(2)}) async-start(f32[16,24,256]{2,1,0:T(8,128)} %shard_map.121), calls=%async_computation.4 | async-start | bytes 786432 | tf_op jit(solution)/shard_map/all_to_all | solution.py:828
  20.7 3.2 %collective-permute-start.4 = (f32[24,256]{1,0:T(8,128)S(1)}, f32[24,256]{1,0:T(8,128)S(1)}, u32[]{:S(2)}, u32[]{:S(2)}) collective-permute-start(f32[24,256]{1,0:T(8,128)S(1)} %get-tuple-element.164.mine_ref), channel_id=1, source_target_pairs={{0,32},{16,48},{32,0},{48,16},{64,96},{80,112},{96,64},{112,80},{1... | collective-permute-start | bytes 73736 | tf_op jit(solution)/shard_map/ppermute | solution.py:783
  24.0 8.8 %copy-start.20 = (f32[1,2,512,256]{3,2,1,0:T(8,128)S(1)}, f32[1,2,512,256]{3,2,1,0:T(8,128)}, u32[]{:S(2)}) copy-start(f32[1,2,512,256]{3,2,1,0:T(8,128)} %coupling_ref.3) | copy-start | bytes 3145732
  24.0 8.8 %copy-start.24 = (f32[1,2,256,512]{3,2,1,0:T(8,128)S(1)}, f32[1,2,256,512]{3,2,1,0:T(8,128)}, u32[]{:S(2)}) copy-start(f32[1,2,256,512]{3,2,1,0:T(8,128)} %amp_ref.5) | copy-start | bytes 3145732
  24.0 8.8 %copy-start.26 = (f32[2,256]{1,0:T(2,128)S(1)}, f32[2,256]{1,0:T(2,128)}, u32[]{:S(2)}) copy-start(f32[2,256]{1,0:T(2,128)} %refs_1_.9) | copy-start | bytes 6148
  24.0 8.8 %copy-start.27 = (s32[512]{0:T(512)S(1)}, s32[512]{0:T(512)}, u32[]{:S(2)}) copy-start(s32[512]{0:T(512)} %param.31) | copy-start | bytes 6148
  24.0 8.8 %copy-start.28 = (s32[8,2]{0,1:T(2,128)S(1)}, s32[8,2]{0,1:T(2,128)}, u32[]{:S(2)}) copy-start(s32[8,2]{0,1:T(2,128)} %param.29) | copy-start | bytes 196
  24.0 8.8 %copy-start.29 = (s32[8,2]{0,1:T(2,128)S(1)}, s32[8,2]{0,1:T(2,128)}, u32[]{:S(2)}) copy-start(s32[8,2]{0,1:T(2,128)} %param.30) | copy-start | bytes 196
  24.0 4.1 %collective-permute-start.5 = (f32[32,256]{1,0:T(8,128)S(1)}, f32[32,256]{1,0:T(8,128)S(1)}, u32[]{:S(2)}, u32[]{:S(2)}) collective-permute-start(f32[32,256]{1,0:T(8,128)S(1)} %get-tuple-element.166.mine_ref), channel_id=1, source_target_pairs={{0,96},{16,112},{32,64},{48,80},{64,32},{80,48},{96,0},{112,16},{1... | collective-permute-start | bytes 98312 | tf_op jit(solution)/shard_map/ppermute | solution.py:785
  28.1 4.7 %collective-permute-start.6 = (f32[48,256]{1,0:T(8,128)S(1)}, f32[48,256]{1,0:T(8,128)S(1)}, u32[]{:S(2)}, u32[]{:S(2)}) collective-permute-start(f32[48,256]{1,0:T(8,128)S(1)} %get-tuple-element.168.mine_ref), channel_id=1, source_target_pairs={{0,16},{16,0},{32,48},{48,32},{64,80},{80,64},{96,112},{112,96},{1... | collective-permute-start | bytes 147464 | tf_op jit(solution)/shard_map/ppermute | solution.py:787
  35.4 13.1 %all-to-all-start.5 = ((f32[16,24,256]{2,1,0:T(8,128)}), f32[16,24,256]{2,1,0:T(8,128)S(1)}, u32[]{:S(2)}, u32[]{:S(2)}) async-start(f32[16,24,256]{2,1,0:T(8,128)} %get-tuple-element.173), calls=%async_computation.5 | async-start | bytes 786432 | tf_op jit(solution)/shard_map/all_to_all | solution.py:885
  48.5 2.8 %collective-permute-start.7 = (f32[24,256]{1,0:T(8,128)S(1)}, f32[24,256]{1,0:T(8,128)S(1)}, u32[]{:S(2)}, u32[]{:S(2)}) collective-permute-start(f32[24,256]{1,0:T(8,128)S(1)} %get-tuple-element.177.mine_ref), channel_id=1, source_target_pairs={{0,32},{16,48},{32,0},{48,16},{64,96},{80,112},{96,64},{112,80},{1... | collective-permute-start | bytes 73736 | tf_op jit(solution)/shard_map/ppermute | solution.py:783
  51.3 8.9 %copy-start = (f32[2,4,384,128]{3,2,1,0:T(8,128)S(1)}, f32[2,4,384,128]{3,2,1,0:T(8,128)}, u32[]{:S(2)}) copy-start(f32[2,4,384,128]{3,2,1,0:T(8,128)} %get-tuple-element.185.second_ref.refs_6_) | copy-start | bytes 4718596
  51.3 8.9 %copy-start.1 = (f32[33,8,128]{2,1,0:T(8,128)S(1)}, f32[33,8,128]{2,1,0:T(8,128)}, u32[]{:S(2)}) copy-start(f32[33,8,128]{2,1,0:T(8,128)} %get-tuple-element.176.after_ref.notes_ref) | copy-start | bytes 405508
  51.3 8.8 %copy-start.21 = (f32[1,2,512,256]{3,2,1,0:T(8,128)S(1)}, f32[1,2,512,256]{3,2,1,0:T(8,128)}, u32[]{:S(2)}) copy-start(f32[1,2,512,256]{3,2,1,0:T(8,128)} %coupling_ref.3) | copy-start | bytes 3145732
  51.3 8.8 %copy-start.25 = (f32[1,2,256,512]{3,2,1,0:T(8,128)S(1)}, f32[1,2,256,512]{3,2,1,0:T(8,128)}, u32[]{:S(2)}) copy-start(f32[1,2,256,512]{3,2,1,0:T(8,128)} %amp_ref.5) | copy-start | bytes 3145732
  51.3 4.4 %collective-permute-start.8 = (f32[32,256]{1,0:T(8,128)S(1)}, f32[32,256]{1,0:T(8,128)S(1)}, u32[]{:S(2)}, u32[]{:S(2)}) collective-permute-start(f32[32,256]{1,0:T(8,128)S(1)} %get-tuple-element.179.mine_ref), channel_id=1, source_target_pairs={{0,96},{16,112},{32,64},{48,80},{64,32},{80,48},{96,0},{112,16},{1... | collective-permute-start | bytes 98312 | tf_op jit(solution)/shard_map/ppermute | solution.py:785
  55.8 4.3 %collective-permute-start.9 = (f32[48,256]{1,0:T(8,128)S(1)}, f32[48,256]{1,0:T(8,128)S(1)}, u32[]{:S(2)}, u32[]{:S(2)}) collective-permute-start(f32[48,256]{1,0:T(8,128)S(1)} %get-tuple-element.181.mine_ref), channel_id=1, source_target_pairs={{0,16},{16,0},{32,48},{48,32},{64,80},{80,64},{96,112},{112,96},{1... | collective-permute-start | bytes 147464 | tf_op jit(solution)/shard_map/ppermute | solution.py:787
  60.2 16.1 %copy-start.9 = (f32[2,384,512]{2,1,0:T(8,128)S(1)}, f32[2,384,512]{2,1,0:T(8,128)}, u32[]{:S(2)}) copy-start(f32[2,384,512]{2,1,0:T(8,128)} %refs_4_.1) | copy-start | bytes 4718596

commit v6 on v5

--- a/solution.py
+++ b/solution.py
@@ -13,7 +13,7 @@
 slope_coef = 1.0 / (12.0 * 0.25)
 bloch_coef = 2.0
 shift = 1.5
-least_left = 0.02
+least_left = 0.1
 both = ("rad", "chan")
 
 

time: 80 us -> 80 us (level)
  no operation moved by 1% of the time
where the time goes in v6:
time: 80 us; the launch traced here: 79.5 us
  Pallas kernels  27.4 us (34%)
  starting transfers between devices  25.4 us (32%)
  blocking collectives  14.7 us (18%)
  waiting for transfers between devices  10 us (12%)
  between operations  1.05 us (1%)
  loops' own time  0.81 us (1%)
    all_to_all x1, blocking collectives, body(): lax.all_to_all(parts.reshape(count, 1, lanes), both, 0, 0)  14.7 us
    all_to_all x2, starting transfers between devices, body(): got = lax.all_to_all(chunk, 'chan', 0, 0)  12.2 us
    pallas_call x11, Pallas kernels, run(): pl.pallas_call(kernel, out_shape=[jax.ShapeDtypeStruct(*out) if isinstanc...  8.95 us
    all_to_all x2, waiting for transfers between devices, body(): got = lax.all_to_all(chunk, 'chan', 0, 0)  7.44 us
    ppermute x2, starting transfers between devices, across_blocks(): lax.ppermute(mine, 'rad', [(i, i ^ 1) for i in range(blocks)])  7.23 us
    pallas_call x1, Pallas kernels, body(): pl.pallas_call(second_outer_kernel, grid=(1,), out_shape=[jax.ShapeDtypeS...  6.11 us
    pallas_call x1, Pallas kernels, body(): pl.pallas_call(first_outer_kernel, out_shape=[jax.ShapeDtypeStruct((2, ou...  5.14 us
    ppermute x2, starting transfers between devices, across_blocks(): lax.ppermute(mine, 'rad', [(i, 2 * (last - i // 2) + i % 2) for i in rang...  4.66 us
  transfers between devices with their start and end apart: 8, of which 6 were waited for; matrix products, arithmetic and copies ran while one was open for 0% of the time, Pallas kernels for 24%

profile of v6, /device:TPU:1, one launch (start us, length us, event | category | flops | bytes accessed | tf_op | source)
XLA Modules:
  0.0 79.5 jit_solution(6735521433217492102)
XLA Ops:
  0.6 2.3 %shard_map.121 = f32[16,24,256]{2,1,0:T(8,128)} custom-call(f32[2,256]{1,0:T(2,128)} %refs_1_.9, f32[2,384,512]{2,1,0:T(8,128)} %refs_4_.1, f32[2,384,512]{2,1,0:T(8,128)} %refs_4_.1, f32[1,2,256,512]{3,2,1,0:T(8,128)} %amp_ref.5, s32[1,512]{1,0:T(1,128)} %bitcast.132), custom_call_target="tpu_custom_call" | custom-call | tf_op jit(solution)/shard_map/pallas_call | solution.py:814
  2.9 8.6 %all-to-all-start.4 = ((f32[16,24,256]{2,1,0:T(8,128)}), f32[16,24,256]{2,1,0:T(8,128)S(1)}, u32[]{:S(2)}, u32[]{:S(2)}) async-start(f32[16,24,256]{2,1,0:T(8,128)} %shard_map.121), calls=%async_computation.4 | async-start | bytes 786432 | tf_op jit(solution)/shard_map/all_to_all | solution.py:828
  11.5 5.1 %shard_map.124 = (f32[2,4,416,128]{3,2,1,0:T(8,128)S(1)}, bf16[2,512,512]{2,1,0:T(8,128)(2,1)S(1)}, f32[2,3,8,512]{3,2,1,0:T(8,128)S(1)}) custom-call(f32[2,384,512]{2,1,0:T(8,128)} %refs_4_.1, f32[384,512]{1,0:T(8,128)} %pot_in.1, f32[512,512]{1,0:T(8,128)} %mix_ref.1), custom_call_target="tpu_custom_call" | custom-call | tf_op jit(solution)/shard_map/pallas_call | solution.py:829
  16.7 4.0 %all-to-all-done.4.refs_0_.got_ref = f32[16,24,256]{2,1,0:T(8,128)S(1)} async-done(((f32[16,24,256]{2,1,0:T(8,128)}), f32[16,24,256]{2,1,0:T(8,128)S(1)}, u32[]{:S(2)}, u32[]{:S(2)}) %all-to-all-start.4) | async-done | bytes 393248 | tf_op jit(solution)/shard_map/all_to_all | solution.py:828
  20.7 1.3 %collective-permute-start.4 = (f32[24,256]{1,0:T(8,128)S(1)}, f32[24,256]{1,0:T(8,128)S(1)}, u32[]{:S(2)}, u32[]{:S(2)}) collective-permute-start(f32[24,256]{1,0:T(8,128)S(1)} %get-tuple-element.164.mine_ref), channel_id=1, source_target_pairs={{0,32},{16,48},{32,0},{48,16},{64,96},{80,112},{96,64},{112,80},{1... | collective-permute-start | bytes 73736 | tf_op jit(solution)/shard_map/ppermute | solution.py:783
  22.0 1.9 %shard_map.122.after_ref.block_a = f32[2,256]{1,0:T(2,128)S(1)} custom-call(f32[16,24,256]{2,1,0:T(8,128)S(1)} %all-to-all-done.4.refs_0_.got_ref, f32[1,4096,256]{2,1,0:T(8,128)} %refs_1_.8), custom_call_target="tpu_custom_call" | custom-call | tf_op jit(solution)/shard_map/pallas_call | solution.py:195
  23.9 0.0 collective-permute-done.4.other_ref.near_ref
  24.0 0.0 copy-start.20
  24.0 0.0 copy-start.24
  24.0 0.0 copy-start.26
  24.0 0.0 copy-start.27
  24.0 0.0 copy-start.28
  24.0 0.0 copy-start.29
  24.0 2.1 %collective-permute-start.5 = (f32[32,256]{1,0:T(8,128)S(1)}, f32[32,256]{1,0:T(8,128)S(1)}, u32[]{:S(2)}, u32[]{:S(2)}) collective-permute-start(f32[32,256]{1,0:T(8,128)S(1)} %get-tuple-element.166.mine_ref), channel_id=1, source_target_pairs={{0,96},{16,112},{32,64},{48,80},{64,32},{80,48},{96,0},{112,16},{1... | collective-permute-start | bytes 98312 | tf_op jit(solution)/shard_map/ppermute | solution.py:785
  26.1 1.9 %shard_map.123.after_ref.block_b = f32[2,256]{1,0:T(2,128)S(1)} custom-call(f32[16,24,256]{2,1,0:T(8,128)S(1)} %all-to-all-done.4.refs_0_.got_ref, f32[1,4096,256]{2,1,0:T(8,128)} %refs_1_.8), custom_call_target="tpu_custom_call" | custom-call | tf_op jit(solution)/shard_map/pallas_call | solution.py:195
  28.0 0.1 collective-permute-done.5.other_ref
  28.1 3.8 %collective-permute-start.6 = (f32[48,256]{1,0:T(8,128)S(1)}, f32[48,256]{1,0:T(8,128)S(1)}, u32[]{:S(2)}, u32[]{:S(2)}) collective-permute-start(f32[48,256]{1,0:T(8,128)S(1)} %get-tuple-element.168.mine_ref), channel_id=1, source_target_pairs={{0,16},{16,0},{32,48},{48,32},{64,80},{80,64},{96,112},{112,96},{1... | collective-permute-start | bytes 147464 | tf_op jit(solution)/shard_map/ppermute | solution.py:787
  31.9 0.9 %collective-permute-done.6.other_ref = f32[48,256]{1,0:T(8,128)S(1)} collective-permute-done((f32[48,256]{1,0:T(8,128)S(1)}, f32[48,256]{1,0:T(8,128)S(1)}, u32[]{:S(2)}, u32[]{:S(2)}) %collective-permute-start.6) | collective-permute-done | bytes 49184 | tf_op jit(solution)/shard_map/ppermute | solution.py:787
  32.8 0.0 copy-done.20
  32.8 0.0 copy-done.24
  32.8 0.0 copy-done.26
  32.8 0.0 copy-done.27
  32.8 0.0 copy-done.28
  32.8 0.0 copy-done.29
  32.8 2.6 %shard_map.128 = (f32[2,256]{1,0:T(2,128)S(1)}, f32[16,24,256]{2,1,0:T(8,128)}, f32[2,8,512]{2,1,0:T(8,128)}) custom-call(s32[2,8]{1,0:T(2,128)S(1)} %bitcast.135, s32[2,8]{1,0:T(2,128)S(1)} %bitcast.137, f32[2,256]{1,0:T(2,128)S(1)} %shard_map.122.after_ref.block_a, f32[2,256]{1,0:T(2,128)S(1)} %shard_map.123.after_ref.block_b, f32[2,256]{1,0:T(2,128)S(1)} %copy-done.26, ...), custom_call_target="tpu_custom_call" | custom-call | tf_op jit(solution)/shard_map/pallas_call | solution.py:864
  35.4 3.6 %all-to-all-start.5 = ((f32[16,24,256]{2,1,0:T(8,128)}), f32[16,24,256]{2,1,0:T(8,128)S(1)}, u32[]{:S(2)}, u32[]{:S(2)}) async-start(f32[16,24,256]{2,1,0:T(8,128)} %get-tuple-element.173), calls=%async_computation.5 | async-start | bytes 786432 | tf_op jit(solution)/shard_map/all_to_all | solution.py:885
  39.0 6.1 %shard_map.131 = (f32[2,4,416,128]{3,2,1,0:T(8,128)S(1)}, f32[2,4,384,128]{3,2,1,0:T(8,128)}, f32[33,8,128]{2,1,0:T(8,128)}) custom-call(f32[2,8,512]{2,1,0:T(8,128)} %get-tuple-element.175.patch_ref, f32[2,4,416,128]{3,2,1,0:T(8,128)S(1)} %get-tuple-element.163.after_ref.wide_in, f32[2,384,512]{2,1,0:T(8,128)} %refs_4_.1, ...), custom_call_target="tpu_custom_call", output_to_operand_aliasing={{0}: (1, {})} | custom-call | tf_op jit(solution)/shard_map/pallas_call | solution.py:887
  45.1 3.4 %all-to-all-done.5.refs_0_.got_ref = f32[16,24,256]{2,1,0:T(8,128)S(1)} async-done(((f32[16,24,256]{2,1,0:T(8,128)}), f32[16,24,256]{2,1,0:T(8,128)S(1)}, u32[]{:S(2)}, u32[]{:S(2)}) %all-to-all-start.5) | async-done | bytes 393248 | tf_op jit(solution)/shard_map/all_to_all | solution.py:885
  48.5 0.1 collective-permute-start.7
  48.6 1.9 %shard_map.129.after_ref.block_a = f32[2,256]{1,0:T(2,128)S(1)} custom-call(f32[16,24,256]{2,1,0:T(8,128)S(1)} %all-to-all-done.5.refs_0_.got_ref, f32[1,4096,256]{2,1,0:T(8,128)} %refs_1_.8), custom_call_target="tpu_custom_call" | custom-call | tf_op jit(solution)/shard_map/pallas_call | solution.py:195
  50.5 0.8 collective-permute-done.7.other_ref.near_ref
  51.3 0.0 copy-start.1
  51.3 0.0 copy-start.21
  51.3 0.0 copy-start.25
  51.3 2.6 %collective-permute-start.8 = (f32[32,256]{1,0:T(8,128)S(1)}, f32[32,256]{1,0:T(8,128)S(1)}, u32[]{:S(2)}, u32[]{:S(2)}) collective-permute-start(f32[32,256]{1,0:T(8,128)S(1)} %get-tuple-element.179.mine_ref), channel_id=1, source_target_pairs={{0,96},{16,112},{32,64},{48,80},{64,32},{80,48},{96,0},{112,16},{1... | collective-permute-start | bytes 98312 | tf_op jit(solution)/shard_map/ppermute | solution.py:785
  53.9 1.9 %shard_map.130.after_ref.block_b = f32[2,256]{1,0:T(2,128)S(1)} custom-call(f32[16,24,256]{2,1,0:T(8,128)S(1)} %all-to-all-done.5.refs_0_.got_ref, f32[1,4096,256]{2,1,0:T(8,128)} %refs_1_.8), custom_call_target="tpu_custom_call" | custom-call | tf_op jit(solution)/shard_map/pallas_call | solution.py:195
  55.8 0.0 collective-permute-done.8.other_ref
  55.8 3.4 %collective-permute-start.9 = (f32[48,256]{1,0:T(8,128)S(1)}, f32[48,256]{1,0:T(8,128)S(1)}, u32[]{:S(2)}, u32[]{:S(2)}) collective-permute-start(f32[48,256]{1,0:T(8,128)S(1)} %get-tuple-element.181.mine_ref), channel_id=1, source_target_pairs={{0,16},{16,0},{32,48},{48,32},{64,80},{80,64},{96,112},{112,96},{1... | collective-permute-start | bytes 147464 | tf_op jit(solution)/shard_map/ppermute | solution.py:787
  59.3 0.9 %collective-permute-done.9.other_ref = f32[48,256]{1,0:T(8,128)S(1)} collective-permute-done((f32[48,256]{1,0:T(8,128)S(1)}, f32[48,256]{1,0:T(8,128)S(1)}, u32[]{:S(2)}, u32[]{:S(2)}) %collective-permute-start.9) | collective-permute-done | bytes 49184 | tf_op jit(solution)/shard_map/ppermute | solution.py:787
  60.2 0.0 copy-done
  60.2 0.0 copy-done.1
  60.2 0.0 copy-done.21
  60.2 0.0 copy-done.25
  60.2 0.0 copy-start.9
  60.2 1.3 %shard_map.135 = (f32[2,256]{1,0:T(2,128)S(1)}, f32[2,2,8,512]{3,2,1,0:T(8,128)S(1)}, f32[128,128]{1,0:T(8,128)S(1)}) custom-call(s32[2,8]{1,0:T(2,128)S(1)} %bitcast.136, s32[2,8]{1,0:T(2,128)S(1)} %bitcast.138, f32[2,256]{1,0:T(2,128)S(1)} %shard_map.129.after_ref.block_a, f32[2,256]{1,0:T(2,128)S(1)} %shard_map.130.after_ref.block_b, ...), custom_call_target="tpu_custom_call" | custom-call | tf_op jit(solution)/shard_map/pallas_call | solution.py:195
  61.5 14.7 %all_to_all.31 = f32[128,1,128]{2,1,0:T(1,128)S(1)} all-to-all(f32[128,1,128]{2,1,0:T(1,128)S(1)} %bitcast.125), channel_id=1, replica_groups=mesh['rad'=8,'chan'=16] {'rad','chan'}, dimensions={0} | all-to-all | bytes 131072 | tf_op jit(solution)/shard_map/all_to_all | solution.py:923
  76.2 2.3 %shard_map.136 = (f32[2,256]{1,0:T(2,128)}, f32[2,384,512]{2,1,0:T(8,128)}, f32[2,2,3]{2,1,0:T(2,128)}, f32[1,128]{1,0:T(1,128)}) custom-call(f32[128,128]{1,0:T(8,128)S(1)} %bitcast.123, f32[2,256]{1,0:T(2,128)S(1)} %copy-done.26, f32[2,256]{1,0:T(2,128)S(1)} %get-tuple-element.174.inner_ref.refs_2_, f32[2,256]{1,0:T(2,128)S(1)} %get-tuple-element.187.refs_3_, ...), custom_call_target="tpu_custom_call" | custom-call | tf_op jit(solution)/shard_map/pallas_call | solution.py:924
  78.6 0.8 %while.18 = (f32[]{:T(128)}, f32[2,256]{1,0:T(2,128)}, f32[2,384,512]{2,1,0:T(8,128)}, f32[2,2,3]{2,1,0:T(2,128)}, f32[2,256]{1,0:T(2,128)S(1)}, /*index=5*/f32[...) while((f32[]{:T(128)}, f32[2,256]{1,0:T(2,128)}, ...), condition=%region_29.30_spmd, body=%region_0.29_spmd | while | flops 4953002496 | bytes 191500976 | solution.py:944
  (8 shorter events, 0.1 us)
Async XLA Ops:
  2.9 17.8 %all-to-all-start.4 = ((f32[16,24,256]{2,1,0:T(8,128)}), f32[16,24,256]{2,1,0:T(8,128)S(1)}, u32[]{:S(2)}, u32[]{:S(2)}) async-start(f32[16,24,256]{2,1,0:T(8,128)} %shard_map.121), calls=%async_computation.4 | async-start | bytes 786432 | tf_op jit(solution)/shard_map/all_to_all | solution.py:828
  20.7 3.2 %collective-permute-start.4 = (f32[24,256]{1,0:T(8,128)S(1)}, f32[24,256]{1,0:T(8,128)S(1)}, u32[]{:S(2)}, u32[]{:S(2)}) collective-permute-start(f32[24,256]{1,0:T(8,128)S(1)} %get-tuple-element.164.mine_ref), channel_id=1, source_target_pairs={{0,32},{16,48},{32,0},{48,16},{64,96},{80,112},{96,64},{112,80},{1... | collective-permute-start | bytes 73736 | tf_op jit(solution)/shard_map/ppermute | solution.py:783
  24.0 8.8 %copy-start.20 = (f32[1,2,512,256]{3,2,1,0:T(8,128)S(1)}, f32[1,2,512,256]{3,2,1,0:T(8,128)}, u32[]{:S(2)}) copy-start(f32[1,2,512,256]{3,2,1,0:T(8,128)} %coupling_ref.3) | copy-start | bytes 3145732
  24.0 8.8 %copy-start.24 = (f32[1,2,256,512]{3,2,1,0:T(8,128)S(1)}, f32[1,2,256,512]{3,2,1,0:T(8,128)}, u32[]{:S(2)}) copy-start(f32[1,2,256,512]{3,2,1,0:T(8,128)} %amp_ref.5) | copy-start | bytes 3145732
  24.0 8.8 %copy-start.26 = (f32[2,256]{1,0:T(2,128)S(1)}, f32[2,256]{1,0:T(2,128)}, u32[]{:S(2)}) copy-start(f32[2,256]{1,0:T(2,128)} %refs_1_.9) | copy-start | bytes 6148
  24.0 8.8 %copy-start.27 = (s32[512]{0:T(512)S(1)}, s32[512]{0:T(512)}, u32[]{:S(2)}) copy-start(s32[512]{0:T(512)} %param.31) | copy-start | bytes 6148
  24.0 8.8 %copy-start.28 = (s32[8,2]{0,1:T(2,128)S(1)}, s32[8,2]{0,1:T(2,128)}, u32[]{:S(2)}) copy-start(s32[8,2]{0,1:T(2,128)} %param.29) | copy-start | bytes 196
  24.0 8.8 %copy-start.29 = (s32[8,2]{0,1:T(2,128)S(1)}, s32[8,2]{0,1:T(2,128)}, u32[]{:S(2)}) copy-start(s32[8,2]{0,1:T(2,128)} %param.30) | copy-start | bytes 196
  24.0 4.1 %collective-permute-start.5 = (f32[32,256]{1,0:T(8,128)S(1)}, f32[32,256]{1,0:T(8,128)S(1)}, u32[]{:S(2)}, u32[]{:S(2)}) collective-permute-start(f32[32,256]{1,0:T(8,128)S(1)} %get-tuple-element.166.mine_ref), channel_id=1, source_target_pairs={{0,96},{16,112},{32,64},{48,80},{64,32},{80,48},{96,0},{112,16},{1... | collective-permute-start | bytes 98312 | tf_op jit(solution)/shard_map/ppermute | solution.py:785
  28.1 4.7 %collective-permute-start.6 = (f32[48,256]{1,0:T(8,128)S(1)}, f32[48,256]{1,0:T(8,128)S(1)}, u32[]{:S(2)}, u32[]{:S(2)}) collective-permute-start(f32[48,256]{1,0:T(8,128)S(1)} %get-tuple-element.168.mine_ref), channel_id=1, source_target_pairs={{0,16},{16,0},{32,48},{48,32},{64,80},{80,64},{96,112},{112,96},{1... | collective-permute-start | bytes 147464 | tf_op jit(solution)/shard_map/ppermute | solution.py:787
  35.4 13.1 %all-to-all-start.5 = ((f32[16,24,256]{2,1,0:T(8,128)}), f32[16,24,256]{2,1,0:T(8,128)S(1)}, u32[]{:S(2)}, u32[]{:S(2)}) async-start(f32[16,24,256]{2,1,0:T(8,128)} %get-tuple-element.173), calls=%async_computation.5 | async-start | bytes 786432 | tf_op jit(solution)/shard_map/all_to_all | solution.py:885
  48.5 2.8 %collective-permute-start.7 = (f32[24,256]{1,0:T(8,128)S(1)}, f32[24,256]{1,0:T(8,128)S(1)}, u32[]{:S(2)}, u32[]{:S(2)}) collective-permute-start(f32[24,256]{1,0:T(8,128)S(1)} %get-tuple-element.177.mine_ref), channel_id=1, source_target_pairs={{0,32},{16,48},{32,0},{48,16},{64,96},{80,112},{96,64},{112,80},{1... | collective-permute-start | bytes 73736 | tf_op jit(solution)/shard_map/ppermute | solution.py:783
  51.3 8.9 %copy-start = (f32[2,4,384,128]{3,2,1,0:T(8,128)S(1)}, f32[2,4,384,128]{3,2,1,0:T(8,128)}, u32[]{:S(2)}) copy-start(f32[2,4,384,128]{3,2,1,0:T(8,128)} %get-tuple-element.185.second_ref.refs_6_) | copy-start | bytes 4718596
  51.3 8.9 %copy-start.1 = (f32[33,8,128]{2,1,0:T(8,128)S(1)}, f32[33,8,128]{2,1,0:T(8,128)}, u32[]{:S(2)}) copy-start(f32[33,8,128]{2,1,0:T(8,128)} %get-tuple-element.176.after_ref.notes_ref) | copy-start | bytes 405508
  51.3 8.8 %copy-start.21 = (f32[1,2,512,256]{3,2,1,0:T(8,128)S(1)}, f32[1,2,512,256]{3,2,1,0:T(8,128)}, u32[]{:S(2)}) copy-start(f32[1,2,512,256]{3,2,1,0:T(8,128)} %coupling_ref.3) | copy-start | bytes 3145732
  51.3 8.8 %copy-start.25 = (f32[1,2,256,512]{3,2,1,0:T(8,128)S(1)}, f32[1,2,256,512]{3,2,1,0:T(8,128)}, u32[]{:S(2)}) copy-start(f32[1,2,256,512]{3,2,1,0:T(8,128)} %amp_ref.5) | copy-start | bytes 3145732
  51.3 4.4 %collective-permute-start.8 = (f32[32,256]{1,0:T(8,128)S(1)}, f32[32,256]{1,0:T(8,128)S(1)}, u32[]{:S(2)}, u32[]{:S(2)}) collective-permute-start(f32[32,256]{1,0:T(8,128)S(1)} %get-tuple-element.179.mine_ref), channel_id=1, source_target_pairs={{0,96},{16,112},{32,64},{48,80},{64,32},{80,48},{96,0},{112,16},{1... | collective-permute-start | bytes 98312 | tf_op jit(solution)/shard_map/ppermute | solution.py:785
  55.8 4.3 %collective-permute-start.9 = (f32[48,256]{1,0:T(8,128)S(1)}, f32[48,256]{1,0:T(8,128)S(1)}, u32[]{:S(2)}, u32[]{:S(2)}) collective-permute-start(f32[48,256]{1,0:T(8,128)S(1)} %get-tuple-element.181.mine_ref), channel_id=1, source_target_pairs={{0,16},{16,0},{32,48},{48,32},{64,80},{80,64},{96,112},{112,96},{1... | collective-permute-start | bytes 147464 | tf_op jit(solution)/shard_map/ppermute | solution.py:787
  60.2 16.1 %copy-start.9 = (f32[2,384,512]{2,1,0:T(8,128)S(1)}, f32[2,384,512]{2,1,0:T(8,128)}, u32[]{:S(2)}) copy-start(f32[2,384,512]{2,1,0:T(8,128)} %refs_4_.1) | copy-start | bytes 4718596

commit v7 on v6

--- a/solution.py
+++ b/solution.py
@@ -519,7 +519,7 @@
 
 def inner_result(partners_ref, offsets_ref, block_a, block_b, inner_ref, mine_ref, other_ref, coupling_ref, amp_ref, member, row):
     result = block_a[...] + block_b[...] - shift * inner_ref[...]
-    couplings, band_width = coupling_ref.shape[1:3]
+    couplings, _, band_width = coupling_ref.shape[:3]
     block_index = lax.axis_index("rad")
     for couple_index in range(couplings):
         apart = partners_ref[couple_index, block_index] ^ block_index
@@ -531,8 +531,8 @@
         near = jnp.concatenate([near, jnp.zeros((6, near.shape[1]), jnp.float32)], axis=0)
         first = offsets_ref[couple_index, block_index] + band_width
         window = pltpu.roll(near, near.shape[1] - first, 1)[0:2, :band_width]
-        result = result + few_rows_dot(window, two(coupling_ref[0, couple_index]))
-    return result + bloch_coef * few_rows_dot(row * member, two(amp_ref[0, 0]), flipped=True)
+        result = result + few_rows_dot(window, [coupling_ref[couple_index, part] for part in range(2)])
+    return result + bloch_coef * few_rows_dot(row * member, [amp_ref[0, part] for part in range(2)], flipped=True)
 
 
 def unpacked(kept_ref, other_ref):
@@ -609,16 +609,16 @@
         patch_ref[part] = jnp.concatenate(
             [first_rows[part], last_rows[part], jnp.zeros((4, near.shape[1]), jnp.float32)], axis=0
         )
-    copy = pltpu.make_async_copy(patch_ref, patch_out, patch_written)
-    copy.start()
-    copies = [copy] + send_ends(chunk_ref, first_rows, last_rows, ends_held, ends_written)
     image = inner_result(
         partners_ref, offsets_ref, block_a, block_b, inner_ref, mine_ref, other_ref, coupling_ref, amp_ref, member, row
     )
     image_ref[...] = image
     row = jnp.where(at_first(), jnp.concatenate([rows[0:1] for rows in first_rows], axis=0), 0.0)
-    amps = [two(amp_ref[0, radius]) for radius in range(2)]
-    copies += write_chunk(chunk_ref, image, ghost_rows(image, amps, member), row, held_ref, written)
+    amps = [[amp_ref[radius, part] for part in range(2)] for radius in range(2)]
+    copies = write_chunk(chunk_ref, image, ghost_rows(image, amps, member), row, held_ref, written)
+    copies += send_ends(chunk_ref, first_rows, last_rows, ends_held, ends_written)
+    copies.append(pltpu.make_async_copy(patch_ref, patch_out, patch_written))
+    copies[-1].start()
     for copy in copies:
         copy.wait()
 
@@ -773,6 +773,12 @@
         copy.wait()
 
 
+def weights_kernel(coupling_ref, amp_ref, after_ref, coupling_out, amp_out):
+    for k in range(2):
+        coupling_out[k, 0], coupling_out[k, 1] = two(coupling_ref[0, k])
+        amp_out[k, 0], amp_out[k, 1] = two(amp_ref[0, k])
+
+
 def same_kernel(in_ref, out_ref):
     out_ref[...] = in_ref[...]
 
@@ -857,10 +863,19 @@
             )
         return parts
 
+    def split_weights(after):
+        return run(
+            weights_kernel,
+            [((2, 2) + inner_coupling.shape[2:], bf16), ((2, 2) + surface_amp.shape[2:], bf16)],
+            (inner_coupling, surface_amp, after),
+            [whole()] * 2 + [anywhere()],
+        )
+
     gathered = [(24, rows), (16, rows), (2, 8, rows)]
     mine, kept, ends = run(gather_kernel, gathered, (got, wide), [whole(), anywhere()])
     block_parts = block_product(got)
     mine, other, kept = across_blocks(mine, kept, block_parts)
+    coupling, amp = split_weights(mine)
     p_inner, chunk, patch = pl.pallas_call(
         between_kernel,
         out_shape=[
@@ -879,7 +894,7 @@
         + [pltpu.VMEM((2, 8, channels), f32), pltpu.SemaphoreType.DMA, pltpu.VMEM((2, 2, 24, channels), f32)],
         compiler_params=pltpu.CompilerParams(vmem_limit_bytes=vmem_bytes),
     )(
-        *by_coupling, *block_parts, inner_state, mine, other, inner_coupling, surface_amp, group,
+        *by_coupling, *block_parts, inner_state, mine, other, coupling, amp, group,
         edges, mix, ends, kept,
     )
     got = lax.all_to_all(chunk, "chan", 0, 0)
@@ -910,11 +925,12 @@
     )
     block_parts = block_product(got)
     mine, other, kept = across_blocks(mine, kept, block_parts)
+    coupling, amp = split_weights(mine)
     q_inner, q_ends, parts = run(
         last_kernel,
         [(2, rows), (2, 2, 8, channels), (count, lanes)],
         (
-            *by_coupling, *block_parts, p_inner, mine, other, inner_coupling, surface_amp, group,
+            *by_coupling, *block_parts, p_inner, mine, other, coupling, amp, group,
             wide, mix, ends, kept, inner_state, second, notes,
         ),
         [scalars()] * 2 + [whole()] * 15,

time: 80 us -> 79.9 us (level)
    pallas_call x11 -> x13, Pallas kernels: 8.95 us -> 9.7 us  [run(): pl.pallas_call(kernel, out_shape=[jax.ShapeDtypeStruct(*out) if isinstanc...]
  transfers between devices with their start and end apart: 8 -> 8, of which waited for: 6 -> 5; matrix products, arithmetic and copies ran while one was open for 0% -> 0% of each run, Pallas kernels for 24% -> 25%
where the time goes in v7:
time: 79.9 us; the launch traced here: 79.4 us
  Pallas kernels  28.1 us (35%)
  starting transfers between devices  25.4 us (32%)
  blocking collectives  14.7 us (18%)
  waiting for transfers between devices  9.23 us (12%)
  between operations  1.03 us (1%)
  loops' own time  0.82 us (1%)
    all_to_all x1, blocking collectives, body(): lax.all_to_all(parts.reshape(count, 1, lanes), both, 0, 0)  14.7 us
    all_to_all x2, starting transfers between devices, body(): got = lax.all_to_all(chunk, 'chan', 0, 0)  12.2 us
    pallas_call x13, Pallas kernels, run(): pl.pallas_call(kernel, out_shape=[jax.ShapeDtypeStruct(*out) if isinstanc...  9.7 us
    all_to_all x2, waiting for transfers between devices, body(): got = lax.all_to_all(chunk, 'chan', 0, 0)  7.45 us
    ppermute x2, starting transfers between devices, across_blocks(): lax.ppermute(mine, 'rad', [(i, i ^ 1) for i in range(blocks)])  7.21 us
    pallas_call x1, Pallas kernels, body(): pl.pallas_call(second_outer_kernel, grid=(1,), out_shape=[jax.ShapeDtypeS...  6.09 us
    pallas_call x1, Pallas kernels, body(): pl.pallas_call(first_outer_kernel, out_shape=[jax.ShapeDtypeStruct((2, ou...  5.14 us
    ppermute x2, starting transfers between devices, across_blocks(): lax.ppermute(mine, 'rad', [(i, 2 * (last - i // 2) + i % 2) for i in rang...  4.65 us
  transfers between devices with their start and end apart: 8, of which 5 were waited for; matrix products, arithmetic and copies ran while one was open for 0% of the time, Pallas kernels for 25%

profile of v7, /device:TPU:1, one launch (start us, length us, event | category | flops | bytes accessed | tf_op | source)
XLA Modules:
  0.0 79.4 jit_solution(13679026928673112420)
XLA Ops:
  0.6 2.3 %shard_map.121 = f32[16,24,256]{2,1,0:T(8,128)} custom-call(f32[2,256]{1,0:T(2,128)} %refs_1_.9, f32[2,384,512]{2,1,0:T(8,128)} %refs_4_.1, f32[2,384,512]{2,1,0:T(8,128)} %refs_4_.1, f32[1,2,256,512]{3,2,1,0:T(8,128)} %amp_ref.5, s32[1,512]{1,0:T(1,128)} %bitcast.132), custom_call_target="tpu_custom_call" | custom-call | tf_op jit(solution)/shard_map/pallas_call | solution.py:820
  2.9 8.6 %all-to-all-start.4 = ((f32[16,24,256]{2,1,0:T(8,128)}), f32[16,24,256]{2,1,0:T(8,128)S(1)}, u32[]{:S(2)}, u32[]{:S(2)}) async-start(f32[16,24,256]{2,1,0:T(8,128)} %shard_map.121), calls=%async_computation.4 | async-start | bytes 786432 | tf_op jit(solution)/shard_map/all_to_all | solution.py:834
  11.5 5.1 %shard_map.124 = (f32[2,4,416,128]{3,2,1,0:T(8,128)S(1)}, bf16[2,512,512]{2,1,0:T(8,128)(2,1)S(1)}, f32[2,3,8,512]{3,2,1,0:T(8,128)S(1)}) custom-call(f32[2,384,512]{2,1,0:T(8,128)} %refs_4_.1, f32[384,512]{1,0:T(8,128)} %pot_in.1, f32[512,512]{1,0:T(8,128)} %mix_ref.1), custom_call_target="tpu_custom_call" | custom-call | tf_op jit(solution)/shard_map/pallas_call | solution.py:835
  16.7 4.0 %all-to-all-done.4.refs_0_.got_ref = f32[16,24,256]{2,1,0:T(8,128)S(1)} async-done(((f32[16,24,256]{2,1,0:T(8,128)}), f32[16,24,256]{2,1,0:T(8,128)S(1)}, u32[]{:S(2)}, u32[]{:S(2)}) %all-to-all-start.4) | async-done | bytes 393248 | tf_op jit(solution)/shard_map/all_to_all | solution.py:834
  20.7 1.3 %collective-permute-start.4 = (f32[24,256]{1,0:T(8,128)S(1)}, f32[24,256]{1,0:T(8,128)S(1)}, u32[]{:S(2)}, u32[]{:S(2)}) collective-permute-start(f32[24,256]{1,0:T(8,128)S(1)} %get-tuple-element.168.mine_ref), channel_id=1, source_target_pairs={{0,32},{16,48},{32,0},{48,16},{64,96},{80,112},{96,64},{112,80},{1... | collective-permute-start | bytes 73736 | tf_op jit(solution)/shard_map/ppermute | solution.py:789
  22.0 1.9 %shard_map.122.after_ref.block_a = f32[2,256]{1,0:T(2,128)S(1)} custom-call(f32[16,24,256]{2,1,0:T(8,128)S(1)} %all-to-all-done.4.refs_0_.got_ref, f32[1,4096,256]{2,1,0:T(8,128)} %refs_1_.8), custom_call_target="tpu_custom_call" | custom-call | tf_op jit(solution)/shard_map/pallas_call | solution.py:195
  23.9 0.0 collective-permute-done.4.other_ref.near_ref
  24.0 0.0 copy-start.20
  24.0 0.0 copy-start.24
  24.0 2.1 %collective-permute-start.5 = (f32[32,256]{1,0:T(8,128)S(1)}, f32[32,256]{1,0:T(8,128)S(1)}, u32[]{:S(2)}, u32[]{:S(2)}) collective-permute-start(f32[32,256]{1,0:T(8,128)S(1)} %get-tuple-element.170.mine_ref), channel_id=1, source_target_pairs={{0,96},{16,112},{32,64},{48,80},{64,32},{80,48},{96,0},{112,16},{1... | collective-permute-start | bytes 98312 | tf_op jit(solution)/shard_map/ppermute | solution.py:791
  26.1 1.9 %shard_map.123.after_ref.block_b = f32[2,256]{1,0:T(2,128)S(1)} custom-call(f32[16,24,256]{2,1,0:T(8,128)S(1)} %all-to-all-done.4.refs_0_.got_ref, f32[1,4096,256]{2,1,0:T(8,128)} %refs_1_.8), custom_call_target="tpu_custom_call" | custom-call | tf_op jit(solution)/shard_map/pallas_call | solution.py:195
  28.0 0.0 copy-start.27
  28.0 0.0 copy-start.28
  28.0 0.0 copy-start.29
  28.0 0.0 copy-start.30
  28.0 0.0 collective-permute-done.5.other_ref
  28.1 3.8 %collective-permute-start.6 = (f32[48,256]{1,0:T(8,128)S(1)}, f32[48,256]{1,0:T(8,128)S(1)}, u32[]{:S(2)}, u32[]{:S(2)}) collective-permute-start(f32[48,256]{1,0:T(8,128)S(1)} %get-tuple-element.172.after_ref.mine_ref), channel_id=1, source_target_pairs={{0,16},{16,0},{32,48},{48,32},{64,80},{80,64},{96,112},{112,96},{1... | collective-permute-start | bytes 147464 | tf_op jit(solution)/shard_map/ppermute | solution.py:793
  31.8 0.0 copy-done.20
  31.8 0.0 copy-done.24
  31.8 0.4 shard_map.128
  32.2 0.5 collective-permute-done.6.other_ref
  32.7 0.0 copy-done.27
  32.7 0.0 copy-done.28
  32.7 0.0 copy-done.29
  32.7 0.0 copy-done.30
  32.7 2.6 %shard_map.129 = (f32[2,256]{1,0:T(2,128)S(1)}, f32[16,24,256]{2,1,0:T(8,128)}, f32[2,8,512]{2,1,0:T(8,128)}) custom-call(s32[2,8]{1,0:T(2,128)S(1)} %bitcast.135, s32[2,8]{1,0:T(2,128)S(1)} %bitcast.137, f32[2,256]{1,0:T(2,128)S(1)} %shard_map.122.after_ref.block_a, f32[2,256]{1,0:T(2,128)S(1)} %shard_map.123.after_ref.block_b, f32[2,256]{1,0:T(2,128)S(1)} %copy-done.27, ...), custom_call_target="tpu_custom_call" | custom-call | tf_op jit(solution)/shard_map/pallas_call | solution.py:879
  35.3 3.6 %all-to-all-start.5 = ((f32[16,24,256]{2,1,0:T(8,128)}), f32[16,24,256]{2,1,0:T(8,128)S(1)}, u32[]{:S(2)}, u32[]{:S(2)}) async-start(f32[16,24,256]{2,1,0:T(8,128)} %get-tuple-element.179), calls=%async_computation.5 | async-start | bytes 786432 | tf_op jit(solution)/shard_map/all_to_all | solution.py:900
  38.9 6.1 %shard_map.132 = (f32[2,4,416,128]{3,2,1,0:T(8,128)S(1)}, f32[2,4,384,128]{3,2,1,0:T(8,128)}, f32[33,8,128]{2,1,0:T(8,128)}) custom-call(f32[2,8,512]{2,1,0:T(8,128)} %get-tuple-element.181.patch_ref, f32[2,4,416,128]{3,2,1,0:T(8,128)S(1)} %get-tuple-element.167.after_ref.wide_in, f32[2,384,512]{2,1,0:T(8,128)} %refs_4_.1, ...), custom_call_target="tpu_custom_call", output_to_operand_aliasing={{0}: (1, {})} | custom-call | tf_op jit(solution)/shard_map/pallas_call | solution.py:902
  45.0 3.4 %all-to-all-done.5.refs_0_.got_ref = f32[16,24,256]{2,1,0:T(8,128)S(1)} async-done(((f32[16,24,256]{2,1,0:T(8,128)}), f32[16,24,256]{2,1,0:T(8,128)S(1)}, u32[]{:S(2)}, u32[]{:S(2)}) %all-to-all-start.5) | async-done | bytes 393248 | tf_op jit(solution)/shard_map/all_to_all | solution.py:900
  48.4 0.1 collective-permute-start.7
  48.5 1.9 %shard_map.130.after_ref.block_a = f32[2,256]{1,0:T(2,128)S(1)} custom-call(f32[16,24,256]{2,1,0:T(8,128)S(1)} %all-to-all-done.5.refs_0_.got_ref, f32[1,4096,256]{2,1,0:T(8,128)} %refs_1_.8), custom_call_target="tpu_custom_call" | custom-call | tf_op jit(solution)/shard_map/pallas_call | solution.py:195
  50.4 0.8 collective-permute-done.7.other_ref.near_ref
  51.2 0.0 copy-start.25
  51.2 2.6 %collective-permute-start.8 = (f32[32,256]{1,0:T(8,128)S(1)}, f32[32,256]{1,0:T(8,128)S(1)}, u32[]{:S(2)}, u32[]{:S(2)}) collective-permute-start(f32[32,256]{1,0:T(8,128)S(1)} %get-tuple-element.185.mine_ref), channel_id=1, source_target_pairs={{0,96},{16,112},{32,64},{48,80},{64,32},{80,48},{96,0},{112,16},{1... | collective-permute-start | bytes 98312 | tf_op jit(solution)/shard_map/ppermute | solution.py:791
  53.8 1.9 %shard_map.131.after_ref.block_b = f32[2,256]{1,0:T(2,128)S(1)} custom-call(f32[16,24,256]{2,1,0:T(8,128)S(1)} %all-to-all-done.5.refs_0_.got_ref, f32[1,4096,256]{2,1,0:T(8,128)} %refs_1_.8), custom_call_target="tpu_custom_call" | custom-call | tf_op jit(solution)/shard_map/pallas_call | solution.py:195
  55.7 0.0 copy-start
  55.7 0.0 copy-start.1
  55.7 0.0 collective-permute-done.8.other_ref
  55.7 3.4 %collective-permute-start.9 = (f32[48,256]{1,0:T(8,128)S(1)}, f32[48,256]{1,0:T(8,128)S(1)}, u32[]{:S(2)}, u32[]{:S(2)}) collective-permute-start(f32[48,256]{1,0:T(8,128)S(1)} %get-tuple-element.187.after_ref.mine_ref), channel_id=1, source_target_pairs={{0,16},{16,0},{32,48},{48,32},{64,80},{80,64},{96,112},{112,96},{1... | collective-permute-start | bytes 147464 | tf_op jit(solution)/shard_map/ppermute | solution.py:793
  59.2 0.0 copy-done.21
  59.2 0.4 shard_map.136
  59.5 0.5 collective-permute-done.9.other_ref
  60.0 0.0 copy-done
  60.0 1.3 %shard_map.137 = (f32[2,256]{1,0:T(2,128)S(1)}, f32[2,2,8,512]{3,2,1,0:T(8,128)S(1)}, f32[128,128]{1,0:T(8,128)S(1)}) custom-call(s32[2,8]{1,0:T(2,128)S(1)} %bitcast.136, s32[2,8]{1,0:T(2,128)S(1)} %bitcast.138, f32[2,256]{1,0:T(2,128)S(1)} %shard_map.130.after_ref.block_a, f32[2,256]{1,0:T(2,128)S(1)} %shard_map.131.after_ref.block_b, ...), custom_call_target="tpu_custom_call" | custom-call | tf_op jit(solution)/shard_map/pallas_call | solution.py:195
  61.3 14.7 %all_to_all.31 = f32[128,1,128]{2,1,0:T(1,128)S(1)} all-to-all(f32[128,1,128]{2,1,0:T(1,128)S(1)} %bitcast.125), channel_id=1, replica_groups=mesh['rad'=8,'chan'=16] {'rad','chan'}, dimensions={0} | all-to-all | bytes 131072 | tf_op jit(solution)/shard_map/all_to_all | solution.py:939
  76.1 0.0 copy-done.9
  76.1 2.3 %shard_map.138 = (f32[2,256]{1,0:T(2,128)}, f32[2,384,512]{2,1,0:T(8,128)}, f32[2,2,3]{2,1,0:T(2,128)}, f32[1,128]{1,0:T(1,128)}) custom-call(f32[128,128]{1,0:T(8,128)S(1)} %bitcast.123, f32[2,256]{1,0:T(2,128)S(1)} %copy-done.27, f32[2,256]{1,0:T(2,128)S(1)} %get-tuple-element.180.inner_ref.refs_2_, f32[2,256]{1,0:T(2,128)S(1)} %get-tuple-element.195.refs_3_, ...), custom_call_target="tpu_custom_call" | custom-call | tf_op jit(solution)/shard_map/pallas_call | solution.py:940
  78.4 0.8 %while.18 = (f32[]{:T(128)}, f32[2,256]{1,0:T(2,128)}, f32[2,384,512]{2,1,0:T(8,128)}, f32[2,2,3]{2,1,0:T(2,128)}, f32[2,256]{1,0:T(2,128)S(1)}, /*index=5*/f32[...) while((f32[]{:T(128)}, f32[2,256]{1,0:T(2,128)}, ...), condition=%region_29.30_spmd, body=%region_0.29_spmd | while | flops 4953002496 | bytes 195695312 | solution.py:960
  (10 shorter events, 0.1 us)
Async XLA Ops:
  2.9 17.8 %all-to-all-start.4 = ((f32[16,24,256]{2,1,0:T(8,128)}), f32[16,24,256]{2,1,0:T(8,128)S(1)}, u32[]{:S(2)}, u32[]{:S(2)}) async-start(f32[16,24,256]{2,1,0:T(8,128)} %shard_map.121), calls=%async_computation.4 | async-start | bytes 786432 | tf_op jit(solution)/shard_map/all_to_all | solution.py:834
  20.7 3.2 %collective-permute-start.4 = (f32[24,256]{1,0:T(8,128)S(1)}, f32[24,256]{1,0:T(8,128)S(1)}, u32[]{:S(2)}, u32[]{:S(2)}) collective-permute-start(f32[24,256]{1,0:T(8,128)S(1)} %get-tuple-element.168.mine_ref), channel_id=1, source_target_pairs={{0,32},{16,48},{32,0},{48,16},{64,96},{80,112},{96,64},{112,80},{1... | collective-permute-start | bytes 73736 | tf_op jit(solution)/shard_map/ppermute | solution.py:789
  24.0 7.9 %copy-start.20 = (f32[1,2,512,256]{3,2,1,0:T(8,128)S(1)}, f32[1,2,512,256]{3,2,1,0:T(8,128)}, u32[]{:S(2)}) copy-start(f32[1,2,512,256]{3,2,1,0:T(8,128)} %coupling_ref.3) | copy-start | bytes 3145732
  24.0 7.9 %copy-start.24 = (f32[1,2,256,512]{3,2,1,0:T(8,128)S(1)}, f32[1,2,256,512]{3,2,1,0:T(8,128)}, u32[]{:S(2)}) copy-start(f32[1,2,256,512]{3,2,1,0:T(8,128)} %amp_ref.5) | copy-start | bytes 3145732
  24.0 4.1 %collective-permute-start.5 = (f32[32,256]{1,0:T(8,128)S(1)}, f32[32,256]{1,0:T(8,128)S(1)}, u32[]{:S(2)}, u32[]{:S(2)}) collective-permute-start(f32[32,256]{1,0:T(8,128)S(1)} %get-tuple-element.170.mine_ref), channel_id=1, source_target_pairs={{0,96},{16,112},{32,64},{48,80},{64,32},{80,48},{96,0},{112,16},{1... | collective-permute-start | bytes 98312 | tf_op jit(solution)/shard_map/ppermute | solution.py:791
  28.0 4.8 %copy-start.27 = (f32[2,256]{1,0:T(2,128)S(1)}, f32[2,256]{1,0:T(2,128)}, u32[]{:S(2)}) copy-start(f32[2,256]{1,0:T(2,128)} %refs_1_.9) | copy-start | bytes 6148
  28.0 4.7 %copy-start.28 = (s32[512]{0:T(512)S(1)}, s32[512]{0:T(512)}, u32[]{:S(2)}) copy-start(s32[512]{0:T(512)} %param.31) | copy-start | bytes 6148
  28.0 4.7 %copy-start.29 = (s32[8,2]{0,1:T(2,128)S(1)}, s32[8,2]{0,1:T(2,128)}, u32[]{:S(2)}) copy-start(s32[8,2]{0,1:T(2,128)} %param.29) | copy-start | bytes 196
  28.0 4.7 %copy-start.30 = (s32[8,2]{0,1:T(2,128)S(1)}, s32[8,2]{0,1:T(2,128)}, u32[]{:S(2)}) copy-start(s32[8,2]{0,1:T(2,128)} %param.30) | copy-start | bytes 196
  28.1 4.7 %collective-permute-start.6 = (f32[48,256]{1,0:T(8,128)S(1)}, f32[48,256]{1,0:T(8,128)S(1)}, u32[]{:S(2)}, u32[]{:S(2)}) collective-permute-start(f32[48,256]{1,0:T(8,128)S(1)} %get-tuple-element.172.after_ref.mine_ref), channel_id=1, source_target_pairs={{0,16},{16,0},{32,48},{48,32},{64,80},{80,64},{96,112},{112,96},{1... | collective-permute-start | bytes 147464 | tf_op jit(solution)/shard_map/ppermute | solution.py:793
  35.3 13.1 %all-to-all-start.5 = ((f32[16,24,256]{2,1,0:T(8,128)}), f32[16,24,256]{2,1,0:T(8,128)S(1)}, u32[]{:S(2)}, u32[]{:S(2)}) async-start(f32[16,24,256]{2,1,0:T(8,128)} %get-tuple-element.179), calls=%async_computation.5 | async-start | bytes 786432 | tf_op jit(solution)/shard_map/all_to_all | solution.py:900
  48.4 2.8 %collective-permute-start.7 = (f32[24,256]{1,0:T(8,128)S(1)}, f32[24,256]{1,0:T(8,128)S(1)}, u32[]{:S(2)}, u32[]{:S(2)}) collective-permute-start(f32[24,256]{1,0:T(8,128)S(1)} %get-tuple-element.183.mine_ref), channel_id=1, source_target_pairs={{0,32},{16,48},{32,0},{48,16},{64,96},{80,112},{96,64},{112,80},{1... | collective-permute-start | bytes 73736 | tf_op jit(solution)/shard_map/ppermute | solution.py:789
  51.2 8.0 %copy-start.21 = (f32[1,2,512,256]{3,2,1,0:T(8,128)S(1)}, f32[1,2,512,256]{3,2,1,0:T(8,128)}, u32[]{:S(2)}) copy-start(f32[1,2,512,256]{3,2,1,0:T(8,128)} %coupling_ref.3) | copy-start | bytes 3145732
  51.2 8.0 %copy-start.25 = (f32[1,2,256,512]{3,2,1,0:T(8,128)S(1)}, f32[1,2,256,512]{3,2,1,0:T(8,128)}, u32[]{:S(2)}) copy-start(f32[1,2,256,512]{3,2,1,0:T(8,128)} %amp_ref.5) | copy-start | bytes 3145732
  51.2 4.5 %collective-permute-start.8 = (f32[32,256]{1,0:T(8,128)S(1)}, f32[32,256]{1,0:T(8,128)S(1)}, u32[]{:S(2)}, u32[]{:S(2)}) collective-permute-start(f32[32,256]{1,0:T(8,128)S(1)} %get-tuple-element.185.mine_ref), channel_id=1, source_target_pairs={{0,96},{16,112},{32,64},{48,80},{64,32},{80,48},{96,0},{112,16},{1... | collective-permute-start | bytes 98312 | tf_op jit(solution)/shard_map/ppermute | solution.py:791
  55.7 4.4 %copy-start = (f32[2,4,384,128]{3,2,1,0:T(8,128)S(1)}, f32[2,4,384,128]{3,2,1,0:T(8,128)}, u32[]{:S(2)}) copy-start(f32[2,4,384,128]{3,2,1,0:T(8,128)} %get-tuple-element.193.second_ref.refs_6_) | copy-start | bytes 4718596
  55.7 4.4 %copy-start.1 = (f32[33,8,128]{2,1,0:T(8,128)S(1)}, f32[33,8,128]{2,1,0:T(8,128)}, u32[]{:S(2)}) copy-start(f32[33,8,128]{2,1,0:T(8,128)} %get-tuple-element.182.after_ref.notes_ref) | copy-start | bytes 405508
  55.7 4.3 %collective-permute-start.9 = (f32[48,256]{1,0:T(8,128)S(1)}, f32[48,256]{1,0:T(8,128)S(1)}, u32[]{:S(2)}, u32[]{:S(2)}) collective-permute-start(f32[48,256]{1,0:T(8,128)S(1)} %get-tuple-element.187.after_ref.mine_ref), channel_id=1, source_target_pairs={{0,16},{16,0},{32,48},{48,32},{64,80},{80,64},{96,112},{112,96},{1... | collective-permute-start | bytes 147464 | tf_op jit(solution)/shard_map/ppermute | solution.py:793
  60.0 16.0 %copy-start.9 = (f32[2,384,512]{2,1,0:T(8,128)S(1)}, f32[2,384,512]{2,1,0:T(8,128)}, u32[]{:S(2)}) copy-start(f32[2,384,512]{2,1,0:T(8,128)} %refs_4_.1) | copy-start | bytes 4718596

commit v8 on v7

--- a/solution.py
+++ b/solution.py
@@ -244,10 +244,12 @@
         for strip in range(out_ref.shape[0]):
             out_ref[strip, 0:16] = chunk
         return []
-    held_ref[...] = chunk
+    few = held_ref.shape[0]
+    for strip in range(few):
+        held_ref[strip] = chunk
     copies = [
-        pltpu.make_async_copy(held_ref, out_ref.at[strip, pl.ds(0, 16)], written.at[strip])
-        for strip in range(out_ref.shape[0])
+        pltpu.make_async_copy(held_ref, out_ref.at[pl.ds(k * few, few), pl.ds(0, 16)], written.at[k])
+        for k in range(out_ref.shape[0] // few)
     ]
     for copy in copies:
         copy.start()
@@ -886,8 +888,8 @@
         in_specs=[scalars()] * 2 + [whole()] * 12,
         out_specs=[whole()] + [far()] * 2,
         scratch_shapes=[
-            pltpu.VMEM((16, rows), f32),
-            pltpu.SemaphoreType.DMA((strips,)),
+            pltpu.VMEM((4, 16, rows), f32),
+            pltpu.SemaphoreType.DMA((strips // 4,)),
             pltpu.VMEM((2, 8, rows), f32),
             pltpu.SemaphoreType.DMA((2,)),
         ]

time: 79.9 us -> 79.8 us (level)
  no operation moved by 1% of the time
where the time goes in v8:
time: 79.8 us; the launch traced here: 79.3 us
  Pallas kernels  28 us (35%)
  starting transfers between devices  25.4 us (32%)
  blocking collectives  14.7 us (18%)
  waiting for transfers between devices  9.23 us (12%)
  between operations  1.03 us (1%)
  loops' own time  0.82 us (1%)
    all_to_all x1, blocking collectives, body(): lax.all_to_all(parts.reshape(count, 1, lanes), both, 0, 0)  14.7 us
    all_to_all x2, starting transfers between devices, body(): got = lax.all_to_all(chunk, 'chan', 0, 0)  12.2 us
    pallas_call x13, Pallas kernels, run(): pl.pallas_call(kernel, out_shape=[jax.ShapeDtypeStruct(*out) if isinstanc...  9.7 us
    all_to_all x2, waiting for transfers between devices, body(): got = lax.all_to_all(chunk, 'chan', 0, 0)  7.45 us
    ppermute x2, starting transfers between devices, across_blocks(): lax.ppermute(mine, 'rad', [(i, i ^ 1) for i in range(blocks)])  7.2 us
    pallas_call x1, Pallas kernels, body(): pl.pallas_call(second_outer_kernel, grid=(1,), out_shape=[jax.ShapeDtypeS...  6.09 us
    pallas_call x1, Pallas kernels, body(): pl.pallas_call(first_outer_kernel, out_shape=[jax.ShapeDtypeStruct((2, ou...  5.14 us
    ppermute x2, starting transfers between devices, across_blocks(): lax.ppermute(mine, 'rad', [(i, 2 * (last - i // 2) + i % 2) for i in rang...  4.67 us
  transfers between devices with their start and end apart: 8, of which 5 were waited for; matrix products, arithmetic and copies ran while one was open for 0% of the time, Pallas kernels for 25%

profile of v8, /device:TPU:1, one launch (start us, length us, event | category | flops | bytes accessed | tf_op | source)
XLA Modules:
  0.0 79.3 jit_solution(13773897758083112112)
XLA Ops:
  0.6 2.3 %shard_map.121 = f32[16,24,256]{2,1,0:T(8,128)} custom-call(f32[2,256]{1,0:T(2,128)} %refs_1_.9, f32[2,384,512]{2,1,0:T(8,128)} %refs_4_.1, f32[2,384,512]{2,1,0:T(8,128)} %refs_4_.1, f32[1,2,256,512]{3,2,1,0:T(8,128)} %amp_ref.5, s32[1,512]{1,0:T(1,128)} %bitcast.132), custom_call_target="tpu_custom_call" | custom-call | tf_op jit(solution)/shard_map/pallas_call | solution.py:822
  2.9 8.6 %all-to-all-start.4 = ((f32[16,24,256]{2,1,0:T(8,128)}), f32[16,24,256]{2,1,0:T(8,128)S(1)}, u32[]{:S(2)}, u32[]{:S(2)}) async-start(f32[16,24,256]{2,1,0:T(8,128)} %shard_map.121), calls=%async_computation.4 | async-start | bytes 786432 | tf_op jit(solution)/shard_map/all_to_all | solution.py:836
  11.5 5.1 %shard_map.124 = (f32[2,4,416,128]{3,2,1,0:T(8,128)S(1)}, bf16[2,512,512]{2,1,0:T(8,128)(2,1)S(1)}, f32[2,3,8,512]{3,2,1,0:T(8,128)S(1)}) custom-call(f32[2,384,512]{2,1,0:T(8,128)} %refs_4_.1, f32[384,512]{1,0:T(8,128)} %pot_in.1, f32[512,512]{1,0:T(8,128)} %mix_ref.1), custom_call_target="tpu_custom_call" | custom-call | tf_op jit(solution)/shard_map/pallas_call | solution.py:837
  16.7 4.0 %all-to-all-done.4.refs_0_.got_ref = f32[16,24,256]{2,1,0:T(8,128)S(1)} async-done(((f32[16,24,256]{2,1,0:T(8,128)}), f32[16,24,256]{2,1,0:T(8,128)S(1)}, u32[]{:S(2)}, u32[]{:S(2)}) %all-to-all-start.4) | async-done | bytes 393248 | tf_op jit(solution)/shard_map/all_to_all | solution.py:836
  20.7 1.3 %collective-permute-start.4 = (f32[24,256]{1,0:T(8,128)S(1)}, f32[24,256]{1,0:T(8,128)S(1)}, u32[]{:S(2)}, u32[]{:S(2)}) collective-permute-start(f32[24,256]{1,0:T(8,128)S(1)} %get-tuple-element.168.mine_ref), channel_id=1, source_target_pairs={{0,32},{16,48},{32,0},{48,16},{64,96},{80,112},{96,64},{112,80},{1... | collective-permute-start | bytes 73736 | tf_op jit(solution)/shard_map/ppermute | solution.py:791
  22.0 1.9 %shard_map.122.after_ref.block_a = f32[2,256]{1,0:T(2,128)S(1)} custom-call(f32[16,24,256]{2,1,0:T(8,128)S(1)} %all-to-all-done.4.refs_0_.got_ref, f32[1,4096,256]{2,1,0:T(8,128)} %refs_1_.8), custom_call_target="tpu_custom_call" | custom-call | tf_op jit(solution)/shard_map/pallas_call | solution.py:195
  23.9 0.0 collective-permute-done.4.other_ref.near_ref
  24.0 0.0 copy-start.20
  24.0 0.0 copy-start.24
  24.0 2.1 %collective-permute-start.5 = (f32[32,256]{1,0:T(8,128)S(1)}, f32[32,256]{1,0:T(8,128)S(1)}, u32[]{:S(2)}, u32[]{:S(2)}) collective-permute-start(f32[32,256]{1,0:T(8,128)S(1)} %get-tuple-element.170.mine_ref), channel_id=1, source_target_pairs={{0,96},{16,112},{32,64},{48,80},{64,32},{80,48},{96,0},{112,16},{1... | collective-permute-start | bytes 98312 | tf_op jit(solution)/shard_map/ppermute | solution.py:793
  26.1 1.9 %shard_map.123.after_ref.block_b = f32[2,256]{1,0:T(2,128)S(1)} custom-call(f32[16,24,256]{2,1,0:T(8,128)S(1)} %all-to-all-done.4.refs_0_.got_ref, f32[1,4096,256]{2,1,0:T(8,128)} %refs_1_.8), custom_call_target="tpu_custom_call" | custom-call | tf_op jit(solution)/shard_map/pallas_call | solution.py:195
  28.0 0.0 copy-start.27
  28.0 0.0 copy-start.28
  28.0 0.0 copy-start.29
  28.0 0.0 copy-start.30
  28.0 0.0 collective-permute-done.5.other_ref
  28.1 3.8 %collective-permute-start.6 = (f32[48,256]{1,0:T(8,128)S(1)}, f32[48,256]{1,0:T(8,128)S(1)}, u32[]{:S(2)}, u32[]{:S(2)}) collective-permute-start(f32[48,256]{1,0:T(8,128)S(1)} %get-tuple-element.172.after_ref.mine_ref), channel_id=1, source_target_pairs={{0,16},{16,0},{32,48},{48,32},{64,80},{80,64},{96,112},{112,96},{1... | collective-permute-start | bytes 147464 | tf_op jit(solution)/shard_map/ppermute | solution.py:795
  31.8 0.0 copy-done.20
  31.8 0.0 copy-done.24
  31.8 0.4 shard_map.128
  32.2 0.5 collective-permute-done.6.other_ref
  32.7 0.0 copy-done.27
  32.7 0.0 copy-done.28
  32.7 0.0 copy-done.29
  32.7 0.0 copy-done.30
  32.7 2.5 %shard_map.129 = (f32[2,256]{1,0:T(2,128)S(1)}, f32[16,24,256]{2,1,0:T(8,128)}, f32[2,8,512]{2,1,0:T(8,128)}) custom-call(s32[2,8]{1,0:T(2,128)S(1)} %bitcast.135, s32[2,8]{1,0:T(2,128)S(1)} %bitcast.137, f32[2,256]{1,0:T(2,128)S(1)} %shard_map.122.after_ref.block_a, f32[2,256]{1,0:T(2,128)S(1)} %shard_map.123.after_ref.block_b, f32[2,256]{1,0:T(2,128)S(1)} %copy-done.27, ...), custom_call_target="tpu_custom_call" | custom-call | tf_op jit(solution)/shard_map/pallas_call | solution.py:881
  35.2 3.6 %all-to-all-start.5 = ((f32[16,24,256]{2,1,0:T(8,128)}), f32[16,24,256]{2,1,0:T(8,128)S(1)}, u32[]{:S(2)}, u32[]{:S(2)}) async-start(f32[16,24,256]{2,1,0:T(8,128)} %get-tuple-element.179), calls=%async_computation.5 | async-start | bytes 786432 | tf_op jit(solution)/shard_map/all_to_all | solution.py:902
  38.8 6.1 %shard_map.132 = (f32[2,4,416,128]{3,2,1,0:T(8,128)S(1)}, f32[2,4,384,128]{3,2,1,0:T(8,128)}, f32[33,8,128]{2,1,0:T(8,128)}) custom-call(f32[2,8,512]{2,1,0:T(8,128)} %get-tuple-element.181.patch_ref, f32[2,4,416,128]{3,2,1,0:T(8,128)S(1)} %get-tuple-element.167.after_ref.wide_in, f32[2,384,512]{2,1,0:T(8,128)} %refs_4_.1, ...), custom_call_target="tpu_custom_call", output_to_operand_aliasing={{0}: (1, {})} | custom-call | tf_op jit(solution)/shard_map/pallas_call | solution.py:904
  44.9 3.4 %all-to-all-done.5.refs_0_.got_ref = f32[16,24,256]{2,1,0:T(8,128)S(1)} async-done(((f32[16,24,256]{2,1,0:T(8,128)}), f32[16,24,256]{2,1,0:T(8,128)S(1)}, u32[]{:S(2)}, u32[]{:S(2)}) %all-to-all-start.5) | async-done | bytes 393248 | tf_op jit(solution)/shard_map/all_to_all | solution.py:902
  48.3 0.1 collective-permute-start.7
  48.4 1.9 %shard_map.130.after_ref.block_a = f32[2,256]{1,0:T(2,128)S(1)} custom-call(f32[16,24,256]{2,1,0:T(8,128)S(1)} %all-to-all-done.5.refs_0_.got_ref, f32[1,4096,256]{2,1,0:T(8,128)} %refs_1_.8), custom_call_target="tpu_custom_call" | custom-call | tf_op jit(solution)/shard_map/pallas_call | solution.py:195
  50.3 0.8 collective-permute-done.7.other_ref.near_ref
  51.1 0.0 copy-start.25
  51.1 2.6 %collective-permute-start.8 = (f32[32,256]{1,0:T(8,128)S(1)}, f32[32,256]{1,0:T(8,128)S(1)}, u32[]{:S(2)}, u32[]{:S(2)}) collective-permute-start(f32[32,256]{1,0:T(8,128)S(1)} %get-tuple-element.185.mine_ref), channel_id=1, source_target_pairs={{0,96},{16,112},{32,64},{48,80},{64,32},{80,48},{96,0},{112,16},{1... | collective-permute-start | bytes 98312 | tf_op jit(solution)/shard_map/ppermute | solution.py:793
  53.7 1.9 %shard_map.131.after_ref.block_b = f32[2,256]{1,0:T(2,128)S(1)} custom-call(f32[16,24,256]{2,1,0:T(8,128)S(1)} %all-to-all-done.5.refs_0_.got_ref, f32[1,4096,256]{2,1,0:T(8,128)} %refs_1_.8), custom_call_target="tpu_custom_call" | custom-call | tf_op jit(solution)/shard_map/pallas_call | solution.py:195
  55.6 0.0 copy-start
  55.6 0.0 copy-start.1
  55.6 0.0 collective-permute-done.8.other_ref
  55.6 3.4 %collective-permute-start.9 = (f32[48,256]{1,0:T(8,128)S(1)}, f32[48,256]{1,0:T(8,128)S(1)}, u32[]{:S(2)}, u32[]{:S(2)}) collective-permute-start(f32[48,256]{1,0:T(8,128)S(1)} %get-tuple-element.187.after_ref.mine_ref), channel_id=1, source_target_pairs={{0,16},{16,0},{32,48},{48,32},{64,80},{80,64},{96,112},{112,96},{1... | collective-permute-start | bytes 147464 | tf_op jit(solution)/shard_map/ppermute | solution.py:795
  59.1 0.0 copy-done.21
  59.1 0.0 copy-done.25
  59.1 0.4 shard_map.136
  59.4 0.5 collective-permute-done.9.other_ref
  59.9 0.0 copy-done
  59.9 1.3 %shard_map.137 = (f32[2,256]{1,0:T(2,128)S(1)}, f32[2,2,8,512]{3,2,1,0:T(8,128)S(1)}, f32[128,128]{1,0:T(8,128)S(1)}) custom-call(s32[2,8]{1,0:T(2,128)S(1)} %bitcast.136, s32[2,8]{1,0:T(2,128)S(1)} %bitcast.138, f32[2,256]{1,0:T(2,128)S(1)} %shard_map.130.after_ref.block_a, f32[2,256]{1,0:T(2,128)S(1)} %shard_map.131.after_ref.block_b, ...), custom_call_target="tpu_custom_call" | custom-call | tf_op jit(solution)/shard_map/pallas_call | solution.py:195
  61.2 14.7 %all_to_all.31 = f32[128,1,128]{2,1,0:T(1,128)S(1)} all-to-all(f32[128,1,128]{2,1,0:T(1,128)S(1)} %bitcast.125), channel_id=1, replica_groups=mesh['rad'=8,'chan'=16] {'rad','chan'}, dimensions={0} | all-to-all | bytes 131072 | tf_op jit(solution)/shard_map/all_to_all | solution.py:941
  76.0 2.3 %shard_map.138 = (f32[2,256]{1,0:T(2,128)}, f32[2,384,512]{2,1,0:T(8,128)}, f32[2,2,3]{2,1,0:T(2,128)}, f32[1,128]{1,0:T(1,128)}) custom-call(f32[128,128]{1,0:T(8,128)S(1)} %bitcast.123, f32[2,256]{1,0:T(2,128)S(1)} %copy-done.27, f32[2,256]{1,0:T(2,128)S(1)} %get-tuple-element.180.inner_ref.refs_2_, f32[2,256]{1,0:T(2,128)S(1)} %get-tuple-element.195.refs_3_, ...), custom_call_target="tpu_custom_call" | custom-call | tf_op jit(solution)/shard_map/pallas_call | solution.py:942
  78.3 0.8 %while.18 = (f32[]{:T(128)}, f32[2,256]{1,0:T(2,128)}, f32[2,384,512]{2,1,0:T(8,128)}, f32[2,2,3]{2,1,0:T(2,128)}, f32[2,256]{1,0:T(2,128)S(1)}, /*index=5*/f32[...) while((f32[]{:T(128)}, f32[2,256]{1,0:T(2,128)}, ...), condition=%region_29.30_spmd, body=%region_0.29_spmd | while | flops 4953002496 | bytes 195695312 | solution.py:962
  (10 shorter events, 0.1 us)
Async XLA Ops:
  2.9 17.8 %all-to-all-start.4 = ((f32[16,24,256]{2,1,0:T(8,128)}), f32[16,24,256]{2,1,0:T(8,128)S(1)}, u32[]{:S(2)}, u32[]{:S(2)}) async-start(f32[16,24,256]{2,1,0:T(8,128)} %shard_map.121), calls=%async_computation.4 | async-start | bytes 786432 | tf_op jit(solution)/shard_map/all_to_all | solution.py:836
  20.7 3.2 %collective-permute-start.4 = (f32[24,256]{1,0:T(8,128)S(1)}, f32[24,256]{1,0:T(8,128)S(1)}, u32[]{:S(2)}, u32[]{:S(2)}) collective-permute-start(f32[24,256]{1,0:T(8,128)S(1)} %get-tuple-element.168.mine_ref), channel_id=1, source_target_pairs={{0,32},{16,48},{32,0},{48,16},{64,96},{80,112},{96,64},{112,80},{1... | collective-permute-start | bytes 73736 | tf_op jit(solution)/shard_map/ppermute | solution.py:791
  24.0 7.9 %copy-start.20 = (f32[1,2,512,256]{3,2,1,0:T(8,128)S(1)}, f32[1,2,512,256]{3,2,1,0:T(8,128)}, u32[]{:S(2)}) copy-start(f32[1,2,512,256]{3,2,1,0:T(8,128)} %coupling_ref.3) | copy-start | bytes 3145732
  24.0 7.9 %copy-start.24 = (f32[1,2,256,512]{3,2,1,0:T(8,128)S(1)}, f32[1,2,256,512]{3,2,1,0:T(8,128)}, u32[]{:S(2)}) copy-start(f32[1,2,256,512]{3,2,1,0:T(8,128)} %amp_ref.5) | copy-start | bytes 3145732
  24.0 4.1 %collective-permute-start.5 = (f32[32,256]{1,0:T(8,128)S(1)}, f32[32,256]{1,0:T(8,128)S(1)}, u32[]{:S(2)}, u32[]{:S(2)}) collective-permute-start(f32[32,256]{1,0:T(8,128)S(1)} %get-tuple-element.170.mine_ref), channel_id=1, source_target_pairs={{0,96},{16,112},{32,64},{48,80},{64,32},{80,48},{96,0},{112,16},{1... | collective-permute-start | bytes 98312 | tf_op jit(solution)/shard_map/ppermute | solution.py:793
  28.0 4.8 %copy-start.27 = (f32[2,256]{1,0:T(2,128)S(1)}, f32[2,256]{1,0:T(2,128)}, u32[]{:S(2)}) copy-start(f32[2,256]{1,0:T(2,128)} %refs_1_.9) | copy-start | bytes 6148
  28.0 4.7 %copy-start.28 = (s32[512]{0:T(512)S(1)}, s32[512]{0:T(512)}, u32[]{:S(2)}) copy-start(s32[512]{0:T(512)} %param.31) | copy-start | bytes 6148
  28.0 4.7 %copy-start.29 = (s32[8,2]{0,1:T(2,128)S(1)}, s32[8,2]{0,1:T(2,128)}, u32[]{:S(2)}) copy-start(s32[8,2]{0,1:T(2,128)} %param.29) | copy-start | bytes 196
  28.0 4.7 %copy-start.30 = (s32[8,2]{0,1:T(2,128)S(1)}, s32[8,2]{0,1:T(2,128)}, u32[]{:S(2)}) copy-start(s32[8,2]{0,1:T(2,128)} %param.30) | copy-start | bytes 196
  28.1 4.7 %collective-permute-start.6 = (f32[48,256]{1,0:T(8,128)S(1)}, f32[48,256]{1,0:T(8,128)S(1)}, u32[]{:S(2)}, u32[]{:S(2)}) collective-permute-start(f32[48,256]{1,0:T(8,128)S(1)} %get-tuple-element.172.after_ref.mine_ref), channel_id=1, source_target_pairs={{0,16},{16,0},{32,48},{48,32},{64,80},{80,64},{96,112},{112,96},{1... | collective-permute-start | bytes 147464 | tf_op jit(solution)/shard_map/ppermute | solution.py:795
  35.2 13.1 %all-to-all-start.5 = ((f32[16,24,256]{2,1,0:T(8,128)}), f32[16,24,256]{2,1,0:T(8,128)S(1)}, u32[]{:S(2)}, u32[]{:S(2)}) async-start(f32[16,24,256]{2,1,0:T(8,128)} %get-tuple-element.179), calls=%async_computation.5 | async-start | bytes 786432 | tf_op jit(solution)/shard_map/all_to_all | solution.py:902
  48.3 2.8 %collective-permute-start.7 = (f32[24,256]{1,0:T(8,128)S(1)}, f32[24,256]{1,0:T(8,128)S(1)}, u32[]{:S(2)}, u32[]{:S(2)}) collective-permute-start(f32[24,256]{1,0:T(8,128)S(1)} %get-tuple-element.183.mine_ref), channel_id=1, source_target_pairs={{0,32},{16,48},{32,0},{48,16},{64,96},{80,112},{96,64},{112,80},{1... | collective-permute-start | bytes 73736 | tf_op jit(solution)/shard_map/ppermute | solution.py:791
  51.1 8.0 %copy-start.21 = (f32[1,2,512,256]{3,2,1,0:T(8,128)S(1)}, f32[1,2,512,256]{3,2,1,0:T(8,128)}, u32[]{:S(2)}) copy-start(f32[1,2,512,256]{3,2,1,0:T(8,128)} %coupling_ref.3) | copy-start | bytes 3145732
  51.1 8.0 %copy-start.25 = (f32[1,2,256,512]{3,2,1,0:T(8,128)S(1)}, f32[1,2,256,512]{3,2,1,0:T(8,128)}, u32[]{:S(2)}) copy-start(f32[1,2,256,512]{3,2,1,0:T(8,128)} %amp_ref.5) | copy-start | bytes 3145732
  51.1 4.5 %collective-permute-start.8 = (f32[32,256]{1,0:T(8,128)S(1)}, f32[32,256]{1,0:T(8,128)S(1)}, u32[]{:S(2)}, u32[]{:S(2)}) collective-permute-start(f32[32,256]{1,0:T(8,128)S(1)} %get-tuple-element.185.mine_ref), channel_id=1, source_target_pairs={{0,96},{16,112},{32,64},{48,80},{64,32},{80,48},{96,0},{112,16},{1... | collective-permute-start | bytes 98312 | tf_op jit(solution)/shard_map/ppermute | solution.py:793
  55.6 4.4 %copy-start = (f32[2,4,384,128]{3,2,1,0:T(8,128)S(1)}, f32[2,4,384,128]{3,2,1,0:T(8,128)}, u32[]{:S(2)}) copy-start(f32[2,4,384,128]{3,2,1,0:T(8,128)} %get-tuple-element.193.second_ref.refs_6_) | copy-start | bytes 4718596
  55.6 4.4 %copy-start.1 = (f32[33,8,128]{2,1,0:T(8,128)S(1)}, f32[33,8,128]{2,1,0:T(8,128)}, u32[]{:S(2)}) copy-start(f32[33,8,128]{2,1,0:T(8,128)} %get-tuple-element.182.after_ref.notes_ref) | copy-start | bytes 405508
  55.6 4.3 %collective-permute-start.9 = (f32[48,256]{1,0:T(8,128)S(1)}, f32[48,256]{1,0:T(8,128)S(1)}, u32[]{:S(2)}, u32[]{:S(2)}) collective-permute-start(f32[48,256]{1,0:T(8,128)S(1)} %get-tuple-element.187.after_ref.mine_ref), channel_id=1, source_target_pairs={{0,16},{16,0},{32,48},{48,32},{64,80},{80,64},{96,112},{112,96},{1... | collective-permute-start | bytes 147464 | tf_op jit(solution)/shard_map/ppermute | solution.py:795
  59.9 16.0 %copy-start.9 = (f32[2,384,512]{2,1,0:T(8,128)S(1)}, f32[2,384,512]{2,1,0:T(8,128)}, u32[]{:S(2)}) copy-start(f32[2,384,512]{2,1,0:T(8,128)} %refs_4_.1) | copy-start | bytes 4718596
